TPU v7x, 32 devices: a whole 2x2x4 slice. The times are simulated.
32 devices in a mesh: groups: 2 (over x), section: 16 (over z, y, core).
Axes of the slice: x: 2, y: 2, z: 4, core: 2. Of those that a mesh axis runs over, the one named last changes fastest.
Arguments:
- queries: bfloat16 [4096, 4096], P(('groups', 'section')), parts along dimension 0, may hold values from -400 to 400
- keys: bfloat16 [4096, 256], P(('groups', 'section')), parts along dimension 0, may hold values from -4 to 4
- values: bfloat16 [4096, 256], P(('groups', 'section')), parts along dimension 0, may hold values from -6 to 6
- windows: int32 [32], P('groups'), parts along dimension 0, may hold values from 0 to 1024, as said below
Outputs:
- attended: bfloat16 [4096, 4096], P(('groups', 'section')), parts along dimension 0
- log_total: float32 [4096, 32], P(('groups', 'section')), parts along dimension 0
There are 2 independent parts, one for each index of `groups`. A program takes and returns all parts, laid end to end along the dimension named above; each array names one. Nothing has to cross between parts.
Inputs may be any that keep to these rules, and one draw needn't show every extreme that they name: `windows`: the first slice's window is 0 and the last slice's window is 1024.
All inputs are finite; a program needn't handle non-finite values.
Results may differ from a plain program's by a relative error of at most 0.0055.
Values may be sent and summed in bfloat16 or wider, within the bound.
No kernel may reach another device: no remote copies, remote signals or barrier semaphores. Data moves between devices by JAX's collectives and lax.ppermute only.
A program may use at most 64 MiB of HBM per device.

v0:
```python
import functools
import math

import jax
import jax.numpy as jnp
from jax import lax
from jax.experimental import pallas as pl
from jax.experimental.pallas import tpu as pltpu
from jax.sharding import PartitionSpec as P

HD = 128
SCALE = HD ** (-0.5)
TO_EXP2 = SCALE * math.log2(math.e)
HIDDEN = -1e30


def shifted(block, axis, distance):
    size = lax.axis_size(axis)
    return lax.ppermute(block, axis, [(i, (i + distance) % size) for i in range(size)])


def swapped(block, axis):
    return lax.ppermute(block, axis, [(i ^ 1, i) for i in range(lax.axis_size(axis))])


def head_rows(q_ref):
    heads = q_ref.shape[1] // HD
    return jnp.concatenate([q_ref[:, h * HD : (h + 1) * HD] for h in range(heads)], 0)


def scores_of(key_rows, query_rows):
    return lax.dot_general(
        key_rows, query_rows, (((1,), (1,)), ((), ())), preferred_element_type=jnp.float32
    )


def weighted(value_rows, weights):
    return lax.dot_general(
        value_rows,
        weights.astype(jnp.bfloat16),
        (((0,), (0,)), ((), ())),
        preferred_element_type=jnp.float32,
    )


def finish(summed, top, total, out_ref, log_ref, log_scratch):
    heads = out_ref.shape[1] // HD
    result = summed * (1.0 / total)
    for h in range(heads):
        out_ref[:, h * HD : (h + 1) * HD] = result[:, h * HD : (h + 1) * HD].T.astype(
            out_ref.dtype
        )
    logs = top * SCALE + jnp.log(total)
    group = pl.program_id(0)
    log_scratch[pl.ds(group * heads, heads), :] = jnp.concatenate(
        [logs[:, h * HD : (h + 1) * HD] for h in range(heads)], 0
    )

    @pl.when(group == pl.num_programs(0) - 1)
    def _():
        log_ref[...] = log_scratch[...].T


def near_kernel(axis, win_ref, q_ref, k0, v0, k1, v1, sum_ref, stat_ref):
    me = lax.axis_index(axis)
    rows = k0.shape[0]
    lowest = jnp.maximum(rows - win_ref[me], 0)
    query_rows = head_rows(q_ref)
    count = query_rows.shape[0]
    keys = jnp.concatenate([k1[...], k0[...]], 0)
    values = jnp.concatenate([v1[...], v0[...]], 0)
    scores = scores_of(keys, query_rows)
    key_pos = lax.broadcasted_iota(jnp.int32, (2 * rows, rows), 0)
    row_pos = lax.broadcasted_iota(jnp.int32, (2 * rows, rows), 1) + rows
    odd = (me & 1) == 1
    start = jnp.where(odd, lowest, rows)
    visible = (key_pos >= start) & (key_pos <= row_pos)
    bias = jnp.where(visible, 0.0, HIDDEN)
    scores = scores + jnp.concatenate([bias] * (count // rows), 1)
    top = jnp.max(scores, 0, keepdims=True)
    weights = jnp.exp2((scores - top) * TO_EXP2)
    stat_ref[0:1] = top
    stat_ref[1:2] = jnp.sum(weights, 0, keepdims=True)
    sum_ref[...] = weighted(values, weights)


def far_kernel(axis, distances, last, win_ref, q_ref, *refs):
    me = lax.axis_index(axis)
    sibling = me ^ 1
    pieces = 2 * len(distances)
    key_refs, value_refs = refs[:pieces], refs[pieces : 2 * pieces]
    sum_in, stat_in = refs[2 * pieces : 2 * pieces + 2]
    outs = refs[2 * pieces + 2 :]
    rows = key_refs[0].shape[0]
    lowest = jnp.maximum(me * rows - win_ref[me], 0)
    starts = [(who - d) * rows for d in distances for who in (me, sibling)]
    needed = functools.reduce(jnp.logical_or, [s + rows > lowest for s in starts])

    def emit(summed, top, total):
        if last:
            finish(summed, top, total, *outs)
        else:
            outs[0][...] = summed
            outs[1][0:1] = top
            outs[1][1:2] = total

    @pl.when(needed)
    def _():
        query_rows = head_rows(q_ref)
        keys = jnp.concatenate([r[...] for r in key_refs], 0)
        values = jnp.concatenate([r[...] for r in value_refs], 0)
        scores = scores_of(keys, query_rows)
        local = lax.broadcasted_iota(jnp.int32, (rows, 1), 0)
        key_pos = jnp.concatenate([local + s for s in starts], 0)
        scores = jnp.where(key_pos >= lowest, scores, HIDDEN)
        old_top, old_total = stat_in[0:1], stat_in[1:2]
        top = jnp.maximum(old_top, jnp.max(scores, 0, keepdims=True))
        factor = jnp.exp2((old_top - top) * TO_EXP2)
        weights = jnp.exp2((scores - top) * TO_EXP2)
        total = old_total * factor + jnp.sum(weights, 0, keepdims=True)
        emit(sum_in[...] * factor + weighted(values, weights), top, total)

    @pl.when(jnp.logical_not(needed))
    def _():
        emit(sum_in[...], stat_in[0:1], stat_in[1:2])


def attend(kernel, axis, windows, queries, blocks, state, last):
    rows, width = queries.shape
    groups = blocks[0].shape[1] // (2 * HD)
    wide = width // groups
    whole = lambda g, w: (0, 0)
    mine = lambda g, w: (0, g)
    values = lambda g, w: (0, groups + g)
    state_shapes = [
        jax.ShapeDtypeStruct((HD, width), jnp.float32),
        jax.ShapeDtypeStruct((2, width), jnp.float32),
    ]
    state_specs = [pl.BlockSpec((HD, wide), mine), pl.BlockSpec((2, wide), mine)]
    heads = width // HD
    if last:
        out_shape = [
            jax.ShapeDtypeStruct((rows, width), jnp.bfloat16),
            jax.ShapeDtypeStruct((rows, heads), jnp.float32),
        ]
        out_specs = [pl.BlockSpec((rows, wide), mine), pl.BlockSpec((rows, heads), whole)]
        scratch = [pltpu.VMEM((heads, rows), jnp.float32)]
    else:
        out_shape, out_specs, scratch = state_shapes, state_specs, []
    keys_spec = pl.BlockSpec((rows, HD), mine)
    values_spec = pl.BlockSpec((rows, HD), values)
    count = len(blocks)
    if kernel is near_kernel:
        operands = [x for b in blocks for x in (b, b)]
        specs = [keys_spec, values_spec] * count
    else:
        operands = list(blocks) * 2
        specs = [keys_spec] * count + [values_spec] * count
    aliases = {}
    if state is not None:
        if not last:
            aliases = {2 + len(operands): 0, 3 + len(operands): 1}
        operands += list(state)
        specs += state_specs
    flops = 4 * count * rows * rows * width
    return pl.pallas_call(
        kernel if kernel is not near_kernel else functools.partial(near_kernel, axis),
        grid_spec=pltpu.PrefetchScalarGridSpec(
            num_scalar_prefetch=1,
            grid=(groups,),
            in_specs=[pl.BlockSpec((rows, wide), mine)] + specs,
            out_specs=out_specs,
            scratch_shapes=scratch,
        ),
        out_shape=out_shape,
        input_output_aliases=aliases,
        cost_estimate=pl.CostEstimate(
            flops=flops,
            bytes_accessed=rows * width * 2,
            transcendentals=count * rows * rows * width // HD,
        ),
        compiler_params=pltpu.CompilerParams(vmem_limit_bytes=40 << 20),
    )(windows, queries, *operands)


def on_device(queries, keys, values, windows):
    axis = "section"
    reach = lax.axis_size(axis) // 2
    own = jnp.concatenate([keys, values], 1)
    state = attend(
        near_kernel, axis, windows, queries, [own, swapped(own, axis)], None, False
    )
    held = {4: shifted(own, axis, 4), 2: shifted(own, axis, 2)}
    for first in range(2, reach + 1, 4):
        distances = [d for d in (first, first + 2) if d <= reach]
        last = first + 4 > reach
        blocks = [x for d in distances for x in (held[d], swapped(held[d], axis))]
        if not last:
            for d in (first + 6, first + 4):
                if d <= reach:
                    held[d] = shifted(held[d - 4], axis, 4)
        state = attend(
            functools.partial(far_kernel, axis, distances, last),
            axis,
            windows,
            queries,
            blocks,
            state,
            last,
        )
    return tuple(state)


def solution(mesh):
    placed = (
        P(("groups", "section"), None),
        P(("groups", "section"), None),
        P(("groups", "section"), None),
        P("groups"),
    )
    return jax.shard_map(
        on_device,
        mesh=mesh,
        in_specs=placed,
        out_specs=(P(("groups", "section"), None), P(("groups", "section"), None)),
        check_vma=False,
    )
```

profile of v0, /device:TPU:29, one launch (start us, length us, event | category | flops | bytes accessed | tf_op | source)
XLA Modules:
  0.0 34.5 jit_solution(18391947154708678749)
XLA Ops:
  0.6 0.8 %constant_dynamic-update-slice_fusion.1 = bf16[128,512]{1,0:T(8,128)(2,1)S(1)} fusion(bf16[128,256]{1,0:T(8,128)(2,1)} %param.5), kind=kLoop, calls=%fused_computation.1 | loop fusion | bytes 131072
  1.5 0.8 %constant_dynamic-update-slice_fusion.k0.v0 = bf16[128,512]{1,0:T(8,128)(2,1)S(1)} fusion(bf16[128,512]{1,0:T(8,128)(2,1)S(1)} %constant_dynamic-update-slice_fusion.1, bf16[128,256]{1,0:T(8,128)(2,1)} %param.6), kind=kLoop, calls=%fused_computation | loop fusion | bytes 131072 | tf_op jit(solution)/shard_map/concatenate | solution.py:189
  2.3 0.0 collective-permute-start
  2.3 1.2 %collective-permute-start.3 = (bf16[128,512]{1,0:T(8,128)(2,1)S(1)}, bf16[128,512]{1,0:T(8,128)(2,1)S(1)}, u32[]{:S(2)}, u32[]{:S(2)}) collective-permute-start(bf16[128,512]{1,0:T(8,128)(2,1)S(1)} %constant_dynamic-update-slice_fusion.k0.v0), channel_id=1, source_target_pairs={{0,4},{1,5},{2,6},{3,7},{4,8},{5,9},{6,10},{7,11},{8,12},{9,13},{1... | collective-permute-start | bytes 393224 | tf_op jit(solution)/shard_map/ppermute | solution.py:19
  3.5 3.2 %collective-permute-done.refs_0_.refs_4_ = bf16[128,512]{1,0:T(8,128)(2,1)S(1)} collective-permute-done((bf16[128,512]{1,0:T(8,128)(2,1)S(1)}, bf16[128,512]{1,0:T(8,128)(2,1)S(1)}, u32[]{:S(2)}, u32[]{:S(2)}) %collective-permute-start) | collective-permute-done | bytes 131104 | tf_op jit(solution)/shard_map/ppermute | solution.py:19
  6.7 0.0 collective-permute-start.1
  6.7 2.7 %collective-permute-done.3.refs_2_.refs_6_ = bf16[128,512]{1,0:T(8,128)(2,1)S(1)} collective-permute-done((bf16[128,512]{1,0:T(8,128)(2,1)S(1)}, bf16[128,512]{1,0:T(8,128)(2,1)S(1)}, u32[]{:S(2)}, u32[]{:S(2)}) %collective-permute-start.3) | collective-permute-done | bytes 131104 | tf_op jit(solution)/shard_map/ppermute | solution.py:19
  9.4 2.2 %collective-permute-start.4 = (bf16[128,512]{1,0:T(8,128)(2,1)S(1)}, bf16[128,512]{1,0:T(8,128)(2,1)S(1)}, u32[]{:S(2)}, u32[]{:S(2)}) collective-permute-start(bf16[128,512]{1,0:T(8,128)(2,1)S(1)} %collective-permute-done.3.refs_2_.refs_6_), channel_id=1, source_target_pairs={{0,4},{1,5},{2,6},{3,7},{4,8},{5,9},{6,10},{7,11},{8,12},{9,13},{1... | collective-permute-start | bytes 393224 | tf_op jit(solution)/shard_map/ppermute | solution.py:19
  11.6 2.3 %collective-permute-start.8 = (bf16[128,512]{1,0:T(8,128)(2,1)S(1)}, bf16[128,512]{1,0:T(8,128)(2,1)S(1)}, u32[]{:S(2)}, u32[]{:S(2)}) collective-permute-start(bf16[128,512]{1,0:T(8,128)(2,1)S(1)} %constant_dynamic-update-slice_fusion.k0.v0), channel_id=1, source_target_pairs={{1,0},{0,1},{3,2},{2,3},{5,4},{4,5},{7,6},{6,7},{9,8},{8,9},{11,10... | collective-permute-start | bytes 393224 | tf_op jit(solution)/shard_map/ppermute | solution.py:23
  14.0 0.0 collective-permute-start.6
  14.0 0.5 %collective-permute-start.7 = (bf16[128,512]{1,0:T(8,128)(2,1)S(1)}, bf16[128,512]{1,0:T(8,128)(2,1)S(1)}, u32[]{:S(2)}, u32[]{:S(2)}) collective-permute-start(bf16[128,512]{1,0:T(8,128)(2,1)S(1)} %collective-permute-done.3.refs_2_.refs_6_), channel_id=1, source_target_pairs={{1,0},{0,1},{3,2},{2,3},{5,4},{4,5},{7,6},{6,7},{9,8},{8,9},{11,10... | collective-permute-start | bytes 393224 | tf_op jit(solution)/shard_map/ppermute | solution.py:23
  14.5 0.0 collective-permute-done.1.refs_0_.refs_4_
  14.5 0.5 %collective-permute-start.2 = (bf16[128,512]{1,0:T(8,128)(2,1)S(1)}, bf16[128,512]{1,0:T(8,128)(2,1)S(1)}, u32[]{:S(2)}, u32[]{:S(2)}) collective-permute-start(bf16[128,512]{1,0:T(8,128)(2,1)S(1)} %collective-permute-done.1.refs_0_.refs_4_), channel_id=1, source_target_pairs={{1,0},{0,1},{3,2},{2,3},{5,4},{4,5},{7,6},{6,7},{9,8},{8,9},{11,10... | collective-permute-start | bytes 393224 | tf_op jit(solution)/shard_map/ppermute | solution.py:23
  14.9 0.0 collective-permute-done.4.refs_2_.refs_6_
  14.9 2.2 %collective-permute-start.5 = (bf16[128,512]{1,0:T(8,128)(2,1)S(1)}, bf16[128,512]{1,0:T(8,128)(2,1)S(1)}, u32[]{:S(2)}, u32[]{:S(2)}) collective-permute-start(bf16[128,512]{1,0:T(8,128)(2,1)S(1)} %collective-permute-done.4.refs_2_.refs_6_), channel_id=1, source_target_pairs={{1,0},{0,1},{3,2},{2,3},{5,4},{4,5},{7,6},{6,7},{9,8},{8,9},{11,10... | collective-permute-start | bytes 393224 | tf_op jit(solution)/shard_map/ppermute | solution.py:23
  17.1 0.0 collective-permute-done.8.k1.v1
  17.1 1.2 %copy-done = bf16[128,4096]{1,0:T(8,128)(2,1)S(1)} copy-done((bf16[128,4096]{1,0:T(8,128)(2,1)S(1)}, bf16[128,4096]{1,0:T(8,128)(2,1)}, u32[]{:S(2)}) %copy-start) | copy-done | bytes 1048600
  18.3 0.7 %copy-done.1 = s32[16]{0:T(128)S(1)} copy-done((s32[16]{0:T(128)S(1)}, s32[16]{0:T(128)}, u32[]{:S(2)}) %copy-start.1) | copy-done | bytes 88
  19.0 2.9 %shard_map.59 = (f32[128,4096]{1,0:T(8,128)S(1)}, f32[2,4096]{1,0:T(2,128)S(1)}) custom-call(s32[16]{0:T(128)S(1)} %copy-done.1, bf16[128,4096]{1,0:T(8,128)(2,1)S(1)} %copy-done, bf16[128,512]{1,0:T(8,128)(2,1)S(1)} %constant_dynamic-update-slice_fusion.k0.v0, bf16[128,512]{1,0:T(8,128)(2,1)S(1)} %constant_dynamic-update-slice_fusion.k0.v0, ...), custom_call_target="tpu_custom_call" | custom-call | flops 536870912 | bytes 1048576 | tf_op jit(solution)/shard_map/pallas_call | solution.py:166
  21.8 0.0 collective-permute-done.6.refs_1_.refs_5_
  21.9 5.4 %shard_map.60 = (f32[128,4096]{1,0:T(8,128)S(1)}, f32[2,4096]{1,0:T(2,128)S(1)}) custom-call(s32[16]{0:T(128)S(1)} %copy-done.1, bf16[128,4096]{1,0:T(8,128)(2,1)S(1)} %copy-done, bf16[128,512]{1,0:T(8,128)(2,1)S(1)} %collective-permute-done.refs_0_.refs_4_, ...), custom_call_target="tpu_custom_call", output_to_operand_aliasing={{0}: (10, {}), {1}: (11, {})} | custom-call | flops 1073741824 | bytes 1048576 | tf_op jit(solution)/shard_map/pallas_call | solution.py:166
  27.3 0.0 collective-permute-done.5.refs_3_.refs_7_
  27.3 6.5 %shard_map.61 = (bf16[128,4096]{1,0:T(8,128)(2,1)}, f32[128,32]{1,0:T(8,128)S(1)}) custom-call(s32[16]{0:T(128)S(1)} %copy-done.1, bf16[128,4096]{1,0:T(8,128)(2,1)S(1)} %copy-done, bf16[128,512]{1,0:T(8,128)(2,1)S(1)} %collective-permute-done.1.refs_0_.refs_4_, bf16[128,512]{1,0:T(8,128)(2,1)S(1)} %collective-permute-done.2.refs_1_.refs_5_, ...), custom_call_target="tpu_custom_call" | custom-call | flops 1073741824 | bytes 1048576 | tf_op jit(solution)/shard_map/pallas_call | solution.py:166
  33.8 0.7 %copy.8 = f32[128,32]{0,1:T(8,128)} copy(f32[128,32]{1,0:T(8,128)S(1)} %get-tuple-element.11) | data formatting | bytes 32768 | tf_op jit(solution)/shard_map/pallas_call | solution.py:166
  (4 shorter events, 0.0 us)
Async XLA Ops:
  2.3 4.4 %collective-permute-start = (bf16[128,512]{1,0:T(8,128)(2,1)S(1)}, bf16[128,512]{1,0:T(8,128)(2,1)S(1)}, u32[]{:S(2)}, u32[]{:S(2)}) collective-permute-start(bf16[128,512]{1,0:T(8,128)(2,1)S(1)} %constant_dynamic-update-slice_fusion.k0.v0), channel_id=1, source_target_pairs={{0,2},{1,3},{2,4},{3,5},{4,6},{5,7},{6,8},{7,9},{8,10},{9,11},{10,... | collective-permute-start | bytes 393224 | tf_op jit(solution)/shard_map/ppermute | solution.py:19
  2.3 7.1 %collective-permute-start.3 = (bf16[128,512]{1,0:T(8,128)(2,1)S(1)}, bf16[128,512]{1,0:T(8,128)(2,1)S(1)}, u32[]{:S(2)}, u32[]{:S(2)}) collective-permute-start(bf16[128,512]{1,0:T(8,128)(2,1)S(1)} %constant_dynamic-update-slice_fusion.k0.v0), channel_id=1, source_target_pairs={{0,4},{1,5},{2,6},{3,7},{4,8},{5,9},{6,10},{7,11},{8,12},{9,13},{1... | collective-permute-start | bytes 393224 | tf_op jit(solution)/shard_map/ppermute | solution.py:19
  6.7 7.8 %collective-permute-start.1 = (bf16[128,512]{1,0:T(8,128)(2,1)S(1)}, bf16[128,512]{1,0:T(8,128)(2,1)S(1)}, u32[]{:S(2)}, u32[]{:S(2)}) collective-permute-start(bf16[128,512]{1,0:T(8,128)(2,1)S(1)} %collective-permute-done.refs_0_.refs_4_), channel_id=1, source_target_pairs={{0,4},{1,5},{2,6},{3,7},{4,8},{5,9},{6,10},{7,11},{8,12},{9,13},{1... | collective-permute-start | bytes 393224 | tf_op jit(solution)/shard_map/ppermute | solution.py:19
  9.4 5.5 %collective-permute-start.4 = (bf16[128,512]{1,0:T(8,128)(2,1)S(1)}, bf16[128,512]{1,0:T(8,128)(2,1)S(1)}, u32[]{:S(2)}, u32[]{:S(2)}) collective-permute-start(bf16[128,512]{1,0:T(8,128)(2,1)S(1)} %collective-permute-done.3.refs_2_.refs_6_), channel_id=1, source_target_pairs={{0,4},{1,5},{2,6},{3,7},{4,8},{5,9},{6,10},{7,11},{8,12},{9,13},{1... | collective-permute-start | bytes 393224 | tf_op jit(solution)/shard_map/ppermute | solution.py:19
  11.6 5.5 %collective-permute-start.8 = (bf16[128,512]{1,0:T(8,128)(2,1)S(1)}, bf16[128,512]{1,0:T(8,128)(2,1)S(1)}, u32[]{:S(2)}, u32[]{:S(2)}) collective-permute-start(bf16[128,512]{1,0:T(8,128)(2,1)S(1)} %constant_dynamic-update-slice_fusion.k0.v0), channel_id=1, source_target_pairs={{1,0},{0,1},{3,2},{2,3},{5,4},{4,5},{7,6},{6,7},{9,8},{8,9},{11,10... | collective-permute-start | bytes 393224 | tf_op jit(solution)/shard_map/ppermute | solution.py:23
  14.0 7.9 %collective-permute-start.6 = (bf16[128,512]{1,0:T(8,128)(2,1)S(1)}, bf16[128,512]{1,0:T(8,128)(2,1)S(1)}, u32[]{:S(2)}, u32[]{:S(2)}) collective-permute-start(bf16[128,512]{1,0:T(8,128)(2,1)S(1)} %collective-permute-done.refs_0_.refs_4_), channel_id=1, source_target_pairs={{1,0},{0,1},{3,2},{2,3},{5,4},{4,5},{7,6},{6,7},{9,8},{8,9},{11,10... | collective-permute-start | bytes 393224 | tf_op jit(solution)/shard_map/ppermute | solution.py:23
  14.0 7.9 %collective-permute-start.7 = (bf16[128,512]{1,0:T(8,128)(2,1)S(1)}, bf16[128,512]{1,0:T(8,128)(2,1)S(1)}, u32[]{:S(2)}, u32[]{:S(2)}) collective-permute-start(bf16[128,512]{1,0:T(8,128)(2,1)S(1)} %collective-permute-done.3.refs_2_.refs_6_), channel_id=1, source_target_pairs={{1,0},{0,1},{3,2},{2,3},{5,4},{4,5},{7,6},{6,7},{9,8},{8,9},{11,10... | collective-permute-start | bytes 393224 | tf_op jit(solution)/shard_map/ppermute | solution.py:23
  14.5 12.8 %collective-permute-start.2 = (bf16[128,512]{1,0:T(8,128)(2,1)S(1)}, bf16[128,512]{1,0:T(8,128)(2,1)S(1)}, u32[]{:S(2)}, u32[]{:S(2)}) collective-permute-start(bf16[128,512]{1,0:T(8,128)(2,1)S(1)} %collective-permute-done.1.refs_0_.refs_4_), channel_id=1, source_target_pairs={{1,0},{0,1},{3,2},{2,3},{5,4},{4,5},{7,6},{6,7},{9,8},{8,9},{11,10... | collective-permute-start | bytes 393224 | tf_op jit(solution)/shard_map/ppermute | solution.py:23
  14.9 12.4 %collective-permute-start.5 = (bf16[128,512]{1,0:T(8,128)(2,1)S(1)}, bf16[128,512]{1,0:T(8,128)(2,1)S(1)}, u32[]{:S(2)}, u32[]{:S(2)}) collective-permute-start(bf16[128,512]{1,0:T(8,128)(2,1)S(1)} %collective-permute-done.4.refs_2_.refs_6_), channel_id=1, source_target_pairs={{1,0},{0,1},{3,2},{2,3},{5,4},{4,5},{7,6},{6,7},{9,8},{8,9},{11,10... | collective-permute-start | bytes 393224 | tf_op jit(solution)/shard_map/ppermute | solution.py:23
  17.1 1.2 %copy-start = (bf16[128,4096]{1,0:T(8,128)(2,1)S(1)}, bf16[128,4096]{1,0:T(8,128)(2,1)}, u32[]{:S(2)}) copy-start(bf16[128,4096]{1,0:T(8,128)(2,1)} %q_ref.5) | copy-start | bytes 3145732
  18.3 0.7 %copy-start.1 = (s32[16]{0:T(128)S(1)}, s32[16]{0:T(128)}, u32[]{:S(2)}) copy-start(s32[16]{0:T(128)} %win_ref.5) | copy-start | bytes 196
where the time goes:
time: 34.8 us; the launch traced here: 34.5 us
  Pallas kernels  14.8 us (43%)
  starting transfers between devices  8.84 us (25%)
  waiting for transfers between devices  5.95 us (17%)
  local copies, waits for them, and re-layouts  4.25 us (12%)
  between operations  0.69 us (2%)
    pallas_call x3, Pallas kernels, attend(): pl.pallas_call(kernel if kernel is not near_kernel else functools.partial...  14.8 us
    ppermute x4, waiting for transfers between devices, shifted(): lax.ppermute(block, axis, [(i, (i + distance) % size) for i in range(size)])  5.94 us
    ppermute x5, starting transfers between devices, swapped(): lax.ppermute(block, axis, [(i ^ 1, i) for i in range(lax.axis_size(axis))])  5.48 us
    ppermute x4, starting transfers between devices, shifted(): lax.ppermute(block, axis, [(i, (i + distance) % size) for i in range(size)])  3.36 us
    unnamed x5, local copies, waits for them, and re-layouts  2.73 us
    concatenate x1, local copies, waits for them, and re-layouts, on_device(): own = jnp.concatenate([keys, values], 1)  0.84 us
  transfers between devices with their start and end apart: 9, of which 2 were waited for; matrix products, arithmetic and copies ran while one was open for 0% of the time, Pallas kernels for 24%

commit v1 on v0

v1 whole, which is shorter than its diff:
```python
import functools
import math

import jax
import jax.numpy as jnp
from jax import lax
from jax.experimental import pallas as pl
from jax.experimental.pallas import tpu as pltpu
from jax.sharding import PartitionSpec as P

HD = 128
SCALE = HD ** (-0.5)
TO_EXP2 = SCALE * math.log2(math.e)
HIDDEN = -1e30
SUM_ROWS = 8
STATE_ROWS = HD + 2 * SUM_ROWS
TOP_ROW = HD + SUM_ROWS
TILE = 64
VMEM = pl.BlockSpec(memory_space=pltpu.VMEM)
ANY = pl.BlockSpec(memory_space=pl.ANY)
SMEM = pl.BlockSpec(memory_space=pltpu.SMEM)


def shifted(block, axis, distance):
    size = lax.axis_size(axis)
    return lax.ppermute(block, axis, [(i, (i + distance) % size) for i in range(size)])


def swapped(block, axis):
    return lax.ppermute(block, axis, [(i ^ 1, i) for i in range(lax.axis_size(axis))])


def dot(left, right, dims):
    return lax.dot_general(left, right, (dims, ((), ())), preferred_element_type=jnp.float32)


def run_chunks(q_ref, blocks, flags, row_flags, state_in, state_out, s_buf, p_buf, out_ref, log_ref):
    rows, width = q_ref.shape
    groups = blocks[0].shape[1] // (2 * HD)
    slots, keys, wide = s_buf.shape
    heads = wide // HD
    chunks = width // wide
    per_group = chunks // groups
    row_part = jnp.concatenate([row_flags] * heads, 0)
    ones = jnp.ones((2 * SUM_ROWS, keys), jnp.bfloat16)
    key_ext, value_ext = [], []
    for g in range(groups):
        key_rows = jnp.concatenate([b[:, g * HD : (g + 1) * HD] for b in blocks], 0)
        value_rows = jnp.concatenate(
            [b[:, (groups + g) * HD : (groups + g + 1) * HD] for b in blocks], 0
        )
        key_ext.append(jnp.concatenate([key_rows, flags], 1))
        value_ext.append(jnp.concatenate([value_rows.T, ones], 0))

    def score(c):
        parts = [q_ref[:, c * wide + h * HD : c * wide + (h + 1) * HD] for h in range(heads)]
        query_rows = jnp.concatenate([jnp.concatenate(parts, 0), row_part], 1)
        s_buf[c % slots] = dot(key_ext[c // per_group], query_rows, ((1,), (1,)))

    def weigh(c):
        slot, step = c % slots, min(2 * HD, wide)
        tops, factors = [], []
        for j in range(0, wide, step):
            tiles = [
                (k, slice(j, j + step)) for k in range(0, keys, TILE)
            ]
            top = None
            for k, lanes in tiles:
                part = s_buf[slot, k : k + TILE, lanes].reshape(TILE // 8, 8, step)
                part = jnp.max(part, 0)
                top = part if top is None else jnp.maximum(top, part)
            top = jnp.max(top, 0, keepdims=True)
            if state_in is not None:
                old = state_in[TOP_ROW : TOP_ROW + 1, c * wide + j : c * wide + j + step]
                top = jnp.maximum(top, old)
                factors.append(jnp.exp2((old - top) * TO_EXP2))
            for k, lanes in tiles:
                weights = jnp.exp2((s_buf[slot, k : k + TILE, lanes] - top) * TO_EXP2)
                p_buf[slot, k : k + TILE, lanes] = weights.astype(jnp.bfloat16)
            tops.append(top)
        top = jnp.concatenate(tops, 1)
        return top, (jnp.concatenate(factors, 1) if factors else None)

    def sum_up(c, top, factor):
        lanes = slice(c * wide, (c + 1) * wide)
        summed = dot(value_ext[c // per_group], p_buf[c % slots], ((1,), (0,)))[:TOP_ROW]
        if factor is not None:
            summed = summed + state_in[0:TOP_ROW, lanes] * factor
        if out_ref is None:
            state_out[0:TOP_ROW, lanes] = summed
            state_out[TOP_ROW : TOP_ROW + 1, lanes] = top
        else:
            finish(summed, top, c, heads, out_ref, log_ref)

    held = {}
    for t in range(chunks + 2):
        if t < chunks:
            score(t)
        if 0 <= t - 1 < chunks:
            held[t - 1] = weigh(t - 1)
        if 0 <= t - 2 < chunks:
            sum_up(t - 2, *held.pop(t - 2))


def finish(summed, top, c, heads, out_ref, log_ref):
    total = summed[HD : HD + 1]
    result = summed[:HD] * (1.0 / total)
    logs = top * SCALE + jnp.log(total)
    first = c * heads
    for h in range(heads):
        lanes = slice(h * HD, (h + 1) * HD)
        out_ref[:, (first + h) * HD : (first + h + 1) * HD] = result[:, lanes].T.astype(
            out_ref.dtype
        )
    log_ref[first : first + heads, :] = jnp.concatenate(
        [logs[:, h * HD : (h + 1) * HD] for h in range(heads)], 0
    )


def lane_row(rows):
    lane = lax.broadcasted_iota(jnp.int32, (rows, HD), 1)
    row = lax.broadcasted_iota(jnp.int32, (rows, HD), 0)
    return lane, row


def near_kernel(axis, win_ref, q_ref, own, other, state_out, s_buf, p_buf):
    me = lax.axis_index(axis)
    rows = own.shape[0]
    lane, row = lane_row(rows)
    first_seen = jnp.where((me & 1) == 1, jnp.maximum(rows - win_ref[me], 0), rows)
    other_flags = jnp.where((lane == 0) & (row < first_seen), 1.0, 0.0)
    own_flags = jnp.where((lane == row) & (row > 0), 1.0, 0.0)
    flags = jnp.concatenate([other_flags, own_flags], 0).astype(jnp.bfloat16)
    row_flags = jnp.where((lane == 0) | (lane > row), HIDDEN, 0.0).astype(jnp.bfloat16)
    run_chunks(
        q_ref, [other, own], flags, row_flags, None, state_out, s_buf, p_buf, None, None
    )


def far_kernel(axis, distances, last, win_ref, q_ref, *refs):
    me = lax.axis_index(axis)
    count = 2 * len(distances)
    blocks, state_in = refs[:count], refs[count]
    if last:
        state_out, (out_ref, log_ref, s_buf, p_buf) = None, refs[count + 1 :]
    else:
        (state_out, s_buf, p_buf), out_ref, log_ref = refs[count + 1 :], None, None
    rows = blocks[0].shape[0]
    lowest = jnp.maximum(me * rows - win_ref[me], 0)
    starts = [(who - d) * rows for d in distances for who in (me, me ^ 1)]
    needed = functools.reduce(jnp.logical_or, [s + rows > lowest for s in starts])

    @pl.when(needed)
    def _():
        lane, row = lane_row(rows)
        flags = jnp.concatenate(
            [jnp.where((lane == 0) & (row + s < lowest), 1.0, 0.0) for s in starts], 0
        ).astype(jnp.bfloat16)
        row_flags = jnp.where(lane == 0, HIDDEN, 0.0).astype(jnp.bfloat16)
        run_chunks(
            q_ref, blocks, flags, row_flags, state_in, state_out, s_buf, p_buf, out_ref, log_ref
        )

    @pl.when(jnp.logical_not(needed))
    def _():
        if last:
            wide = s_buf.shape[2]
            for c in range(q_ref.shape[1] // wide):
                lanes = slice(c * wide, (c + 1) * wide)
                top = state_in[TOP_ROW : TOP_ROW + 1, lanes]
                finish(state_in[0:TOP_ROW, lanes], top, c, wide // HD, out_ref, log_ref)
        else:
            state_out[...] = state_in[...]


def attend(kernel, windows, queries, blocks, state, last):
    rows, width = queries.shape
    heads = width // HD
    groups = blocks[0].shape[1] // (2 * HD)
    wide = HD * math.gcd(heads // groups, 4)
    keys = len(blocks) * rows
    operands = [windows, queries, *blocks]
    aliases = {}
    if state is not None:
        if not last:
            aliases = {len(operands): 0}
        operands.append(state)
    if last:
        out_shape = [
            jax.ShapeDtypeStruct((rows, width), jnp.bfloat16),
            jax.ShapeDtypeStruct((heads, rows), jnp.float32),
        ]
    else:
        out_shape = [jax.ShapeDtypeStruct((STATE_ROWS, width), jnp.float32)]
    return pl.pallas_call(
        kernel,
        in_specs=[SMEM] + [VMEM] * (len(operands) - 1),
        out_specs=[VMEM] * len(out_shape),
        out_shape=out_shape,
        scratch_shapes=[
            pltpu.VMEM((2, keys, wide), jnp.float32),
            pltpu.VMEM((2, keys, wide), jnp.bfloat16),
        ],
        input_output_aliases=aliases,
        cost_estimate=pl.CostEstimate(
            flops=4 * keys * rows * width,
            bytes_accessed=rows * width * 2,
            transcendentals=keys * rows * heads,
        ),
        compiler_params=pltpu.CompilerParams(vmem_limit_bytes=32 << 20),
    )(*operands)


def pack_kernel(k_ref, v_ref, out_ref):
    width = k_ref.shape[1]
    out_ref[:, :width] = k_ref[...]
    out_ref[:, width:] = v_ref[...]


def packed(keys, values):
    rows, width = keys.shape
    return pl.pallas_call(
        pack_kernel,
        in_specs=[VMEM] * 2,
        out_specs=VMEM,
        out_shape=jax.ShapeDtypeStruct((rows, 2 * width), keys.dtype),
    )(keys, values)


def tied(block, earlier):
    def kernel(block_ref, earlier_ref, out_ref):
        pass

    return pl.pallas_call(
        kernel,
        in_specs=[ANY, ANY],
        out_specs=ANY,
        out_shape=jax.ShapeDtypeStruct(block.shape, block.dtype),
        input_output_aliases={0: 0},
    )(block, earlier)


def on_device(queries, keys, values, windows):
    axis = "section"
    reach = lax.axis_size(axis) // 2
    own = packed(keys, values)
    other = swapped(own, axis)
    held = {4: shifted(own, axis, 4), 2: shifted(own, axis, 2)}
    (state,) = attend(
        functools.partial(near_kernel, axis), windows, queries, [own, other], None, False
    )
    for first in range(2, reach + 1, 4):
        distances = [d for d in (first + 2, first) if d <= reach]
        last = first + 4 > reach
        blocks = []
        for d in distances:
            held[d] = tied(held[d], state)
            if d + 4 <= reach:
                held[d + 4] = shifted(held[d], axis, 4)
            blocks += [held[d], swapped(held[d], axis)]
        result = attend(
            functools.partial(far_kernel, axis, distances, last),
            windows,
            queries,
            blocks,
            state,
            last,
        )
        state = result[0]
    return result[0], result[1].T


def solution(mesh):
    placed = (
        P(("groups", "section"), None),
        P(("groups", "section"), None),
        P(("groups", "section"), None),
        P("groups"),
    )
    return jax.shard_map(
        on_device,
        mesh=mesh,
        in_specs=placed,
        out_specs=(P(("groups", "section"), None), P(("groups", "section"), None)),
        check_vma=False,
    )
```

time: 34.8 us -> 31.6 us (0.908)
  the two profiles are of different devices: /device:TPU:29 before, /device:TPU:21 now
where the time goes in v1:
time: 31.6 us; the launch traced here: 31.3 us
  Pallas kernels  13.5 us (43%)
  local copies, waits for them, and re-layouts  8.79 us (28%)
  starting transfers between devices  6.67 us (21%)
  waiting for transfers between devices  1.56 us (5%)
  between operations  0.72 us (2%)
    pallas_call x3, Pallas kernels, attend(): pl.pallas_call(kernel, in_specs=[SMEM] + [VMEM] * (len(operands) - 1), ou...  12 us
    unnamed x26, local copies, waits for them, and re-layouts  8.79 us
    ppermute x4, starting transfers between devices, shifted(): lax.ppermute(block, axis, [(i, (i + distance) % size) for i in range(size)])  4.45 us
    ppermute x5, starting transfers between devices, swapped(): lax.ppermute(block, axis, [(i ^ 1, i) for i in range(lax.axis_size(axis))])  2.21 us
    ppermute x5, waiting for transfers between devices, swapped(): lax.ppermute(block, axis, [(i ^ 1, i) for i in range(lax.axis_size(axis))])  1.55 us
    pallas_call x1, Pallas kernels, packed(): pl.pallas_call(pack_kernel, in_specs=[VMEM] * 2, out_specs=VMEM, out_shap...  1.54 us
  transfers between devices with their start and end apart: 9, of which 2 were waited for; matrix products, arithmetic and copies ran while one was open for 0% of the time, Pallas kernels for 21%

profile of v1, /device:TPU:21, one launch (start us, length us, event | category | flops | bytes accessed | tf_op | source)
XLA Modules:
  0.0 31.3 jit_solution(7461287244614716003)
XLA Ops:
  0.6 1.5 %shard_map.59.own = bf16[128,512]{1,0:T(8,128)(2,1)} custom-call(bf16[128,256]{1,0:T(8,128)(2,1)} %k_ref.1, bf16[128,256]{1,0:T(8,128)(2,1)} %v_ref.1), custom_call_target="tpu_custom_call" | custom-call | tf_op jit(solution)/shard_map/pallas_call | solution.py:222
  2.2 0.7 %collective-permute-start.1 = (bf16[128,512]{1,0:T(8,128)(2,1)}, bf16[128,512]{1,0:T(8,128)(2,1)S(1)}, u32[]{:S(2)}, u32[]{:S(2)}) collective-permute-start(bf16[128,512]{1,0:T(8,128)(2,1)} %shard_map.59.own), channel_id=1, source_target_pairs={{1,0},{0,1},{3,2},{2,3},{5,4},{4,5},{7,6},{6,7},{9,8},{8,9},{11,10... | collective-permute-start | bytes 393224 | tf_op jit(solution)/shard_map/ppermute | solution.py:30
  2.8 1.2 %collective-permute-start.4 = (bf16[128,512]{1,0:T(8,128)(2,1)}, bf16[128,512]{1,0:T(8,128)(2,1)}, u32[]{:S(2)}, u32[]{:S(2)}) collective-permute-start(bf16[128,512]{1,0:T(8,128)(2,1)} %shard_map.59.own), channel_id=1, source_target_pairs={{0,2},{1,3},{2,4},{3,5},{4,6},{5,7},{6,8},{7,9},{8,10},{9,11},{10,... | collective-permute-start | bytes 393224 | tf_op jit(solution)/shard_map/ppermute | solution.py:26
  4.1 0.1 collective-permute-start
  4.1 1.2 %copy-done.4 = bf16[128,4096]{1,0:T(8,128)(2,1)S(1)} copy-done((bf16[128,4096]{1,0:T(8,128)(2,1)S(1)}, bf16[128,4096]{1,0:T(8,128)(2,1)}, u32[]{:S(2)}) %copy-start.4) | copy-done | bytes 1048600
  5.4 0.9 %copy-done.8 = bf16[128,512]{1,0:T(8,128)(2,1)S(1)} copy-done((bf16[128,512]{1,0:T(8,128)(2,1)S(1)}, bf16[128,512]{1,0:T(8,128)(2,1)}, u32[]{:S(2)}) %copy-start.8) | copy-done | bytes 131096
  6.3 0.7 %copy-done.11 = s32[16]{0:T(128)S(1)} copy-done((s32[16]{0:T(128)S(1)}, s32[16]{0:T(128)}, u32[]{:S(2)}) %copy-start.11) | copy-done | bytes 88
  6.9 2.3 %shard_map.60.earlier_ref.refs_4_ = f32[144,4096]{1,0:T(8,128)S(1)} custom-call(s32[16]{0:T(128)S(1)} %copy-done.11, bf16[128,4096]{1,0:T(8,128)(2,1)S(1)} %copy-done.4, bf16[128,512]{1,0:T(8,128)(2,1)S(1)} %copy-done.8, bf16[128,512]{1,0:T(8,128)(2,1)S(1)} %collective-permute-done.1.other), custom_call_target="tpu_custom_call" | custom-call | flops 536870912 | bytes 1048576 | tf_op jit(solution)/shard_map/pallas_call | solution.py:195
  9.3 1.4 %copy-done = f32[144,4096]{1,0:T(8,128)} copy-done((f32[144,4096]{1,0:T(8,128)}, f32[144,4096]{1,0:T(8,128)S(1)}, u32[]{:S(2)}) %copy-start) | copy-done | bytes 2359320
  10.8 0.3 %collective-permute-start.5 = (bf16[128,512]{1,0:T(8,128)(2,1)}, bf16[128,512]{1,0:T(8,128)(2,1)}, u32[]{:S(2)}, u32[]{:S(2)}) collective-permute-start(bf16[128,512]{1,0:T(8,128)(2,1)} %shard_map.62.refs_2_), channel_id=1, source_target_pairs={{1,0},{0,1},{3,2},{2,3},{5,4},{4,5},{7,6},{6,7},{9,8},{8,9},{11,10... | collective-permute-start | bytes 393224 | tf_op jit(solution)/shard_map/ppermute | solution.py:30
  11.1 0.7 %copy-done.6 = bf16[128,512]{1,0:T(8,128)(2,1)} copy-done((bf16[128,512]{1,0:T(8,128)(2,1)}, bf16[128,512]{1,0:T(8,128)(2,1)S(1)}, u32[]{:S(2)}) %copy-start.6) | copy-done | bytes 131096
  11.7 0.6 %collective-permute-start.3 = (bf16[128,512]{1,0:T(8,128)(2,1)}, bf16[128,512]{1,0:T(8,128)(2,1)S(1)}, u32[]{:S(2)}, u32[]{:S(2)}) collective-permute-start(bf16[128,512]{1,0:T(8,128)(2,1)} %shard_map.61.refs_0_), channel_id=1, source_target_pairs={{1,0},{0,1},{3,2},{2,3},{5,4},{4,5},{7,6},{6,7},{9,8},{8,9},{11,10... | collective-permute-start | bytes 393224 | tf_op jit(solution)/shard_map/ppermute | solution.py:30
  12.4 1.3 %collective-permute-start.7 = (bf16[128,512]{1,0:T(8,128)(2,1)}, bf16[128,512]{1,0:T(8,128)(2,1)}, u32[]{:S(2)}, u32[]{:S(2)}) collective-permute-start(bf16[128,512]{1,0:T(8,128)(2,1)} %shard_map.62.refs_2_), channel_id=1, source_target_pairs={{0,4},{1,5},{2,6},{3,7},{4,8},{5,9},{6,10},{7,11},{8,12},{9,13},{1... | collective-permute-start | bytes 393224 | tf_op jit(solution)/shard_map/ppermute | solution.py:26
  13.7 1.9 %collective-permute-start.2 = (bf16[128,512]{1,0:T(8,128)(2,1)}, bf16[128,512]{1,0:T(8,128)(2,1)S(1)}, u32[]{:S(2)}, u32[]{:S(2)}) collective-permute-start(bf16[128,512]{1,0:T(8,128)(2,1)} %shard_map.61.refs_0_), channel_id=1, source_target_pairs={{0,4},{1,5},{2,6},{3,7},{4,8},{5,9},{6,10},{7,11},{8,12},{9,13},{1... | collective-permute-start | bytes 393224 | tf_op jit(solution)/shard_map/ppermute | solution.py:26
  15.6 0.9 %copy-done.7 = bf16[128,512]{1,0:T(8,128)(2,1)S(1)} copy-done((bf16[128,512]{1,0:T(8,128)(2,1)S(1)}, bf16[128,512]{1,0:T(8,128)(2,1)}, u32[]{:S(2)}) %copy-start.7) | copy-done | bytes 131096
  16.5 4.3 %shard_map.63.earlier_ref.refs_4_ = f32[144,4096]{1,0:T(8,128)S(1)} custom-call(s32[16]{0:T(128)S(1)} %copy-done.12, bf16[128,4096]{1,0:T(8,128)(2,1)S(1)} %copy-done.5, bf16[128,512]{1,0:T(8,128)(2,1)S(1)} %copy-done.7, bf16[128,512]{1,0:T(8,128)(2,1)S(1)} %collective-permute-done.3.refs_1_, ...), custom_call_target="tpu_custom_call", output_to_operand_aliasing={{}: (6, {})} | custom-call | flops 1073741824 | bytes 1048576 | tf_op jit(solution)/shard_map/pallas_call | solution.py:195
  20.7 1.4 %copy-done.2 = f32[144,4096]{1,0:T(8,128)} copy-done((f32[144,4096]{1,0:T(8,128)}, f32[144,4096]{1,0:T(8,128)S(1)}, u32[]{:S(2)}) %copy-start.2) | copy-done | bytes 2359320
  22.2 0.6 %collective-permute-start.8 = (bf16[128,512]{1,0:T(8,128)(2,1)}, bf16[128,512]{1,0:T(8,128)(2,1)}, u32[]{:S(2)}, u32[]{:S(2)}) collective-permute-start(bf16[128,512]{1,0:T(8,128)(2,1)} %shard_map.65.refs_2_), channel_id=1, source_target_pairs={{1,0},{0,1},{3,2},{2,3},{5,4},{4,5},{7,6},{6,7},{9,8},{8,9},{11,10... | collective-permute-start | bytes 393224 | tf_op jit(solution)/shard_map/ppermute | solution.py:30
  22.8 0.7 %copy-done.9 = bf16[128,512]{1,0:T(8,128)(2,1)} copy-done((bf16[128,512]{1,0:T(8,128)(2,1)}, bf16[128,512]{1,0:T(8,128)(2,1)S(1)}, u32[]{:S(2)}) %copy-start.9) | copy-done | bytes 131096
  23.4 0.0 collective-permute-start.6
  23.4 0.6 %collective-permute-done.8.refs_3_ = bf16[128,512]{1,0:T(8,128)(2,1)} collective-permute-done((bf16[128,512]{1,0:T(8,128)(2,1)}, bf16[128,512]{1,0:T(8,128)(2,1)}, u32[]{:S(2)}, u32[]{:S(2)}) %collective-permute-start.8) | collective-permute-done | bytes 131104 | tf_op jit(solution)/shard_map/ppermute | solution.py:30
  24.1 0.9 %collective-permute-done.6.refs_1_ = bf16[128,512]{1,0:T(8,128)(2,1)S(1)} collective-permute-done((bf16[128,512]{1,0:T(8,128)(2,1)}, bf16[128,512]{1,0:T(8,128)(2,1)S(1)}, u32[]{:S(2)}, u32[]{:S(2)}) %collective-permute-start.6) | collective-permute-done | bytes 131104 | tf_op jit(solution)/shard_map/ppermute | solution.py:30
  25.0 0.9 %copy-done.10 = bf16[128,512]{1,0:T(8,128)(2,1)S(1)} copy-done((bf16[128,512]{1,0:T(8,128)(2,1)S(1)}, bf16[128,512]{1,0:T(8,128)(2,1)}, u32[]{:S(2)}) %copy-start.10) | copy-done | bytes 131096
  25.9 5.4 %shard_map.66 = (bf16[128,4096]{1,0:T(8,128)(2,1)}, f32[32,128]{1,0:T(8,128)}) custom-call(s32[16]{0:T(128)S(1)} %copy-done.12, bf16[128,4096]{1,0:T(8,128)(2,1)S(1)} %copy-done.5, bf16[128,512]{1,0:T(8,128)(2,1)S(1)} %copy-done.10, bf16[128,512]{1,0:T(8,128)(2,1)S(1)} %collective-permute-done.6.refs_1_, bf16[128,512]{1,0:T(8,128)(2,1)} %shard_map.65.refs_2_, ...), custom_call_target="tpu_custom_call" | custom-call | flops 1073741824 | bytes 1048576 | tf_op jit(solution)/shard_map/pallas_call | solution.py:195
  (28 shorter events, 0.1 us)
Async XLA Ops:
  2.2 2.0 %collective-permute-start.1 = (bf16[128,512]{1,0:T(8,128)(2,1)}, bf16[128,512]{1,0:T(8,128)(2,1)S(1)}, u32[]{:S(2)}, u32[]{:S(2)}) collective-permute-start(bf16[128,512]{1,0:T(8,128)(2,1)} %shard_map.59.own), channel_id=1, source_target_pairs={{1,0},{0,1},{3,2},{2,3},{5,4},{4,5},{7,6},{6,7},{9,8},{8,9},{11,10... | collective-permute-start | bytes 393224 | tf_op jit(solution)/shard_map/ppermute | solution.py:30
  2.8 7.9 %collective-permute-start.4 = (bf16[128,512]{1,0:T(8,128)(2,1)}, bf16[128,512]{1,0:T(8,128)(2,1)}, u32[]{:S(2)}, u32[]{:S(2)}) collective-permute-start(bf16[128,512]{1,0:T(8,128)(2,1)} %shard_map.59.own), channel_id=1, source_target_pairs={{0,2},{1,3},{2,4},{3,5},{4,6},{5,7},{6,8},{7,9},{8,10},{9,11},{10,... | collective-permute-start | bytes 393224 | tf_op jit(solution)/shard_map/ppermute | solution.py:26
  4.1 7.0 %collective-permute-start = (bf16[128,512]{1,0:T(8,128)(2,1)}, bf16[128,512]{1,0:T(8,128)(2,1)S(1)}, u32[]{:S(2)}, u32[]{:S(2)}) collective-permute-start(bf16[128,512]{1,0:T(8,128)(2,1)} %shard_map.59.own), channel_id=1, source_target_pairs={{0,4},{1,5},{2,6},{3,7},{4,8},{5,9},{6,10},{7,11},{8,12},{9,13},{1... | collective-permute-start | bytes 393224 | tf_op jit(solution)/shard_map/ppermute | solution.py:26
  4.1 1.2 %copy-start.4 = (bf16[128,4096]{1,0:T(8,128)(2,1)S(1)}, bf16[128,4096]{1,0:T(8,128)(2,1)}, u32[]{:S(2)}) copy-start(bf16[128,4096]{1,0:T(8,128)(2,1)} %q_ref.5) | copy-start | bytes 3145732
  5.4 0.9 %copy-start.8 = (bf16[128,512]{1,0:T(8,128)(2,1)S(1)}, bf16[128,512]{1,0:T(8,128)(2,1)}, u32[]{:S(2)}) copy-start(bf16[128,512]{1,0:T(8,128)(2,1)} %shard_map.59.own) | copy-start | bytes 393220
  6.3 0.7 %copy-start.11 = (s32[16]{0:T(128)S(1)}, s32[16]{0:T(128)}, u32[]{:S(2)}) copy-start(s32[16]{0:T(128)} %win_ref.5) | copy-start | bytes 196
  9.3 1.4 %copy-start = (f32[144,4096]{1,0:T(8,128)}, f32[144,4096]{1,0:T(8,128)S(1)}, u32[]{:S(2)}) copy-start(f32[144,4096]{1,0:T(8,128)S(1)} %shard_map.60.earlier_ref.refs_4_) | copy-start | bytes 7077892
  10.7 4.8 %copy-start.5 = (bf16[128,4096]{1,0:T(8,128)(2,1)S(1)}, bf16[128,4096]{1,0:T(8,128)(2,1)}, u32[]{:S(2)}) copy-start(bf16[128,4096]{1,0:T(8,128)(2,1)} %q_ref.5) | copy-start | bytes 3145732
  10.7 4.8 %copy-start.12 = (s32[16]{0:T(128)S(1)}, s32[16]{0:T(128)}, u32[]{:S(2)}) copy-start(s32[16]{0:T(128)} %win_ref.5) | copy-start | bytes 196
  10.7 4.8 %copy-start.1 = (f32[144,4096]{1,0:T(8,128)S(1)}, f32[144,4096]{1,0:T(8,128)}, u32[]{:S(2)}) copy-start(f32[144,4096]{1,0:T(8,128)} %copy-done) | copy-start | bytes 7077892
  10.8 4.8 %collective-permute-start.5 = (bf16[128,512]{1,0:T(8,128)(2,1)}, bf16[128,512]{1,0:T(8,128)(2,1)}, u32[]{:S(2)}, u32[]{:S(2)}) collective-permute-start(bf16[128,512]{1,0:T(8,128)(2,1)} %shard_map.62.refs_2_), channel_id=1, source_target_pairs={{1,0},{0,1},{3,2},{2,3},{5,4},{4,5},{7,6},{6,7},{9,8},{8,9},{11,10... | collective-permute-start | bytes 393224 | tf_op jit(solution)/shard_map/ppermute | solution.py:30
  11.1 0.7 %copy-start.6 = (bf16[128,512]{1,0:T(8,128)(2,1)}, bf16[128,512]{1,0:T(8,128)(2,1)S(1)}, u32[]{:S(2)}) copy-start(bf16[128,512]{1,0:T(8,128)(2,1)S(1)} %collective-permute-done.block_ref) | copy-start | bytes 393220
  11.7 3.8 %collective-permute-start.3 = (bf16[128,512]{1,0:T(8,128)(2,1)}, bf16[128,512]{1,0:T(8,128)(2,1)S(1)}, u32[]{:S(2)}, u32[]{:S(2)}) collective-permute-start(bf16[128,512]{1,0:T(8,128)(2,1)} %shard_map.61.refs_0_), channel_id=1, source_target_pairs={{1,0},{0,1},{3,2},{2,3},{5,4},{4,5},{7,6},{6,7},{9,8},{8,9},{11,10... | collective-permute-start | bytes 393224 | tf_op jit(solution)/shard_map/ppermute | solution.py:30
  12.4 9.8 %collective-permute-start.7 = (bf16[128,512]{1,0:T(8,128)(2,1)}, bf16[128,512]{1,0:T(8,128)(2,1)}, u32[]{:S(2)}, u32[]{:S(2)}) collective-permute-start(bf16[128,512]{1,0:T(8,128)(2,1)} %shard_map.62.refs_2_), channel_id=1, source_target_pairs={{0,4},{1,5},{2,6},{3,7},{4,8},{5,9},{6,10},{7,11},{8,12},{9,13},{1... | collective-permute-start | bytes 393224 | tf_op jit(solution)/shard_map/ppermute | solution.py:26
  13.7 9.1 %collective-permute-start.2 = (bf16[128,512]{1,0:T(8,128)(2,1)}, bf16[128,512]{1,0:T(8,128)(2,1)S(1)}, u32[]{:S(2)}, u32[]{:S(2)}) collective-permute-start(bf16[128,512]{1,0:T(8,128)(2,1)} %shard_map.61.refs_0_), channel_id=1, source_target_pairs={{0,4},{1,5},{2,6},{3,7},{4,8},{5,9},{6,10},{7,11},{8,12},{9,13},{1... | collective-permute-start | bytes 393224 | tf_op jit(solution)/shard_map/ppermute | solution.py:26
  15.6 0.9 %copy-start.7 = (bf16[128,512]{1,0:T(8,128)(2,1)S(1)}, bf16[128,512]{1,0:T(8,128)(2,1)}, u32[]{:S(2)}) copy-start(bf16[128,512]{1,0:T(8,128)(2,1)} %shard_map.61.refs_0_) | copy-start | bytes 393220
  20.7 1.4 %copy-start.2 = (f32[144,4096]{1,0:T(8,128)}, f32[144,4096]{1,0:T(8,128)S(1)}, u32[]{:S(2)}) copy-start(f32[144,4096]{1,0:T(8,128)S(1)} %shard_map.63.earlier_ref.refs_4_) | copy-start | bytes 7077892
  22.2 2.8 %copy-start.3 = (f32[144,4096]{1,0:T(8,128)S(1)}, f32[144,4096]{1,0:T(8,128)}, u32[]{:S(2)}) copy-start(f32[144,4096]{1,0:T(8,128)} %copy-done.2) | copy-start | bytes 7077892
  22.2 1.9 %collective-permute-start.8 = (bf16[128,512]{1,0:T(8,128)(2,1)}, bf16[128,512]{1,0:T(8,128)(2,1)}, u32[]{:S(2)}, u32[]{:S(2)}) collective-permute-start(bf16[128,512]{1,0:T(8,128)(2,1)} %shard_map.65.refs_2_), channel_id=1, source_target_pairs={{1,0},{0,1},{3,2},{2,3},{5,4},{4,5},{7,6},{6,7},{9,8},{8,9},{11,10... | collective-permute-start | bytes 393224 | tf_op jit(solution)/shard_map/ppermute | solution.py:30
  22.8 0.7 %copy-start.9 = (bf16[128,512]{1,0:T(8,128)(2,1)}, bf16[128,512]{1,0:T(8,128)(2,1)S(1)}, u32[]{:S(2)}) copy-start(bf16[128,512]{1,0:T(8,128)(2,1)S(1)} %collective-permute-done.2.block_ref) | copy-start | bytes 393220
  23.4 1.6 %collective-permute-start.6 = (bf16[128,512]{1,0:T(8,128)(2,1)}, bf16[128,512]{1,0:T(8,128)(2,1)S(1)}, u32[]{:S(2)}, u32[]{:S(2)}) collective-permute-start(bf16[128,512]{1,0:T(8,128)(2,1)} %shard_map.64.refs_0_), channel_id=1, source_target_pairs={{1,0},{0,1},{3,2},{2,3},{5,4},{4,5},{7,6},{6,7},{9,8},{8,9},{11,10... | collective-permute-start | bytes 393224 | tf_op jit(solution)/shard_map/ppermute | solution.py:30
  25.0 0.9 %copy-start.10 = (bf16[128,512]{1,0:T(8,128)(2,1)S(1)}, bf16[128,512]{1,0:T(8,128)(2,1)}, u32[]{:S(2)}) copy-start(bf16[128,512]{1,0:T(8,128)(2,1)} %shard_map.64.refs_0_) | copy-start | bytes 393220

commit v2 on v1

--- a/solution.py
+++ b/solution.py
@@ -17,8 +17,10 @@
 TOP_ROW = HD + SUM_ROWS
 TILE = 64
 VMEM = pl.BlockSpec(memory_space=pltpu.VMEM)
-ANY = pl.BlockSpec(memory_space=pl.ANY)
+SMALL = pltpu.CompilerParams(vmem_limit_bytes=1 << 20)
 SMEM = pl.BlockSpec(memory_space=pltpu.SMEM)
+HBM = pl.BlockSpec(memory_space=pltpu.HBM)
+MARK = (8, HD)
 
 
 def shifted(block, axis, distance):
@@ -123,11 +125,17 @@
     return lane, row
 
 
-def near_kernel(axis, win_ref, q_ref, own, other, state_out, s_buf, p_buf):
+def lowest_of(mark_ref):
+    return jnp.max(mark_ref[...]).astype(jnp.int32)
+
+
+def near_kernel(axis, win_ref, q_ref, own, other, state_out, mark, s_buf, p_buf):
     me = lax.axis_index(axis)
     rows = own.shape[0]
+    lowest = jnp.maximum(me * rows - win_ref[me], 0)
+    mark[...] = jnp.full(mark.shape, lowest.astype(jnp.float32))
     lane, row = lane_row(rows)
-    first_seen = jnp.where((me & 1) == 1, jnp.maximum(rows - win_ref[me], 0), rows)
+    first_seen = jnp.where((me & 1) == 1, lowest - (me - 1) * rows, rows)
     other_flags = jnp.where((lane == 0) & (row < first_seen), 1.0, 0.0)
     own_flags = jnp.where((lane == row) & (row > 0), 1.0, 0.0)
     flags = jnp.concatenate([other_flags, own_flags], 0).astype(jnp.bfloat16)
@@ -137,16 +145,17 @@
     )
 
 
-def far_kernel(axis, distances, last, win_ref, q_ref, *refs):
+def far_kernel(axis, distances, last, mark_in, q_ref, *refs):
     me = lax.axis_index(axis)
     count = 2 * len(distances)
     blocks, state_in = refs[:count], refs[count]
     if last:
         state_out, (out_ref, log_ref, s_buf, p_buf) = None, refs[count + 1 :]
     else:
-        (state_out, s_buf, p_buf), out_ref, log_ref = refs[count + 1 :], None, None
+        (state_out, mark, s_buf, p_buf), out_ref, log_ref = refs[count + 1 :], None, None
+        mark[...] = mark_in[...]
     rows = blocks[0].shape[0]
-    lowest = jnp.maximum(me * rows - win_ref[me], 0)
+    lowest = lowest_of(mark_in)
     starts = [(who - d) * rows for d in distances for who in (me, me ^ 1)]
     needed = functools.reduce(jnp.logical_or, [s + rows > lowest for s in starts])
 
@@ -173,13 +182,13 @@
             state_out[...] = state_in[...]
 
 
-def attend(kernel, windows, queries, blocks, state, last):
+def attend(kernel, mark, queries, blocks, state, last):
     rows, width = queries.shape
     heads = width // HD
     groups = blocks[0].shape[1] // (2 * HD)
     wide = HD * math.gcd(heads // groups, 4)
     keys = len(blocks) * rows
-    operands = [windows, queries, *blocks]
+    operands = [mark, queries, *blocks]
     aliases = {}
     if state is not None:
         if not last:
@@ -191,10 +200,13 @@
             jax.ShapeDtypeStruct((heads, rows), jnp.float32),
         ]
     else:
-        out_shape = [jax.ShapeDtypeStruct((STATE_ROWS, width), jnp.float32)]
+        out_shape = [
+            jax.ShapeDtypeStruct((STATE_ROWS, width), jnp.float32),
+            jax.ShapeDtypeStruct(MARK, jnp.float32),
+        ]
     return pl.pallas_call(
         kernel,
-        in_specs=[SMEM] + [VMEM] * (len(operands) - 1),
+        in_specs=[VMEM if state is not None else SMEM] + [VMEM] * (len(operands) - 1),
         out_specs=[VMEM] * len(out_shape),
         out_shape=out_shape,
         scratch_shapes=[
@@ -207,23 +219,31 @@
             bytes_accessed=rows * width * 2,
             transcendentals=keys * rows * heads,
         ),
-        compiler_params=pltpu.CompilerParams(vmem_limit_bytes=32 << 20),
+        compiler_params=pltpu.CompilerParams(vmem_limit_bytes=12 << 20),
     )(*operands)
 
 
-def pack_kernel(k_ref, v_ref, out_ref):
-    width = k_ref.shape[1]
-    out_ref[:, :width] = k_ref[...]
-    out_ref[:, width:] = v_ref[...]
+def pack_kernel(k_hbm, v_hbm, own_hbm, sems):
+    width = k_hbm.shape[1]
+    copies = [
+        pltpu.make_async_copy(k_hbm, own_hbm.at[:, pl.ds(0, width)], sems.at[0]),
+        pltpu.make_async_copy(v_hbm, own_hbm.at[:, pl.ds(width, width)], sems.at[1]),
+    ]
+    for copy in copies:
+        copy.start()
+    for copy in copies:
+        copy.wait()
 
 
 def packed(keys, values):
     rows, width = keys.shape
     return pl.pallas_call(
         pack_kernel,
-        in_specs=[VMEM] * 2,
-        out_specs=VMEM,
+        in_specs=[HBM] * 2,
+        out_specs=HBM,
         out_shape=jax.ShapeDtypeStruct((rows, 2 * width), keys.dtype),
+        scratch_shapes=[pltpu.SemaphoreType.DMA((2,))],
+        compiler_params=pltpu.CompilerParams(vmem_limit_bytes=60 << 20),
     )(keys, values)
 
 
@@ -233,10 +253,11 @@
 
     return pl.pallas_call(
         kernel,
-        in_specs=[ANY, ANY],
-        out_specs=ANY,
+        in_specs=[VMEM, VMEM],
+        out_specs=VMEM,
         out_shape=jax.ShapeDtypeStruct(block.shape, block.dtype),
         input_output_aliases={0: 0},
+        compiler_params=SMALL,
     )(block, earlier)
 
 
@@ -246,7 +267,7 @@
     own = packed(keys, values)
     other = swapped(own, axis)
     held = {4: shifted(own, axis, 4), 2: shifted(own, axis, 2)}
-    (state,) = attend(
+    state, mark = attend(
         functools.partial(near_kernel, axis), windows, queries, [own, other], None, False
     )
     for first in range(2, reach + 1, 4):
@@ -254,19 +275,19 @@
         last = first + 4 > reach
         blocks = []
         for d in distances:
-            held[d] = tied(held[d], state)
+            held[d] = tied(held[d], mark)
             if d + 4 <= reach:
                 held[d + 4] = shifted(held[d], axis, 4)
             blocks += [held[d], swapped(held[d], axis)]
         result = attend(
             functools.partial(far_kernel, axis, distances, last),
-            windows,
+            mark,
             queries,
             blocks,
             state,
             last,
         )
-        state = result[0]
+        state, mark = result
     return result[0], result[1].T
 
 

time: 31.6 us -> 30.4 us (0.962)
  the two profiles are of different devices: /device:TPU:21 before, /device:TPU:0 now
where the time goes in v2:
time: 30.4 us; the launch traced here: 29.8 us
  waiting for transfers between devices  9.59 us (32%)
  Pallas kernels  9.3 us (31%)
  starting transfers between devices  7.47 us (25%)
  local copies, waits for them, and re-layouts  2.81 us (9%)
  between operations  0.67 us (2%)
    ppermute x4, waiting for transfers between devices, shifted(): lax.ppermute(block, axis, [(i, (i + distance) % size) for i in range(size)])  8.24 us
    ppermute x4, starting transfers between devices, shifted(): lax.ppermute(block, axis, [(i, (i + distance) % size) for i in range(size)])  6.5 us
    pallas_call x1, Pallas kernels, packed(): pl.pallas_call(pack_kernel, in_specs=[HBM] * 2, out_specs=HBM, out_shape=...  5.09 us
    pallas_call x3, Pallas kernels, attend(): pl.pallas_call(kernel, in_specs=[VMEM if state is not None else SMEM] + [...  4.21 us
    unnamed x6, local copies, waits for them, and re-layouts  2.81 us
    ppermute x5, waiting for transfers between devices, swapped(): lax.ppermute(block, axis, [(i ^ 1, i) for i in range(lax.axis_size(axis))])  1.35 us
    ppermute x5, starting transfers between devices, swapped(): lax.ppermute(block, axis, [(i ^ 1, i) for i in range(lax.axis_size(axis))])  0.97 us
  transfers between devices with their start and end apart: 9, of which 5 were waited for; matrix products, arithmetic and copies ran while one was open for 0% of the time, Pallas kernels for 9%

profile of v2, /device:TPU:0, one launch (start us, length us, event | category | flops | bytes accessed | tf_op | source)
XLA Modules:
  0.0 29.8 jit_solution(12855855066356693579)
XLA Ops:
  0.6 5.1 %shard_map.59.own = bf16[128,512]{1,0:T(8,128)(2,1)} custom-call(bf16[128,256]{1,0:T(8,128)(2,1)} %k_hbm.1, bf16[128,256]{1,0:T(8,128)(2,1)} %v_hbm.1), custom_call_target="tpu_custom_call" | custom-call | tf_op jit(solution)/shard_map/pallas_call | solution.py:240
  5.7 0.5 %collective-permute-start = (bf16[128,512]{1,0:T(8,128)(2,1)}, bf16[128,512]{1,0:T(8,128)(2,1)S(1)}, u32[]{:S(2)}, u32[]{:S(2)}) collective-permute-start(bf16[128,512]{1,0:T(8,128)(2,1)} %shard_map.59.own), channel_id=1, source_target_pairs={{1,0},{0,1},{3,2},{2,3},{5,4},{4,5},{7,6},{6,7},{9,8},{8,9},{11,10... | collective-permute-start | bytes 393224 | tf_op jit(solution)/shard_map/ppermute | solution.py:32
  6.2 2.6 %collective-permute-start.3 = (bf16[128,512]{1,0:T(8,128)(2,1)}, bf16[128,512]{1,0:T(8,128)(2,1)S(1)}, u32[]{:S(2)}, u32[]{:S(2)}) collective-permute-start(bf16[128,512]{1,0:T(8,128)(2,1)} %shard_map.59.own), channel_id=1, source_target_pairs={{0,2},{1,3},{2,4},{3,5},{4,6},{5,7},{6,8},{7,9},{8,10},{9,11},{10,... | collective-permute-start | bytes 393224 | tf_op jit(solution)/shard_map/ppermute | solution.py:28
  8.8 1.6 %collective-permute-start.1 = (bf16[128,512]{1,0:T(8,128)(2,1)}, bf16[128,512]{1,0:T(8,128)(2,1)S(1)}, u32[]{:S(2)}, u32[]{:S(2)}) collective-permute-start(bf16[128,512]{1,0:T(8,128)(2,1)} %shard_map.59.own), channel_id=1, source_target_pairs={{0,4},{1,5},{2,6},{3,7},{4,8},{5,9},{6,10},{7,11},{8,12},{9,13},{1... | collective-permute-start | bytes 393224 | tf_op jit(solution)/shard_map/ppermute | solution.py:28
  10.4 0.0 collective-permute-done.other
  10.4 0.9 %copy-done = bf16[128,512]{1,0:T(8,128)(2,1)S(1)} copy-done((bf16[128,512]{1,0:T(8,128)(2,1)S(1)}, bf16[128,512]{1,0:T(8,128)(2,1)}, u32[]{:S(2)}) %copy-start) | copy-done | bytes 131096
  11.3 1.2 %copy-done.1 = bf16[128,4096]{1,0:T(8,128)(2,1)S(1)} copy-done((bf16[128,4096]{1,0:T(8,128)(2,1)S(1)}, bf16[128,4096]{1,0:T(8,128)(2,1)}, u32[]{:S(2)}) %copy-start.1) | copy-done | bytes 1048600
  12.6 0.7 %copy-done.2 = s32[16]{0:T(128)S(1)} copy-done((s32[16]{0:T(128)S(1)}, s32[16]{0:T(128)}, u32[]{:S(2)}) %copy-start.2) | copy-done | bytes 88
  13.2 2.3 %shard_map.60 = (f32[144,4096]{1,0:T(8,128)S(1)}, f32[8,128]{1,0:T(8,128)S(1)}) custom-call(s32[16]{0:T(128)S(1)} %copy-done.2, bf16[128,4096]{1,0:T(8,128)(2,1)S(1)} %copy-done.1, bf16[128,512]{1,0:T(8,128)(2,1)S(1)} %copy-done, bf16[128,512]{1,0:T(8,128)(2,1)S(1)} %collective-permute-done.other), custom_call_target="tpu_custom_call" | custom-call | flops 536870912 | bytes 1048576 | tf_op jit(solution)/shard_map/pallas_call | solution.py:207
  15.5 0.9 %collective-permute-done.3.block_ref = bf16[128,512]{1,0:T(8,128)(2,1)S(1)} collective-permute-done((bf16[128,512]{1,0:T(8,128)(2,1)}, bf16[128,512]{1,0:T(8,128)(2,1)S(1)}, u32[]{:S(2)}, u32[]{:S(2)}) %collective-permute-start.3) | collective-permute-done | bytes 131104 | tf_op jit(solution)/shard_map/ppermute | solution.py:28
  16.4 0.0 collective-permute-start.4
  16.4 0.1 collective-permute-done.1.block_ref
  16.5 0.4 %collective-permute-start.2 = (bf16[128,512]{1,0:T(8,128)(2,1)S(1)}, bf16[128,512]{1,0:T(8,128)(2,1)S(1)}, u32[]{:S(2)}, u32[]{:S(2)}) collective-permute-start(bf16[128,512]{1,0:T(8,128)(2,1)S(1)} %shard_map.61.refs_0_), channel_id=1, source_target_pairs={{1,0},{0,1},{3,2},{2,3},{5,4},{4,5},{7,6},{6,7},{9,8},{8,9},{11,10... | collective-permute-start | bytes 393224 | tf_op jit(solution)/shard_map/ppermute | solution.py:32
  16.9 0.8 %collective-permute-start.7 = (bf16[128,512]{1,0:T(8,128)(2,1)S(1)}, bf16[128,512]{1,0:T(8,128)(2,1)S(1)}, u32[]{:S(2)}, u32[]{:S(2)}) collective-permute-start(bf16[128,512]{1,0:T(8,128)(2,1)S(1)} %shard_map.62.refs_2_), channel_id=1, source_target_pairs={{0,4},{1,5},{2,6},{3,7},{4,8},{5,9},{6,10},{7,11},{8,12},{9,13},{1... | collective-permute-start | bytes 393224 | tf_op jit(solution)/shard_map/ppermute | solution.py:28
  17.7 1.6 %collective-permute-start.5 = (bf16[128,512]{1,0:T(8,128)(2,1)S(1)}, bf16[128,512]{1,0:T(8,128)(2,1)S(1)}, u32[]{:S(2)}, u32[]{:S(2)}) collective-permute-start(bf16[128,512]{1,0:T(8,128)(2,1)S(1)} %shard_map.61.refs_0_), channel_id=1, source_target_pairs={{0,4},{1,5},{2,6},{3,7},{4,8},{5,9},{6,10},{7,11},{8,12},{9,13},{1... | collective-permute-start | bytes 393224 | tf_op jit(solution)/shard_map/ppermute | solution.py:28
  19.3 0.0 collective-permute-done.4.refs_3_
  19.3 0.0 collective-permute-done.2.refs_1_
  19.3 0.4 %shard_map.63 = (f32[144,4096]{1,0:T(8,128)S(1)}, f32[8,128]{1,0:T(8,128)S(1)}) custom-call(f32[8,128]{1,0:T(8,128)S(1)} %get-tuple-element.8.earlier_ref.mark_in, bf16[128,4096]{1,0:T(8,128)(2,1)S(1)} %copy-done.1, bf16[128,512]{1,0:T(8,128)(2,1)S(1)} %shard_map.61.refs_0_, ...), custom_call_target="tpu_custom_call", output_to_operand_aliasing={{0}: (6, {})} | custom-call | flops 1073741824 | bytes 1048576 | tf_op jit(solution)/shard_map/pallas_call | solution.py:207
  19.7 5.4 %collective-permute-done.7.block_ref = bf16[128,512]{1,0:T(8,128)(2,1)S(1)} collective-permute-done((bf16[128,512]{1,0:T(8,128)(2,1)S(1)}, bf16[128,512]{1,0:T(8,128)(2,1)S(1)}, u32[]{:S(2)}, u32[]{:S(2)}) %collective-permute-start.7) | collective-permute-done | bytes 131104 | tf_op jit(solution)/shard_map/ppermute | solution.py:28
  25.1 0.0 collective-permute-start.8
  25.1 1.9 %collective-permute-done.5.block_ref = bf16[128,512]{1,0:T(8,128)(2,1)S(1)} collective-permute-done((bf16[128,512]{1,0:T(8,128)(2,1)S(1)}, bf16[128,512]{1,0:T(8,128)(2,1)S(1)}, u32[]{:S(2)}, u32[]{:S(2)}) %collective-permute-start.5) | collective-permute-done | bytes 131104 | tf_op jit(solution)/shard_map/ppermute | solution.py:28
  27.0 0.0 collective-permute-start.6
  27.0 1.3 %collective-permute-done.6.refs_1_ = bf16[128,512]{1,0:T(8,128)(2,1)S(1)} collective-permute-done((bf16[128,512]{1,0:T(8,128)(2,1)S(1)}, bf16[128,512]{1,0:T(8,128)(2,1)S(1)}, u32[]{:S(2)}, u32[]{:S(2)}) %collective-permute-start.6) | collective-permute-done | bytes 131104 | tf_op jit(solution)/shard_map/ppermute | solution.py:32
  28.4 1.5 %shard_map.66 = (bf16[128,4096]{1,0:T(8,128)(2,1)}, f32[32,128]{1,0:T(8,128)}) custom-call(f32[8,128]{1,0:T(8,128)S(1)} %get-tuple-element.10.earlier_ref.mark_in, bf16[128,4096]{1,0:T(8,128)(2,1)S(1)} %copy-done.1, bf16[128,512]{1,0:T(8,128)(2,1)S(1)} %shard_map.64.refs_0_, bf16[128,512]{1,0:T(8,128)(2,1)S(1)} %collective-permute-done.6.refs_1_, ...), custom_call_target="tpu_custom_call" | custom-call | flops 1073741824 | bytes 1048576 | tf_op jit(solution)/shard_map/pallas_call | solution.py:207
  (8 shorter events, 0.0 us)
Async XLA Ops:
  5.7 4.7 %collective-permute-start = (bf16[128,512]{1,0:T(8,128)(2,1)}, bf16[128,512]{1,0:T(8,128)(2,1)S(1)}, u32[]{:S(2)}, u32[]{:S(2)}) collective-permute-start(bf16[128,512]{1,0:T(8,128)(2,1)} %shard_map.59.own), channel_id=1, source_target_pairs={{1,0},{0,1},{3,2},{2,3},{5,4},{4,5},{7,6},{6,7},{9,8},{8,9},{11,10... | collective-permute-start | bytes 393224 | tf_op jit(solution)/shard_map/ppermute | solution.py:32
  6.2 10.2 %collective-permute-start.3 = (bf16[128,512]{1,0:T(8,128)(2,1)}, bf16[128,512]{1,0:T(8,128)(2,1)S(1)}, u32[]{:S(2)}, u32[]{:S(2)}) collective-permute-start(bf16[128,512]{1,0:T(8,128)(2,1)} %shard_map.59.own), channel_id=1, source_target_pairs={{0,2},{1,3},{2,4},{3,5},{4,6},{5,7},{6,8},{7,9},{8,10},{9,11},{10,... | collective-permute-start | bytes 393224 | tf_op jit(solution)/shard_map/ppermute | solution.py:28
  8.8 7.7 %collective-permute-start.1 = (bf16[128,512]{1,0:T(8,128)(2,1)}, bf16[128,512]{1,0:T(8,128)(2,1)S(1)}, u32[]{:S(2)}, u32[]{:S(2)}) collective-permute-start(bf16[128,512]{1,0:T(8,128)(2,1)} %shard_map.59.own), channel_id=1, source_target_pairs={{0,4},{1,5},{2,6},{3,7},{4,8},{5,9},{6,10},{7,11},{8,12},{9,13},{1... | collective-permute-start | bytes 393224 | tf_op jit(solution)/shard_map/ppermute | solution.py:28
  10.4 0.9 %copy-start = (bf16[128,512]{1,0:T(8,128)(2,1)S(1)}, bf16[128,512]{1,0:T(8,128)(2,1)}, u32[]{:S(2)}) copy-start(bf16[128,512]{1,0:T(8,128)(2,1)} %shard_map.59.own) | copy-start | bytes 393220
  11.3 1.2 %copy-start.1 = (bf16[128,4096]{1,0:T(8,128)(2,1)S(1)}, bf16[128,4096]{1,0:T(8,128)(2,1)}, u32[]{:S(2)}) copy-start(bf16[128,4096]{1,0:T(8,128)(2,1)} %q_ref.5) | copy-start | bytes 3145732
  12.6 0.7 %copy-start.2 = (s32[16]{0:T(128)S(1)}, s32[16]{0:T(128)}, u32[]{:S(2)}) copy-start(s32[16]{0:T(128)} %win_ref.1) | copy-start | bytes 196
  16.4 2.9 %collective-permute-start.4 = (bf16[128,512]{1,0:T(8,128)(2,1)S(1)}, bf16[128,512]{1,0:T(8,128)(2,1)S(1)}, u32[]{:S(2)}, u32[]{:S(2)}) collective-permute-start(bf16[128,512]{1,0:T(8,128)(2,1)S(1)} %shard_map.62.refs_2_), channel_id=1, source_target_pairs={{1,0},{0,1},{3,2},{2,3},{5,4},{4,5},{7,6},{6,7},{9,8},{8,9},{11,10... | collective-permute-start | bytes 393224 | tf_op jit(solution)/shard_map/ppermute | solution.py:32
  16.5 2.8 %collective-permute-start.2 = (bf16[128,512]{1,0:T(8,128)(2,1)S(1)}, bf16[128,512]{1,0:T(8,128)(2,1)S(1)}, u32[]{:S(2)}, u32[]{:S(2)}) collective-permute-start(bf16[128,512]{1,0:T(8,128)(2,1)S(1)} %shard_map.61.refs_0_), channel_id=1, source_target_pairs={{1,0},{0,1},{3,2},{2,3},{5,4},{4,5},{7,6},{6,7},{9,8},{8,9},{11,10... | collective-permute-start | bytes 393224 | tf_op jit(solution)/shard_map/ppermute | solution.py:32
  16.9 8.2 %collective-permute-start.7 = (bf16[128,512]{1,0:T(8,128)(2,1)S(1)}, bf16[128,512]{1,0:T(8,128)(2,1)S(1)}, u32[]{:S(2)}, u32[]{:S(2)}) collective-permute-start(bf16[128,512]{1,0:T(8,128)(2,1)S(1)} %shard_map.62.refs_2_), channel_id=1, source_target_pairs={{0,4},{1,5},{2,6},{3,7},{4,8},{5,9},{6,10},{7,11},{8,12},{9,13},{1... | collective-permute-start | bytes 393224 | tf_op jit(solution)/shard_map/ppermute | solution.py:28
  17.7 9.3 %collective-permute-start.5 = (bf16[128,512]{1,0:T(8,128)(2,1)S(1)}, bf16[128,512]{1,0:T(8,128)(2,1)S(1)}, u32[]{:S(2)}, u32[]{:S(2)}) collective-permute-start(bf16[128,512]{1,0:T(8,128)(2,1)S(1)} %shard_map.61.refs_0_), channel_id=1, source_target_pairs={{0,4},{1,5},{2,6},{3,7},{4,8},{5,9},{6,10},{7,11},{8,12},{9,13},{1... | collective-permute-start | bytes 393224 | tf_op jit(solution)/shard_map/ppermute | solution.py:28
  25.1 1.9 %collective-permute-start.8 = (bf16[128,512]{1,0:T(8,128)(2,1)S(1)}, bf16[128,512]{1,0:T(8,128)(2,1)S(1)}, u32[]{:S(2)}, u32[]{:S(2)}) collective-permute-start(bf16[128,512]{1,0:T(8,128)(2,1)S(1)} %shard_map.65.refs_2_), channel_id=1, source_target_pairs={{1,0},{0,1},{3,2},{2,3},{5,4},{4,5},{7,6},{6,7},{9,8},{8,9},{11,10... | collective-permute-start | bytes 393224 | tf_op jit(solution)/shard_map/ppermute | solution.py:32
  27.0 1.3 %collective-permute-start.6 = (bf16[128,512]{1,0:T(8,128)(2,1)S(1)}, bf16[128,512]{1,0:T(8,128)(2,1)S(1)}, u32[]{:S(2)}, u32[]{:S(2)}) collective-permute-start(bf16[128,512]{1,0:T(8,128)(2,1)S(1)} %shard_map.64.refs_0_), channel_id=1, source_target_pairs={{1,0},{0,1},{3,2},{2,3},{5,4},{4,5},{7,6},{6,7},{9,8},{8,9},{11,10... | collective-permute-start | bytes 393224 | tf_op jit(solution)/shard_map/ppermute | solution.py:32

commit v3 on v2

--- a/solution.py
+++ b/solution.py
@@ -18,7 +18,6 @@
 TILE = 64
 VMEM = pl.BlockSpec(memory_space=pltpu.VMEM)
 SMALL = pltpu.CompilerParams(vmem_limit_bytes=1 << 20)
-SMEM = pl.BlockSpec(memory_space=pltpu.SMEM)
 HBM = pl.BlockSpec(memory_space=pltpu.HBM)
 MARK = (8, HD)
 
@@ -129,11 +128,11 @@
     return jnp.max(mark_ref[...]).astype(jnp.int32)
 
 
-def near_kernel(axis, win_ref, q_ref, own, other, state_out, mark, s_buf, p_buf):
+def near_kernel(axis, mark_in, q_ref, own, other, state_out, mark, s_buf, p_buf):
     me = lax.axis_index(axis)
     rows = own.shape[0]
-    lowest = jnp.maximum(me * rows - win_ref[me], 0)
-    mark[...] = jnp.full(mark.shape, lowest.astype(jnp.float32))
+    lowest = lowest_of(mark_in)
+    mark[...] = mark_in[...]
     lane, row = lane_row(rows)
     first_seen = jnp.where((me & 1) == 1, lowest - (me - 1) * rows, rows)
     other_flags = jnp.where((lane == 0) & (row < first_seen), 1.0, 0.0)
@@ -206,7 +205,7 @@
         ]
     return pl.pallas_call(
         kernel,
-        in_specs=[VMEM if state is not None else SMEM] + [VMEM] * (len(operands) - 1),
+        in_specs=[VMEM] * len(operands),
         out_specs=[VMEM] * len(out_shape),
         out_shape=out_shape,
         scratch_shapes=[
@@ -223,28 +222,43 @@
     )(*operands)
 
 
-def pack_kernel(k_hbm, v_hbm, own_hbm, sems):
-    width = k_hbm.shape[1]
+def fetch_kernel(axis, k_hbm, v_hbm, win_hbm, q_hbm, own_ref, mark_ref, q_ref, win_ref, sems):
+    rows, width = k_hbm.shape
     copies = [
-        pltpu.make_async_copy(k_hbm, own_hbm.at[:, pl.ds(0, width)], sems.at[0]),
-        pltpu.make_async_copy(v_hbm, own_hbm.at[:, pl.ds(width, width)], sems.at[1]),
+        pltpu.make_async_copy(k_hbm, own_ref.at[:, pl.ds(0, width)], sems.at[0]),
+        pltpu.make_async_copy(v_hbm, own_ref.at[:, pl.ds(width, width)], sems.at[1]),
+        pltpu.make_async_copy(win_hbm, win_ref, sems.at[2]),
+        pltpu.make_async_copy(q_hbm, q_ref, sems.at[3]),
     ]
     for copy in copies:
         copy.start()
     for copy in copies:
         copy.wait()
-
-
-def packed(keys, values):
+    me = lax.axis_index(axis)
+    lowest = jnp.maximum(me * rows - win_ref[me], 0)
+    mark_ref[...] = jnp.full(mark_ref.shape, lowest.astype(jnp.float32))
+
+
+def fetched(axis, queries, keys, values, windows):
     rows, width = keys.shape
+    sources = [
+        pltpu.with_memory_space_constraint(x, pltpu.HBM) for x in (keys, values, windows, queries)
+    ]
     return pl.pallas_call(
-        pack_kernel,
-        in_specs=[HBM] * 2,
-        out_specs=HBM,
-        out_shape=jax.ShapeDtypeStruct((rows, 2 * width), keys.dtype),
-        scratch_shapes=[pltpu.SemaphoreType.DMA((2,))],
-        compiler_params=pltpu.CompilerParams(vmem_limit_bytes=60 << 20),
-    )(keys, values)
+        functools.partial(fetch_kernel, axis),
+        in_specs=[HBM] * 4,
+        out_specs=[VMEM] * 3,
+        out_shape=[
+            jax.ShapeDtypeStruct((rows, 2 * width), keys.dtype),
+            jax.ShapeDtypeStruct(MARK, jnp.float32),
+            jax.ShapeDtypeStruct(queries.shape, queries.dtype),
+        ],
+        scratch_shapes=[
+            pltpu.SMEM(windows.shape, windows.dtype),
+            pltpu.SemaphoreType.DMA((4,)),
+        ],
+        compiler_params=SMALL,
+    )(*sources)
 
 
 def tied(block, earlier):
@@ -264,11 +278,11 @@
 def on_device(queries, keys, values, windows):
     axis = "section"
     reach = lax.axis_size(axis) // 2
-    own = packed(keys, values)
+    own, mark, queries = fetched(axis, queries, keys, values, windows)
     other = swapped(own, axis)
     held = {4: shifted(own, axis, 4), 2: shifted(own, axis, 2)}
     state, mark = attend(
-        functools.partial(near_kernel, axis), windows, queries, [own, other], None, False
+        functools.partial(near_kernel, axis), mark, queries, [own, other], None, False
     )
     for first in range(2, reach + 1, 4):
         distances = [d for d in (first + 2, first) if d <= reach]

time: 30.4 us -> 26.4 us (0.87)
  the two profiles are of different devices: /device:TPU:0 before, /device:TPU:15 now
where the time goes in v3:
time: 26.4 us; the launch traced here: 26.3 us
  Pallas kernels  11.2 us (42%)
  starting transfers between devices  8.79 us (33%)
  waiting for transfers between devices  5.62 us (21%)
  between operations  0.68 us (3%)
    pallas_call x3, Pallas kernels, attend(): pl.pallas_call(kernel, in_specs=[VMEM] * len(operands), out_specs=[VMEM]...  9.85 us
    ppermute x4, starting transfers between devices, shifted(): lax.ppermute(block, axis, [(i, (i + distance) % size) for i in range(size)])  5.13 us
    ppermute x4, waiting for transfers between devices, shifted(): lax.ppermute(block, axis, [(i, (i + distance) % size) for i in range(size)])  4.63 us
    ppermute x5, starting transfers between devices, swapped(): lax.ppermute(block, axis, [(i ^ 1, i) for i in range(lax.axis_size(axis))])  3.66 us
    pallas_call x1, Pallas kernels, fetched(): pl.pallas_call(functools.partial(fetch_kernel, axis), in_specs=[HBM] * 4,...  1.34 us
    ppermute x5, waiting for transfers between devices, swapped(): lax.ppermute(block, axis, [(i ^ 1, i) for i in range(lax.axis_size(axis))])  0.99 us
  transfers between devices with their start and end apart: 9, of which 4 were waited for; matrix products, arithmetic and copies ran while one was open for 0% of the time, Pallas kernels for 20%

profile of v3, /device:TPU:15, one launch (start us, length us, event | category | flops | bytes accessed | tf_op | source)
XLA Modules:
  0.0 26.3 jit_solution(2399373366077253823)
XLA Ops:
  0.6 1.3 %shard_map.59 = (bf16[128,512]{1,0:T(8,128)(2,1)S(1)}, f32[8,128]{1,0:T(8,128)S(1)}, bf16[128,4096]{1,0:T(8,128)(2,1)S(1)}) custom-call(bf16[128,256]{1,0:T(8,128)(2,1)} %k_hbm.1, bf16[128,256]{1,0:T(8,128)(2,1)} %v_hbm.1, s32[16]{0:T(128)} %win_hbm.1, bf16[128,4096]{1,0:T(8,128)(2,1)} %q_hbm.1), custom_call_target="tpu_custom_call" | custom-call | tf_op jit(solution)/shard_map/pallas_call | solution.py:247
  2.0 0.7 %collective-permute-start = (bf16[128,512]{1,0:T(8,128)(2,1)S(1)}, bf16[128,512]{1,0:T(8,128)(2,1)S(1)}, u32[]{:S(2)}, u32[]{:S(2)}) collective-permute-start(bf16[128,512]{1,0:T(8,128)(2,1)S(1)} %get-tuple-element.13.own), channel_id=1, source_target_pairs={{1,0},{0,1},{3,2},{2,3},{5,4},{4,5},{7,6},{6,7},{9,8},{8,9},{11,10... | collective-permute-start | bytes 393224 | tf_op jit(solution)/shard_map/ppermute | solution.py:31
  2.7 1.2 %collective-permute-start.3 = (bf16[128,512]{1,0:T(8,128)(2,1)S(1)}, bf16[128,512]{1,0:T(8,128)(2,1)S(1)}, u32[]{:S(2)}, u32[]{:S(2)}) collective-permute-start(bf16[128,512]{1,0:T(8,128)(2,1)S(1)} %get-tuple-element.13.own), channel_id=1, source_target_pairs={{0,2},{1,3},{2,4},{3,5},{4,6},{5,7},{6,8},{7,9},{8,10},{9,11},{10,... | collective-permute-start | bytes 393224 | tf_op jit(solution)/shard_map/ppermute | solution.py:27
  4.0 1.3 %collective-permute-start.1 = (bf16[128,512]{1,0:T(8,128)(2,1)S(1)}, bf16[128,512]{1,0:T(8,128)(2,1)S(1)}, u32[]{:S(2)}, u32[]{:S(2)}) collective-permute-start(bf16[128,512]{1,0:T(8,128)(2,1)S(1)} %get-tuple-element.13.own), channel_id=1, source_target_pairs={{0,4},{1,5},{2,6},{3,7},{4,8},{5,9},{6,10},{7,11},{8,12},{9,13},{1... | collective-permute-start | bytes 393224 | tf_op jit(solution)/shard_map/ppermute | solution.py:27
  5.3 0.0 collective-permute-done.other
  5.3 1.8 %shard_map.60 = (f32[144,4096]{1,0:T(8,128)S(1)}, f32[8,128]{1,0:T(8,128)S(1)}) custom-call(f32[8,128]{1,0:T(8,128)S(1)} %get-tuple-element.11.mark_in, bf16[128,4096]{1,0:T(8,128)(2,1)S(1)} %get-tuple-element.12.q_ref, bf16[128,512]{1,0:T(8,128)(2,1)S(1)} %get-tuple-element.13.own, bf16[128,512]{1,0:T(8,128)(2,1)S(1)} %collective-permute-done.other), custom_call_target="tpu_custom_call" | custom-call | flops 536870912 | bytes 1048576 | tf_op jit(solution)/shard_map/pallas_call | solution.py:206
  7.1 0.7 %collective-permute-done.3.block_ref = bf16[128,512]{1,0:T(8,128)(2,1)S(1)} collective-permute-done((bf16[128,512]{1,0:T(8,128)(2,1)S(1)}, bf16[128,512]{1,0:T(8,128)(2,1)S(1)}, u32[]{:S(2)}, u32[]{:S(2)}) %collective-permute-start.3) | collective-permute-done | bytes 131104 | tf_op jit(solution)/shard_map/ppermute | solution.py:27
  7.8 0.8 %collective-permute-start.4 = (bf16[128,512]{1,0:T(8,128)(2,1)S(1)}, bf16[128,512]{1,0:T(8,128)(2,1)S(1)}, u32[]{:S(2)}, u32[]{:S(2)}) collective-permute-start(bf16[128,512]{1,0:T(8,128)(2,1)S(1)} %shard_map.62.refs_2_), channel_id=1, source_target_pairs={{1,0},{0,1},{3,2},{2,3},{5,4},{4,5},{7,6},{6,7},{9,8},{8,9},{11,10... | collective-permute-start | bytes 393224 | tf_op jit(solution)/shard_map/ppermute | solution.py:31
  8.6 1.9 %collective-permute-done.1.block_ref = bf16[128,512]{1,0:T(8,128)(2,1)S(1)} collective-permute-done((bf16[128,512]{1,0:T(8,128)(2,1)S(1)}, bf16[128,512]{1,0:T(8,128)(2,1)S(1)}, u32[]{:S(2)}, u32[]{:S(2)}) %collective-permute-start.1) | collective-permute-done | bytes 131104 | tf_op jit(solution)/shard_map/ppermute | solution.py:27
  10.5 0.8 %collective-permute-start.2 = (bf16[128,512]{1,0:T(8,128)(2,1)S(1)}, bf16[128,512]{1,0:T(8,128)(2,1)S(1)}, u32[]{:S(2)}, u32[]{:S(2)}) collective-permute-start(bf16[128,512]{1,0:T(8,128)(2,1)S(1)} %shard_map.61.refs_0_), channel_id=1, source_target_pairs={{1,0},{0,1},{3,2},{2,3},{5,4},{4,5},{7,6},{6,7},{9,8},{8,9},{11,10... | collective-permute-start | bytes 393224 | tf_op jit(solution)/shard_map/ppermute | solution.py:31
  11.4 1.3 %collective-permute-start.7 = (bf16[128,512]{1,0:T(8,128)(2,1)S(1)}, bf16[128,512]{1,0:T(8,128)(2,1)S(1)}, u32[]{:S(2)}, u32[]{:S(2)}) collective-permute-start(bf16[128,512]{1,0:T(8,128)(2,1)S(1)} %shard_map.62.refs_2_), channel_id=1, source_target_pairs={{0,4},{1,5},{2,6},{3,7},{4,8},{5,9},{6,10},{7,11},{8,12},{9,13},{1... | collective-permute-start | bytes 393224 | tf_op jit(solution)/shard_map/ppermute | solution.py:27
  12.7 1.3 %collective-permute-start.5 = (bf16[128,512]{1,0:T(8,128)(2,1)S(1)}, bf16[128,512]{1,0:T(8,128)(2,1)S(1)}, u32[]{:S(2)}, u32[]{:S(2)}) collective-permute-start(bf16[128,512]{1,0:T(8,128)(2,1)S(1)} %shard_map.61.refs_0_), channel_id=1, source_target_pairs={{0,4},{1,5},{2,6},{3,7},{4,8},{5,9},{6,10},{7,11},{8,12},{9,13},{1... | collective-permute-start | bytes 393224 | tf_op jit(solution)/shard_map/ppermute | solution.py:27
  14.0 0.0 collective-permute-done.4.refs_3_
  14.0 0.0 collective-permute-done.2.refs_1_
  14.0 3.4 %shard_map.63 = (f32[144,4096]{1,0:T(8,128)S(1)}, f32[8,128]{1,0:T(8,128)S(1)}) custom-call(f32[8,128]{1,0:T(8,128)S(1)} %get-tuple-element.14.earlier_ref.mark_in, bf16[128,4096]{1,0:T(8,128)(2,1)S(1)} %get-tuple-element.12.q_ref, bf16[128,512]{1,0:T(8,128)(2,1)S(1)} %shard_map.61.refs_0_, ...), custom_call_target="tpu_custom_call", output_to_operand_aliasing={{0}: (6, {})} | custom-call | flops 1073741824 | bytes 1048576 | tf_op jit(solution)/shard_map/pallas_call | solution.py:206
  17.4 0.0 collective-permute-done.7.block_ref
  17.5 0.6 %collective-permute-start.8 = (bf16[128,512]{1,0:T(8,128)(2,1)S(1)}, bf16[128,512]{1,0:T(8,128)(2,1)S(1)}, u32[]{:S(2)}, u32[]{:S(2)}) collective-permute-start(bf16[128,512]{1,0:T(8,128)(2,1)S(1)} %shard_map.65.refs_2_), channel_id=1, source_target_pairs={{1,0},{0,1},{3,2},{2,3},{5,4},{4,5},{7,6},{6,7},{9,8},{8,9},{11,10... | collective-permute-start | bytes 393224 | tf_op jit(solution)/shard_map/ppermute | solution.py:31
  18.1 2.0 %collective-permute-done.5.block_ref = bf16[128,512]{1,0:T(8,128)(2,1)S(1)} collective-permute-done((bf16[128,512]{1,0:T(8,128)(2,1)S(1)}, bf16[128,512]{1,0:T(8,128)(2,1)S(1)}, u32[]{:S(2)}, u32[]{:S(2)}) %collective-permute-start.5) | collective-permute-done | bytes 131104 | tf_op jit(solution)/shard_map/ppermute | solution.py:27
  20.1 0.6 %collective-permute-start.6 = (bf16[128,512]{1,0:T(8,128)(2,1)S(1)}, bf16[128,512]{1,0:T(8,128)(2,1)S(1)}, u32[]{:S(2)}, u32[]{:S(2)}) collective-permute-start(bf16[128,512]{1,0:T(8,128)(2,1)S(1)} %shard_map.64.refs_0_), channel_id=1, source_target_pairs={{1,0},{0,1},{3,2},{2,3},{5,4},{4,5},{7,6},{6,7},{9,8},{8,9},{11,10... | collective-permute-start | bytes 393224 | tf_op jit(solution)/shard_map/ppermute | solution.py:31
  20.7 0.0 collective-permute-done.8.refs_3_
  20.7 1.0 %collective-permute-done.6.refs_1_ = bf16[128,512]{1,0:T(8,128)(2,1)S(1)} collective-permute-done((bf16[128,512]{1,0:T(8,128)(2,1)S(1)}, bf16[128,512]{1,0:T(8,128)(2,1)S(1)}, u32[]{:S(2)}, u32[]{:S(2)}) %collective-permute-start.6) | collective-permute-done | bytes 131104 | tf_op jit(solution)/shard_map/ppermute | solution.py:31
  21.7 4.6 %shard_map.66 = (bf16[128,4096]{1,0:T(8,128)(2,1)}, f32[32,128]{1,0:T(8,128)}) custom-call(f32[8,128]{1,0:T(8,128)S(1)} %get-tuple-element.16.earlier_ref.mark_in, bf16[128,4096]{1,0:T(8,128)(2,1)S(1)} %get-tuple-element.12.q_ref, bf16[128,512]{1,0:T(8,128)(2,1)S(1)} %shard_map.64.refs_0_, bf16[128,512]{1,0:T(8,128)(2,1)S(1)} %collective-permute-done.6.refs_1_, ...), custom_call_target="tpu_custom_call" | custom-call | flops 1073741824 | bytes 1048576 | tf_op jit(solution)/shard_map/pallas_call | solution.py:206
  (4 shorter events, 0.0 us)
Async XLA Ops:
  2.0 3.3 %collective-permute-start = (bf16[128,512]{1,0:T(8,128)(2,1)S(1)}, bf16[128,512]{1,0:T(8,128)(2,1)S(1)}, u32[]{:S(2)}, u32[]{:S(2)}) collective-permute-start(bf16[128,512]{1,0:T(8,128)(2,1)S(1)} %get-tuple-element.13.own), channel_id=1, source_target_pairs={{1,0},{0,1},{3,2},{2,3},{5,4},{4,5},{7,6},{6,7},{9,8},{8,9},{11,10... | collective-permute-start | bytes 393224 | tf_op jit(solution)/shard_map/ppermute | solution.py:31
  2.7 5.1 %collective-permute-start.3 = (bf16[128,512]{1,0:T(8,128)(2,1)S(1)}, bf16[128,512]{1,0:T(8,128)(2,1)S(1)}, u32[]{:S(2)}, u32[]{:S(2)}) collective-permute-start(bf16[128,512]{1,0:T(8,128)(2,1)S(1)} %get-tuple-element.13.own), channel_id=1, source_target_pairs={{0,2},{1,3},{2,4},{3,5},{4,6},{5,7},{6,8},{7,9},{8,10},{9,11},{10,... | collective-permute-start | bytes 393224 | tf_op jit(solution)/shard_map/ppermute | solution.py:27
  4.0 6.6 %collective-permute-start.1 = (bf16[128,512]{1,0:T(8,128)(2,1)S(1)}, bf16[128,512]{1,0:T(8,128)(2,1)S(1)}, u32[]{:S(2)}, u32[]{:S(2)}) collective-permute-start(bf16[128,512]{1,0:T(8,128)(2,1)S(1)} %get-tuple-element.13.own), channel_id=1, source_target_pairs={{0,4},{1,5},{2,6},{3,7},{4,8},{5,9},{6,10},{7,11},{8,12},{9,13},{1... | collective-permute-start | bytes 393224 | tf_op jit(solution)/shard_map/ppermute | solution.py:27
  7.8 6.2 %collective-permute-start.4 = (bf16[128,512]{1,0:T(8,128)(2,1)S(1)}, bf16[128,512]{1,0:T(8,128)(2,1)S(1)}, u32[]{:S(2)}, u32[]{:S(2)}) collective-permute-start(bf16[128,512]{1,0:T(8,128)(2,1)S(1)} %shard_map.62.refs_2_), channel_id=1, source_target_pairs={{1,0},{0,1},{3,2},{2,3},{5,4},{4,5},{7,6},{6,7},{9,8},{8,9},{11,10... | collective-permute-start | bytes 393224 | tf_op jit(solution)/shard_map/ppermute | solution.py:31
  10.5 3.5 %collective-permute-start.2 = (bf16[128,512]{1,0:T(8,128)(2,1)S(1)}, bf16[128,512]{1,0:T(8,128)(2,1)S(1)}, u32[]{:S(2)}, u32[]{:S(2)}) collective-permute-start(bf16[128,512]{1,0:T(8,128)(2,1)S(1)} %shard_map.61.refs_0_), channel_id=1, source_target_pairs={{1,0},{0,1},{3,2},{2,3},{5,4},{4,5},{7,6},{6,7},{9,8},{8,9},{11,10... | collective-permute-start | bytes 393224 | tf_op jit(solution)/shard_map/ppermute | solution.py:31
  11.4 6.1 %collective-permute-start.7 = (bf16[128,512]{1,0:T(8,128)(2,1)S(1)}, bf16[128,512]{1,0:T(8,128)(2,1)S(1)}, u32[]{:S(2)}, u32[]{:S(2)}) collective-permute-start(bf16[128,512]{1,0:T(8,128)(2,1)S(1)} %shard_map.62.refs_2_), channel_id=1, source_target_pairs={{0,4},{1,5},{2,6},{3,7},{4,8},{5,9},{6,10},{7,11},{8,12},{9,13},{1... | collective-permute-start | bytes 393224 | tf_op jit(solution)/shard_map/ppermute | solution.py:27
  12.7 7.5 %collective-permute-start.5 = (bf16[128,512]{1,0:T(8,128)(2,1)S(1)}, bf16[128,512]{1,0:T(8,128)(2,1)S(1)}, u32[]{:S(2)}, u32[]{:S(2)}) collective-permute-start(bf16[128,512]{1,0:T(8,128)(2,1)S(1)} %shard_map.61.refs_0_), channel_id=1, source_target_pairs={{0,4},{1,5},{2,6},{3,7},{4,8},{5,9},{6,10},{7,11},{8,12},{9,13},{1... | collective-permute-start | bytes 393224 | tf_op jit(solution)/shard_map/ppermute | solution.py:27
  17.5 3.3 %collective-permute-start.8 = (bf16[128,512]{1,0:T(8,128)(2,1)S(1)}, bf16[128,512]{1,0:T(8,128)(2,1)S(1)}, u32[]{:S(2)}, u32[]{:S(2)}) collective-permute-start(bf16[128,512]{1,0:T(8,128)(2,1)S(1)} %shard_map.65.refs_2_), channel_id=1, source_target_pairs={{1,0},{0,1},{3,2},{2,3},{5,4},{4,5},{7,6},{6,7},{9,8},{8,9},{11,10... | collective-permute-start | bytes 393224 | tf_op jit(solution)/shard_map/ppermute | solution.py:31
  20.1 1.6 %collective-permute-start.6 = (bf16[128,512]{1,0:T(8,128)(2,1)S(1)}, bf16[128,512]{1,0:T(8,128)(2,1)S(1)}, u32[]{:S(2)}, u32[]{:S(2)}) collective-permute-start(bf16[128,512]{1,0:T(8,128)(2,1)S(1)} %shard_map.64.refs_0_), channel_id=1, source_target_pairs={{1,0},{0,1},{3,2},{2,3},{5,4},{4,5},{7,6},{6,7},{9,8},{8,9},{11,10... | collective-permute-start | bytes 393224 | tf_op jit(solution)/shard_map/ppermute | solution.py:31

commit v4 on v3

--- a/solution.py
+++ b/solution.py
@@ -22,9 +22,15 @@
 MARK = (8, HD)
 
 
-def shifted(block, axis, distance):
+def reach_of(core, turn):
+    return 4 - 2 * (core ^ turn)
+
+
+def shifted(block, axis, turn):
     size = lax.axis_size(axis)
-    return lax.ppermute(block, axis, [(i, (i + distance) % size) for i in range(size)])
+    return lax.ppermute(
+        block, axis, [(i, (i + reach_of(i % 2, turn)) % size) for i in range(size)]
+    )
 
 
 def swapped(block, axis):
@@ -144,9 +150,9 @@
     )
 
 
-def far_kernel(axis, distances, last, mark_in, q_ref, *refs):
+def far_kernel(axis, level, last, mark_in, q_ref, *refs):
     me = lax.axis_index(axis)
-    count = 2 * len(distances)
+    count = 4
     blocks, state_in = refs[:count], refs[count]
     if last:
         state_out, (out_ref, log_ref, s_buf, p_buf) = None, refs[count + 1 :]
@@ -155,7 +161,9 @@
         mark[...] = mark_in[...]
     rows = blocks[0].shape[0]
     lowest = lowest_of(mark_in)
-    starts = [(who - d) * rows for d in distances for who in (me, me ^ 1)]
+    starts = [
+        (who - level - reach_of(who & 1, turn)) * rows for turn in (0, 1) for who in (me, me ^ 1)
+    ]
     needed = functools.reduce(jnp.logical_or, [s + rows > lowest for s in starts])
 
     @pl.when(needed)
@@ -261,8 +269,8 @@
     )(*sources)
 
 
-def tied(block, earlier):
-    def kernel(block_ref, earlier_ref, out_ref):
+def tied(block, mark):
+    def kernel(block_ref, mark_ref, out_ref):
         pass
 
     return pl.pallas_call(
@@ -272,7 +280,29 @@
         out_shape=jax.ShapeDtypeStruct(block.shape, block.dtype),
         input_output_aliases={0: 0},
         compiler_params=SMALL,
-    )(block, earlier)
+    )(block, mark)
+
+
+def choose_kernel(axis, first_ref, second_ref, mark_ref, out_ref):
+    odd = (lax.axis_index(axis) & 1) == 1
+
+    @pl.when(odd)
+    def _():
+        out_ref[...] = second_ref[...]
+
+    @pl.when(jnp.logical_not(odd))
+    def _():
+        out_ref[...] = first_ref[...]
+
+
+def chosen(axis, first, second, mark):
+    return pl.pallas_call(
+        functools.partial(choose_kernel, axis),
+        in_specs=[VMEM] * 3,
+        out_specs=VMEM,
+        out_shape=jax.ShapeDtypeStruct(first.shape, first.dtype),
+        compiler_params=SMALL,
+    )(first, second, mark)
 
 
 def on_device(queries, keys, values, windows):
@@ -280,21 +310,20 @@
     reach = lax.axis_size(axis) // 2
     own, mark, queries = fetched(axis, queries, keys, values, windows)
     other = swapped(own, axis)
-    held = {4: shifted(own, axis, 4), 2: shifted(own, axis, 2)}
+    arrived = [shifted(own, axis, turn) for turn in (0, 1)]
     state, mark = attend(
         functools.partial(near_kernel, axis), mark, queries, [own, other], None, False
     )
-    for first in range(2, reach + 1, 4):
-        distances = [d for d in (first + 2, first) if d <= reach]
-        last = first + 4 > reach
-        blocks = []
-        for d in distances:
-            held[d] = tied(held[d], mark)
-            if d + 4 <= reach:
-                held[d + 4] = shifted(held[d], axis, 4)
-            blocks += [held[d], swapped(held[d], axis)]
+    for level in range(0, reach, 4):
+        last = level + 4 >= reach
+        if level:
+            arrived = [tied(block, mark) for block in arrived]
+        blocks = [x for block in arrived for x in (block, swapped(block, axis))]
+        if not last:
+            farthest = chosen(axis, *arrived, mark)
+            arrived = [shifted(farthest, axis, turn) for turn in (0, 1)]
         result = attend(
-            functools.partial(far_kernel, axis, distances, last),
+            functools.partial(far_kernel, axis, level, last),
             mark,
             queries,
             blocks,

time: 26.4 us -> 28.9 us (1.095)
  the two profiles are of different devices: /device:TPU:15 before, /device:TPU:0 now
where the time goes in v4:
time: 28.9 us; the launch traced here: 28.7 us
  waiting for transfers between devices  13.8 us (48%)
  starting transfers between devices  9.15 us (32%)
  Pallas kernels  5.11 us (18%)
  between operations  0.68 us (2%)
    ppermute x4, waiting for transfers between devices, shifted(): lax.ppermute(block, axis, [(i, (i + reach_of(i % 2, turn)) % size) for i...  12.8 us
    ppermute x4, starting transfers between devices, shifted(): lax.ppermute(block, axis, [(i, (i + reach_of(i % 2, turn)) % size) for i...  6.24 us
    pallas_call x3, Pallas kernels, attend(): pl.pallas_call(kernel, in_specs=[VMEM] * len(operands), out_specs=[VMEM]...  3.74 us
    ppermute x5, starting transfers between devices, swapped(): lax.ppermute(block, axis, [(i ^ 1, i) for i in range(lax.axis_size(axis))])  2.91 us
    pallas_call x1, Pallas kernels, fetched(): pl.pallas_call(functools.partial(fetch_kernel, axis), in_specs=[HBM] * 4,...  1.34 us
    ppermute x5, waiting for transfers between devices, swapped(): lax.ppermute(block, axis, [(i ^ 1, i) for i in range(lax.axis_size(axis))])  0.99 us
  transfers between devices with their start and end apart: 9, of which 3 were waited for; matrix products, arithmetic and copies ran while one was open for 0% of the time, Pallas kernels for 8%

profile of v4, /device:TPU:0, one launch (start us, length us, event | category | flops | bytes accessed | tf_op | source)
XLA Modules:
  0.0 28.7 jit_solution(14293484735480552872)
XLA Ops:
  0.6 1.3 %shard_map.59 = (bf16[128,512]{1,0:T(8,128)(2,1)S(1)}, f32[8,128]{1,0:T(8,128)S(1)}, bf16[128,4096]{1,0:T(8,128)(2,1)S(1)}) custom-call(bf16[128,256]{1,0:T(8,128)(2,1)} %k_hbm.1, bf16[128,256]{1,0:T(8,128)(2,1)} %v_hbm.1, s32[16]{0:T(128)} %win_hbm.1, bf16[128,4096]{1,0:T(8,128)(2,1)} %q_hbm.1), custom_call_target="tpu_custom_call" | custom-call | tf_op jit(solution)/shard_map/pallas_call | solution.py:255
  2.0 3.0 %collective-permute-start.3 = (bf16[128,512]{1,0:T(8,128)(2,1)S(1)}, bf16[128,512]{1,0:T(8,128)(2,1)S(1)}, u32[]{:S(2)}, u32[]{:S(2)}) collective-permute-start(bf16[128,512]{1,0:T(8,128)(2,1)S(1)} %get-tuple-element.13.own), channel_id=1, source_target_pairs={{0,2},{1,5},{2,4},{3,7},{4,6},{5,9},{6,8},{7,11},{8,10},{9,13},{10... | collective-permute-start | bytes 393224 | tf_op jit(solution)/shard_map/ppermute | solution.py:31
  5.0 1.6 %collective-permute-start.1 = (bf16[128,512]{1,0:T(8,128)(2,1)S(1)}, bf16[128,512]{1,0:T(8,128)(2,1)S(1)}, u32[]{:S(2)}, u32[]{:S(2)}) collective-permute-start(bf16[128,512]{1,0:T(8,128)(2,1)S(1)} %get-tuple-element.13.own), channel_id=1, source_target_pairs={{0,4},{1,3},{2,6},{3,5},{4,8},{5,7},{6,10},{7,9},{8,12},{9,11},{10... | collective-permute-start | bytes 393224 | tf_op jit(solution)/shard_map/ppermute | solution.py:31
  6.6 0.0 collective-permute-start
  6.6 5.8 %collective-permute-done.3.refs_2_.second_ref = bf16[128,512]{1,0:T(8,128)(2,1)S(1)} collective-permute-done((bf16[128,512]{1,0:T(8,128)(2,1)S(1)}, bf16[128,512]{1,0:T(8,128)(2,1)S(1)}, u32[]{:S(2)}, u32[]{:S(2)}) %collective-permute-start.3) | collective-permute-done | bytes 131104 | tf_op jit(solution)/shard_map/ppermute | solution.py:31
  12.4 0.0 collective-permute-start.4
  12.4 0.0 collective-permute-done.1.refs_0_.first_ref
  12.4 1.0 %collective-permute-start.2 = (bf16[128,512]{1,0:T(8,128)(2,1)S(1)}, bf16[128,512]{1,0:T(8,128)(2,1)S(1)}, u32[]{:S(2)}, u32[]{:S(2)}) collective-permute-start(bf16[128,512]{1,0:T(8,128)(2,1)S(1)} %collective-permute-done.1.refs_0_.first_ref), channel_id=1, source_target_pairs={{1,0},{0,1},{3,2},{2,3},{5,4},{4,5},{7,6},{6,7},{9,8},{8,9},{11,10... | collective-permute-start | bytes 393224 | tf_op jit(solution)/shard_map/ppermute | solution.py:37
  13.3 0.0 collective-permute-done.other
  13.3 1.8 %shard_map.60 = (f32[144,4096]{1,0:T(8,128)S(1)}, f32[8,128]{1,0:T(8,128)S(1)}) custom-call(f32[8,128]{1,0:T(8,128)S(1)} %get-tuple-element.11.mark_in, bf16[128,4096]{1,0:T(8,128)(2,1)S(1)} %get-tuple-element.12.q_ref, bf16[128,512]{1,0:T(8,128)(2,1)S(1)} %get-tuple-element.13.own, bf16[128,512]{1,0:T(8,128)(2,1)S(1)} %collective-permute-done.other), custom_call_target="tpu_custom_call" | custom-call | flops 536870912 | bytes 1048576 | tf_op jit(solution)/shard_map/pallas_call | solution.py:214
  15.2 1.6 %collective-permute-start.7 = (bf16[128,512]{1,0:T(8,128)(2,1)S(1)}, bf16[128,512]{1,0:T(8,128)(2,1)S(1)}, u32[]{:S(2)}, u32[]{:S(2)}) collective-permute-start(bf16[128,512]{1,0:T(8,128)(2,1)S(1)} %shard_map.62), channel_id=1, source_target_pairs={{0,2},{1,5},{2,4},{3,7},{4,6},{5,9},{6,8},{7,11},{8,10},{9,13},{10... | collective-permute-start | bytes 393224 | tf_op jit(solution)/shard_map/ppermute | solution.py:31
  16.8 0.0 collective-permute-start.5
  16.8 0.0 collective-permute-done.4.refs_3_
  16.9 0.0 collective-permute-done.2.refs_1_
  16.9 0.4 %shard_map.61 = (f32[144,4096]{1,0:T(8,128)S(1)}, f32[8,128]{1,0:T(8,128)S(1)}) custom-call(f32[8,128]{1,0:T(8,128)S(1)} %get-tuple-element.14.mark_in.mark_ref, bf16[128,4096]{1,0:T(8,128)(2,1)S(1)} %get-tuple-element.12.q_ref, bf16[128,512]{1,0:T(8,128)(2,1)S(1)} %collective-permute-done.1.refs_0_.first_ref, ...), custom_call_target="tpu_custom_call", output_to_operand_aliasing={{0}: (6, {})} | custom-call | flops 1073741824 | bytes 1048576 | tf_op jit(solution)/shard_map/pallas_call | solution.py:214
  17.3 7.0 %collective-permute-done.7.block_ref = bf16[128,512]{1,0:T(8,128)(2,1)S(1)} collective-permute-done((bf16[128,512]{1,0:T(8,128)(2,1)S(1)}, bf16[128,512]{1,0:T(8,128)(2,1)S(1)}, u32[]{:S(2)}, u32[]{:S(2)}) %collective-permute-start.7) | collective-permute-done | bytes 131104 | tf_op jit(solution)/shard_map/ppermute | solution.py:31
  24.3 0.0 collective-permute-start.8
  24.3 0.0 collective-permute-done.5.block_ref
  24.3 1.9 %collective-permute-start.6 = (bf16[128,512]{1,0:T(8,128)(2,1)S(1)}, bf16[128,512]{1,0:T(8,128)(2,1)S(1)}, u32[]{:S(2)}, u32[]{:S(2)}) collective-permute-start(bf16[128,512]{1,0:T(8,128)(2,1)S(1)} %shard_map.63.refs_0_), channel_id=1, source_target_pairs={{1,0},{0,1},{3,2},{2,3},{5,4},{4,5},{7,6},{6,7},{9,8},{8,9},{11,10... | collective-permute-start | bytes 393224 | tf_op jit(solution)/shard_map/ppermute | solution.py:37
  26.3 0.0 collective-permute-done.8.refs_3_
  26.3 1.0 %collective-permute-done.6.refs_1_ = bf16[128,512]{1,0:T(8,128)(2,1)S(1)} collective-permute-done((bf16[128,512]{1,0:T(8,128)(2,1)S(1)}, bf16[128,512]{1,0:T(8,128)(2,1)S(1)}, u32[]{:S(2)}, u32[]{:S(2)}) %collective-permute-start.6) | collective-permute-done | bytes 131104 | tf_op jit(solution)/shard_map/ppermute | solution.py:37
  27.3 1.5 %shard_map.65 = (bf16[128,4096]{1,0:T(8,128)(2,1)}, f32[32,128]{1,0:T(8,128)}) custom-call(f32[8,128]{1,0:T(8,128)S(1)} %get-tuple-element.16.mark_ref.mark_in, bf16[128,4096]{1,0:T(8,128)(2,1)S(1)} %get-tuple-element.12.q_ref, bf16[128,512]{1,0:T(8,128)(2,1)S(1)} %shard_map.63.refs_0_, bf16[128,512]{1,0:T(8,128)(2,1)S(1)} %collective-permute-done.6.refs_1_, ...), custom_call_target="tpu_custom_call" | custom-call | flops 1073741824 | bytes 1048576 | tf_op jit(solution)/shard_map/pallas_call | solution.py:214
  (3 shorter events, 0.0 us)
Async XLA Ops:
  2.0 10.4 %collective-permute-start.3 = (bf16[128,512]{1,0:T(8,128)(2,1)S(1)}, bf16[128,512]{1,0:T(8,128)(2,1)S(1)}, u32[]{:S(2)}, u32[]{:S(2)}) collective-permute-start(bf16[128,512]{1,0:T(8,128)(2,1)S(1)} %get-tuple-element.13.own), channel_id=1, source_target_pairs={{0,2},{1,5},{2,4},{3,7},{4,6},{5,9},{6,8},{7,11},{8,10},{9,13},{10... | collective-permute-start | bytes 393224 | tf_op jit(solution)/shard_map/ppermute | solution.py:31
  5.0 7.4 %collective-permute-start.1 = (bf16[128,512]{1,0:T(8,128)(2,1)S(1)}, bf16[128,512]{1,0:T(8,128)(2,1)S(1)}, u32[]{:S(2)}, u32[]{:S(2)}) collective-permute-start(bf16[128,512]{1,0:T(8,128)(2,1)S(1)} %get-tuple-element.13.own), channel_id=1, source_target_pairs={{0,4},{1,3},{2,6},{3,5},{4,8},{5,7},{6,10},{7,9},{8,12},{9,11},{10... | collective-permute-start | bytes 393224 | tf_op jit(solution)/shard_map/ppermute | solution.py:31
  6.6 6.8 %collective-permute-start = (bf16[128,512]{1,0:T(8,128)(2,1)S(1)}, bf16[128,512]{1,0:T(8,128)(2,1)S(1)}, u32[]{:S(2)}, u32[]{:S(2)}) collective-permute-start(bf16[128,512]{1,0:T(8,128)(2,1)S(1)} %get-tuple-element.13.own), channel_id=1, source_target_pairs={{1,0},{0,1},{3,2},{2,3},{5,4},{4,5},{7,6},{6,7},{9,8},{8,9},{11,10... | collective-permute-start | bytes 393224 | tf_op jit(solution)/shard_map/ppermute | solution.py:37
  12.4 4.5 %collective-permute-start.4 = (bf16[128,512]{1,0:T(8,128)(2,1)S(1)}, bf16[128,512]{1,0:T(8,128)(2,1)S(1)}, u32[]{:S(2)}, u32[]{:S(2)}) collective-permute-start(bf16[128,512]{1,0:T(8,128)(2,1)S(1)} %collective-permute-done.3.refs_2_.second_ref), channel_id=1, source_target_pairs={{1,0},{0,1},{3,2},{2,3},{5,4},{4,5},{7,6},{6,7},{9,8},{8,9},{11,10... | collective-permute-start | bytes 393224 | tf_op jit(solution)/shard_map/ppermute | solution.py:37
  12.4 4.5 %collective-permute-start.2 = (bf16[128,512]{1,0:T(8,128)(2,1)S(1)}, bf16[128,512]{1,0:T(8,128)(2,1)S(1)}, u32[]{:S(2)}, u32[]{:S(2)}) collective-permute-start(bf16[128,512]{1,0:T(8,128)(2,1)S(1)} %collective-permute-done.1.refs_0_.first_ref), channel_id=1, source_target_pairs={{1,0},{0,1},{3,2},{2,3},{5,4},{4,5},{7,6},{6,7},{9,8},{8,9},{11,10... | collective-permute-start | bytes 393224 | tf_op jit(solution)/shard_map/ppermute | solution.py:37
  15.2 9.1 %collective-permute-start.7 = (bf16[128,512]{1,0:T(8,128)(2,1)S(1)}, bf16[128,512]{1,0:T(8,128)(2,1)S(1)}, u32[]{:S(2)}, u32[]{:S(2)}) collective-permute-start(bf16[128,512]{1,0:T(8,128)(2,1)S(1)} %shard_map.62), channel_id=1, source_target_pairs={{0,2},{1,5},{2,4},{3,7},{4,6},{5,9},{6,8},{7,11},{8,10},{9,13},{10... | collective-permute-start | bytes 393224 | tf_op jit(solution)/shard_map/ppermute | solution.py:31
  16.8 7.5 %collective-permute-start.5 = (bf16[128,512]{1,0:T(8,128)(2,1)S(1)}, bf16[128,512]{1,0:T(8,128)(2,1)S(1)}, u32[]{:S(2)}, u32[]{:S(2)}) collective-permute-start(bf16[128,512]{1,0:T(8,128)(2,1)S(1)} %shard_map.62), channel_id=1, source_target_pairs={{0,4},{1,3},{2,6},{3,5},{4,8},{5,7},{6,10},{7,9},{8,12},{9,11},{10... | collective-permute-start | bytes 393224 | tf_op jit(solution)/shard_map/ppermute | solution.py:31
  24.3 2.0 %collective-permute-start.8 = (bf16[128,512]{1,0:T(8,128)(2,1)S(1)}, bf16[128,512]{1,0:T(8,128)(2,1)S(1)}, u32[]{:S(2)}, u32[]{:S(2)}) collective-permute-start(bf16[128,512]{1,0:T(8,128)(2,1)S(1)} %shard_map.64.refs_2_), channel_id=1, source_target_pairs={{1,0},{0,1},{3,2},{2,3},{5,4},{4,5},{7,6},{6,7},{9,8},{8,9},{11,10... | collective-permute-start | bytes 393224 | tf_op jit(solution)/shard_map/ppermute | solution.py:37
  24.3 2.9 %collective-permute-start.6 = (bf16[128,512]{1,0:T(8,128)(2,1)S(1)}, bf16[128,512]{1,0:T(8,128)(2,1)S(1)}, u32[]{:S(2)}, u32[]{:S(2)}) collective-permute-start(bf16[128,512]{1,0:T(8,128)(2,1)S(1)} %shard_map.63.refs_0_), channel_id=1, source_target_pairs={{1,0},{0,1},{3,2},{2,3},{5,4},{4,5},{7,6},{6,7},{9,8},{8,9},{11,10... | collective-permute-start | bytes 393224 | tf_op jit(solution)/shard_map/ppermute | solution.py:37

commit v5 on v3

--- a/solution.py
+++ b/solution.py
@@ -22,9 +22,12 @@
 MARK = (8, HD)
 
 
-def shifted(block, axis, distance):
+def shifted(block, axis, distance, offset=0):
     size = lax.axis_size(axis)
-    return lax.ppermute(block, axis, [(i, (i + distance) % size) for i in range(size)])
+    route = [(i, i + distance) for i in range(offset, size - distance)]
+    route += [(i, i) for i in range(offset)]
+    route += [(size - distance + i, offset + i) for i in range(distance)]
+    return lax.ppermute(block, axis, sorted(route))
 
 
 def swapped(block, axis):
@@ -144,9 +147,9 @@
     )
 
 
-def far_kernel(axis, distances, last, mark_in, q_ref, *refs):
+def far_kernel(axis, pieces, last, mark_in, q_ref, *refs):
     me = lax.axis_index(axis)
-    count = 2 * len(distances)
+    count = len(pieces)
     blocks, state_in = refs[:count], refs[count]
     if last:
         state_out, (out_ref, log_ref, s_buf, p_buf) = None, refs[count + 1 :]
@@ -155,7 +158,7 @@
         mark[...] = mark_in[...]
     rows = blocks[0].shape[0]
     lowest = lowest_of(mark_in)
-    starts = [(who - d) * rows for d in distances for who in (me, me ^ 1)]
+    starts = [((me ^ side) - distance) * rows for distance, side in pieces]
     needed = functools.reduce(jnp.logical_or, [s + rows > lowest for s in starts])
 
     @pl.when(needed)
@@ -280,28 +283,31 @@
     reach = lax.axis_size(axis) // 2
     own, mark, queries = fetched(axis, queries, keys, values, windows)
     other = swapped(own, axis)
-    held = {4: shifted(own, axis, 4), 2: shifted(own, axis, 2)}
+    held = {d: shifted(own, axis, d) for d in (4, 2)}
     state, mark = attend(
         functools.partial(near_kernel, axis), mark, queries, [own, other], None, False
     )
     for first in range(2, reach + 1, 4):
         distances = [d for d in (first + 2, first) if d <= reach]
         last = first + 4 > reach
-        blocks = []
+        mine, theirs = {}, {}
         for d in distances:
             held[d] = tied(held[d], mark)
             if d + 4 <= reach:
-                held[d + 4] = shifted(held[d], axis, 4)
-            blocks += [held[d], swapped(held[d], axis)]
-        result = attend(
-            functools.partial(far_kernel, axis, distances, last),
-            mark,
-            queries,
-            blocks,
-            state,
-            last,
-        )
-        state, mark = result
+                held[d + 4] = shifted(held[d], axis, 4, d)
+            mine[d, 0] = held[d]
+            theirs[d, 1] = swapped(held[d], axis)
+        for blocks in (mine, theirs) if last else ({**mine, **theirs},):
+            final = last and blocks is theirs
+            result = attend(
+                functools.partial(far_kernel, axis, list(blocks), final),
+                mark,
+                queries,
+                list(blocks.values()),
+                state,
+                final,
+            )
+            state, mark = result
     return result[0], result[1].T
 
 

time: 26.4 us -> 29.5 us (1.12)
  the two profiles are of different devices: /device:TPU:15 before, /device:TPU:18 now
where the time goes in v5:
time: 29.5 us; the launch traced here: 29 us
  starting transfers between devices  13.6 us (46%)
  Pallas kernels  12.3 us (42%)
  waiting for transfers between devices  2.27 us (8%)
  between operations  0.77 us (3%)
    ppermute x4, starting transfers between devices, shifted(): return lax.ppermute(block, axis, sorted(route))  12.5 us
    pallas_call x4, Pallas kernels, attend(): pl.pallas_call(kernel, in_specs=[VMEM] * len(operands), out_specs=[VMEM]...  11 us
    ppermute x4, waiting for transfers between devices, shifted(): return lax.ppermute(block, axis, sorted(route))  2.26 us
    pallas_call x1, Pallas kernels, fetched(): pl.pallas_call(functools.partial(fetch_kernel, axis), in_specs=[HBM] * 4,...  1.34 us
    ppermute x5, starting transfers between devices, swapped(): lax.ppermute(block, axis, [(i ^ 1, i) for i in range(lax.axis_size(axis))])  1.13 us
  transfers between devices with their start and end apart: 9, of which 1 were waited for; matrix products, arithmetic and copies ran while one was open for 0% of the time, Pallas kernels for 26%

profile of v5, /device:TPU:18, one launch (start us, length us, event | category | flops | bytes accessed | tf_op | source)
XLA Modules:
  0.0 29.0 jit_solution(6331526267447179113)
XLA Ops:
  0.6 1.3 %shard_map.59 = (bf16[128,512]{1,0:T(8,128)(2,1)S(1)}, f32[8,128]{1,0:T(8,128)S(1)}, bf16[128,4096]{1,0:T(8,128)(2,1)S(1)}) custom-call(bf16[128,256]{1,0:T(8,128)(2,1)} %k_hbm.1, bf16[128,256]{1,0:T(8,128)(2,1)} %v_hbm.1, s32[16]{0:T(128)} %win_hbm.1, bf16[128,4096]{1,0:T(8,128)(2,1)} %q_hbm.1), custom_call_target="tpu_custom_call" | custom-call | tf_op jit(solution)/shard_map/pallas_call | solution.py:250
  2.0 0.1 collective-permute-start
  2.1 1.6 %collective-permute-start.2 = (bf16[128,512]{1,0:T(8,128)(2,1)S(1)}, bf16[128,512]{1,0:T(8,128)(2,1)S(1)}, u32[]{:S(2)}, u32[]{:S(2)}) collective-permute-start(bf16[128,512]{1,0:T(8,128)(2,1)S(1)} %get-tuple-element.15.own), channel_id=1, source_target_pairs={{0,2},{1,3},{2,4},{3,5},{4,6},{5,7},{6,8},{7,9},{8,10},{9,11},{10,... | collective-permute-start | bytes 393224 | tf_op jit(solution)/shard_map/ppermute | solution.py:30
  3.6 1.6 %collective-permute-start.1 = (bf16[128,512]{1,0:T(8,128)(2,1)S(1)}, bf16[128,512]{1,0:T(8,128)(2,1)S(1)}, u32[]{:S(2)}, u32[]{:S(2)}) collective-permute-start(bf16[128,512]{1,0:T(8,128)(2,1)S(1)} %get-tuple-element.15.own), channel_id=1, source_target_pairs={{0,4},{1,5},{2,6},{3,7},{4,8},{5,9},{6,10},{7,11},{8,12},{9,13},{1... | collective-permute-start | bytes 393224 | tf_op jit(solution)/shard_map/ppermute | solution.py:30
  5.2 0.0 collective-permute-done.other
  5.2 1.8 %shard_map.60 = (f32[144,4096]{1,0:T(8,128)S(1)}, f32[8,128]{1,0:T(8,128)S(1)}) custom-call(f32[8,128]{1,0:T(8,128)S(1)} %get-tuple-element.13.mark_in, bf16[128,4096]{1,0:T(8,128)(2,1)S(1)} %get-tuple-element.14.q_ref, bf16[128,512]{1,0:T(8,128)(2,1)S(1)} %get-tuple-element.15.own, bf16[128,512]{1,0:T(8,128)(2,1)S(1)} %collective-permute-done.other), custom_call_target="tpu_custom_call" | custom-call | flops 536870912 | bytes 1048576 | tf_op jit(solution)/shard_map/pallas_call | solution.py:209
  7.1 2.2 %collective-permute-done.2.block_ref = bf16[128,512]{1,0:T(8,128)(2,1)S(1)} collective-permute-done((bf16[128,512]{1,0:T(8,128)(2,1)S(1)}, bf16[128,512]{1,0:T(8,128)(2,1)S(1)}, u32[]{:S(2)}, u32[]{:S(2)}) %collective-permute-start.2) | collective-permute-done | bytes 131104 | tf_op jit(solution)/shard_map/ppermute | solution.py:30
  9.3 0.0 collective-permute-start.4
  9.3 0.0 collective-permute-done.1.block_ref
  9.3 0.5 %collective-permute-start.3 = (bf16[128,512]{1,0:T(8,128)(2,1)S(1)}, bf16[128,512]{1,0:T(8,128)(2,1)S(1)}, u32[]{:S(2)}, u32[]{:S(2)}) collective-permute-start(bf16[128,512]{1,0:T(8,128)(2,1)S(1)} %shard_map.61.refs_0_), channel_id=1, source_target_pairs={{1,0},{0,1},{3,2},{2,3},{5,4},{4,5},{7,6},{6,7},{9,8},{8,9},{11,10... | collective-permute-start | bytes 393224 | tf_op jit(solution)/shard_map/ppermute | solution.py:34
  9.8 3.5 %collective-permute-start.6 = (bf16[128,512]{1,0:T(8,128)(2,1)S(1)}, bf16[128,512]{1,0:T(8,128)(2,1)S(1)}, u32[]{:S(2)}, u32[]{:S(2)}) collective-permute-start(bf16[128,512]{1,0:T(8,128)(2,1)S(1)} %shard_map.62.refs_1_), channel_id=1, source_target_pairs={{0,0},{1,1},{2,6},{3,7},{4,8},{5,9},{6,10},{7,11},{8,12},{9,13},{1... | collective-permute-start | bytes 393224 | tf_op jit(solution)/shard_map/ppermute | solution.py:30
  13.3 5.9 %collective-permute-start.5 = (bf16[128,512]{1,0:T(8,128)(2,1)S(1)}, bf16[128,512]{1,0:T(8,128)(2,1)S(1)}, u32[]{:S(2)}, u32[]{:S(2)}) collective-permute-start(bf16[128,512]{1,0:T(8,128)(2,1)S(1)} %shard_map.61.refs_0_), channel_id=1, source_target_pairs={{0,0},{1,1},{2,2},{3,3},{4,8},{5,9},{6,10},{7,11},{8,12},{9,13},{1... | collective-permute-start | bytes 393224 | tf_op jit(solution)/shard_map/ppermute | solution.py:30
  19.2 0.0 collective-permute-done.4.refs_3_
  19.2 0.0 collective-permute-done.3.refs_2_
  19.2 3.5 %shard_map.63 = (f32[144,4096]{1,0:T(8,128)S(1)}, f32[8,128]{1,0:T(8,128)S(1)}) custom-call(f32[8,128]{1,0:T(8,128)S(1)} %get-tuple-element.16.earlier_ref.mark_in, bf16[128,4096]{1,0:T(8,128)(2,1)S(1)} %get-tuple-element.14.q_ref, bf16[128,512]{1,0:T(8,128)(2,1)S(1)} %shard_map.61.refs_0_, ...), custom_call_target="tpu_custom_call", output_to_operand_aliasing={{0}: (6, {})} | custom-call | flops 1073741824 | bytes 1048576 | tf_op jit(solution)/shard_map/pallas_call | solution.py:209
  22.7 0.0 collective-permute-done.6.block_ref
  22.7 0.1 collective-permute-start.8
  22.8 0.0 collective-permute-done.5.block_ref
  22.8 0.5 %collective-permute-start.7 = (bf16[128,512]{1,0:T(8,128)(2,1)S(1)}, bf16[128,512]{1,0:T(8,128)(2,1)S(1)}, u32[]{:S(2)}, u32[]{:S(2)}) collective-permute-start(bf16[128,512]{1,0:T(8,128)(2,1)S(1)} %shard_map.64.refs_0_), channel_id=1, source_target_pairs={{1,0},{0,1},{3,2},{2,3},{5,4},{4,5},{7,6},{6,7},{9,8},{8,9},{11,10... | collective-permute-start | bytes 393224 | tf_op jit(solution)/shard_map/ppermute | solution.py:34
  23.3 2.4 %shard_map.66 = (f32[144,4096]{1,0:T(8,128)S(1)}, f32[8,128]{1,0:T(8,128)S(1)}) custom-call(f32[8,128]{1,0:T(8,128)S(1)} %get-tuple-element.18.earlier_ref.mark_in, bf16[128,4096]{1,0:T(8,128)(2,1)S(1)} %get-tuple-element.14.q_ref, bf16[128,512]{1,0:T(8,128)(2,1)S(1)} %shard_map.64.refs_0_, ...), custom_call_target="tpu_custom_call", output_to_operand_aliasing={{0}: (4, {})} | custom-call | flops 536870912 | bytes 1048576 | tf_op jit(solution)/shard_map/pallas_call | solution.py:209
  25.7 0.0 collective-permute-done.8.refs_1_
  25.7 0.0 collective-permute-done.7.refs_0_
  25.7 3.3 %shard_map.67 = (bf16[128,4096]{1,0:T(8,128)(2,1)}, f32[32,128]{1,0:T(8,128)}) custom-call(f32[8,128]{1,0:T(8,128)S(1)} %get-tuple-element.20.mark_in, bf16[128,4096]{1,0:T(8,128)(2,1)S(1)} %get-tuple-element.14.q_ref, bf16[128,512]{1,0:T(8,128)(2,1)S(1)} %collective-permute-done.7.refs_0_, bf16[128,512]{1,0:T(8,128)(2,1)S(1)} %collective-permute-done.8.refs_1_, ...), custom_call_target="tpu_custom_call" | custom-call | flops 536870912 | bytes 1048576 | tf_op jit(solution)/shard_map/pallas_call | solution.py:209
  (4 shorter events, 0.0 us)
Async XLA Ops:
  2.0 3.2 %collective-permute-start = (bf16[128,512]{1,0:T(8,128)(2,1)S(1)}, bf16[128,512]{1,0:T(8,128)(2,1)S(1)}, u32[]{:S(2)}, u32[]{:S(2)}) collective-permute-start(bf16[128,512]{1,0:T(8,128)(2,1)S(1)} %get-tuple-element.15.own), channel_id=1, source_target_pairs={{1,0},{0,1},{3,2},{2,3},{5,4},{4,5},{7,6},{6,7},{9,8},{8,9},{11,10... | collective-permute-start | bytes 393224 | tf_op jit(solution)/shard_map/ppermute | solution.py:34
  2.1 7.2 %collective-permute-start.2 = (bf16[128,512]{1,0:T(8,128)(2,1)S(1)}, bf16[128,512]{1,0:T(8,128)(2,1)S(1)}, u32[]{:S(2)}, u32[]{:S(2)}) collective-permute-start(bf16[128,512]{1,0:T(8,128)(2,1)S(1)} %get-tuple-element.15.own), channel_id=1, source_target_pairs={{0,2},{1,3},{2,4},{3,5},{4,6},{5,7},{6,8},{7,9},{8,10},{9,11},{10,... | collective-permute-start | bytes 393224 | tf_op jit(solution)/shard_map/ppermute | solution.py:30
  3.6 5.7 %collective-permute-start.1 = (bf16[128,512]{1,0:T(8,128)(2,1)S(1)}, bf16[128,512]{1,0:T(8,128)(2,1)S(1)}, u32[]{:S(2)}, u32[]{:S(2)}) collective-permute-start(bf16[128,512]{1,0:T(8,128)(2,1)S(1)} %get-tuple-element.15.own), channel_id=1, source_target_pairs={{0,4},{1,5},{2,6},{3,7},{4,8},{5,9},{6,10},{7,11},{8,12},{9,13},{1... | collective-permute-start | bytes 393224 | tf_op jit(solution)/shard_map/ppermute | solution.py:30
  9.3 9.9 %collective-permute-start.4 = (bf16[128,512]{1,0:T(8,128)(2,1)S(1)}, bf16[128,512]{1,0:T(8,128)(2,1)S(1)}, u32[]{:S(2)}, u32[]{:S(2)}) collective-permute-start(bf16[128,512]{1,0:T(8,128)(2,1)S(1)} %shard_map.62.refs_1_), channel_id=1, source_target_pairs={{1,0},{0,1},{3,2},{2,3},{5,4},{4,5},{7,6},{6,7},{9,8},{8,9},{11,10... | collective-permute-start | bytes 393224 | tf_op jit(solution)/shard_map/ppermute | solution.py:34
  9.3 9.9 %collective-permute-start.3 = (bf16[128,512]{1,0:T(8,128)(2,1)S(1)}, bf16[128,512]{1,0:T(8,128)(2,1)S(1)}, u32[]{:S(2)}, u32[]{:S(2)}) collective-permute-start(bf16[128,512]{1,0:T(8,128)(2,1)S(1)} %shard_map.61.refs_0_), channel_id=1, source_target_pairs={{1,0},{0,1},{3,2},{2,3},{5,4},{4,5},{7,6},{6,7},{9,8},{8,9},{11,10... | collective-permute-start | bytes 393224 | tf_op jit(solution)/shard_map/ppermute | solution.py:34
  9.8 12.9 %collective-permute-start.6 = (bf16[128,512]{1,0:T(8,128)(2,1)S(1)}, bf16[128,512]{1,0:T(8,128)(2,1)S(1)}, u32[]{:S(2)}, u32[]{:S(2)}) collective-permute-start(bf16[128,512]{1,0:T(8,128)(2,1)S(1)} %shard_map.62.refs_1_), channel_id=1, source_target_pairs={{0,0},{1,1},{2,6},{3,7},{4,8},{5,9},{6,10},{7,11},{8,12},{9,13},{1... | collective-permute-start | bytes 393224 | tf_op jit(solution)/shard_map/ppermute | solution.py:30
  13.3 9.5 %collective-permute-start.5 = (bf16[128,512]{1,0:T(8,128)(2,1)S(1)}, bf16[128,512]{1,0:T(8,128)(2,1)S(1)}, u32[]{:S(2)}, u32[]{:S(2)}) collective-permute-start(bf16[128,512]{1,0:T(8,128)(2,1)S(1)} %shard_map.61.refs_0_), channel_id=1, source_target_pairs={{0,0},{1,1},{2,2},{3,3},{4,8},{5,9},{6,10},{7,11},{8,12},{9,13},{1... | collective-permute-start | bytes 393224 | tf_op jit(solution)/shard_map/ppermute | solution.py:30
  22.7 2.9 %collective-permute-start.8 = (bf16[128,512]{1,0:T(8,128)(2,1)S(1)}, bf16[128,512]{1,0:T(8,128)(2,1)S(1)}, u32[]{:S(2)}, u32[]{:S(2)}) collective-permute-start(bf16[128,512]{1,0:T(8,128)(2,1)S(1)} %shard_map.65.refs_1_), channel_id=1, source_target_pairs={{1,0},{0,1},{3,2},{2,3},{5,4},{4,5},{7,6},{6,7},{9,8},{8,9},{11,10... | collective-permute-start | bytes 393224 | tf_op jit(solution)/shard_map/ppermute | solution.py:34
  22.8 2.9 %collective-permute-start.7 = (bf16[128,512]{1,0:T(8,128)(2,1)S(1)}, bf16[128,512]{1,0:T(8,128)(2,1)S(1)}, u32[]{:S(2)}, u32[]{:S(2)}) collective-permute-start(bf16[128,512]{1,0:T(8,128)(2,1)S(1)} %shard_map.64.refs_0_), channel_id=1, source_target_pairs={{1,0},{0,1},{3,2},{2,3},{5,4},{4,5},{7,6},{6,7},{9,8},{8,9},{11,10... | collective-permute-start | bytes 393224 | tf_op jit(solution)/shard_map/ppermute | solution.py:34

commit v6 on v3

--- a/solution.py
+++ b/solution.py
@@ -144,9 +144,9 @@
     )
 
 
-def far_kernel(axis, distances, last, mark_in, q_ref, *refs):
+def far_kernel(axis, pieces, last, mark_in, q_ref, *refs):
     me = lax.axis_index(axis)
-    count = 2 * len(distances)
+    count = len(pieces)
     blocks, state_in = refs[:count], refs[count]
     if last:
         state_out, (out_ref, log_ref, s_buf, p_buf) = None, refs[count + 1 :]
@@ -155,7 +155,7 @@
         mark[...] = mark_in[...]
     rows = blocks[0].shape[0]
     lowest = lowest_of(mark_in)
-    starts = [(who - d) * rows for d in distances for who in (me, me ^ 1)]
+    starts = [((me ^ side) - distance) * rows for distance, side in pieces]
     needed = functools.reduce(jnp.logical_or, [s + rows > lowest for s in starts])
 
     @pl.when(needed)
@@ -280,24 +280,27 @@
     reach = lax.axis_size(axis) // 2
     own, mark, queries = fetched(axis, queries, keys, values, windows)
     other = swapped(own, axis)
-    held = {4: shifted(own, axis, 4), 2: shifted(own, axis, 2)}
+    held = {d: shifted(own, axis, d) for d in (4, 2)}
     state, mark = attend(
         functools.partial(near_kernel, axis), mark, queries, [own, other], None, False
     )
-    for first in range(2, reach + 1, 4):
-        distances = [d for d in (first + 2, first) if d <= reach]
-        last = first + 4 > reach
-        blocks = []
-        for d in distances:
+    order = [d for first in range(2, reach + 1, 4) for d in (first + 2, first) if d <= reach]
+    early = max(len(order) - 2, 0)
+    groups = [[d] for d in order[:early]] + [order[early:]]
+    for group in groups:
+        last = group is groups[-1]
+        blocks = {}
+        for d in group:
             held[d] = tied(held[d], mark)
             if d + 4 <= reach:
                 held[d + 4] = shifted(held[d], axis, 4)
-            blocks += [held[d], swapped(held[d], axis)]
+            blocks[d, 0] = held[d]
+            blocks[d, 1] = swapped(held[d], axis)
         result = attend(
-            functools.partial(far_kernel, axis, distances, last),
+            functools.partial(far_kernel, axis, list(blocks), last),
             mark,
             queries,
-            blocks,
+            list(blocks.values()),
             state,
             last,
         )

time: 26.4 us -> 33.4 us (1.27)
  the two profiles are of different devices: /device:TPU:15 before, /device:TPU:0 now
where the time goes in v6:
time: 33.4 us; the launch traced here: 33.2 us
  waiting for transfers between devices  22.3 us (67%)
  Pallas kernels  5.51 us (16%)
  starting transfers between devices  4.74 us (14%)
  between operations  0.68 us (2%)
    ppermute x4, waiting for transfers between devices, shifted(): lax.ppermute(block, axis, [(i, (i + distance) % size) for i in range(size)])  19.7 us
    ppermute x4, starting transfers between devices, shifted(): lax.ppermute(block, axis, [(i, (i + distance) % size) for i in range(size)])  4.21 us
    pallas_call x4, Pallas kernels, attend(): pl.pallas_call(kernel, in_specs=[VMEM] * len(operands), out_specs=[VMEM]...  4.17 us
    ppermute x5, waiting for transfers between devices, swapped(): lax.ppermute(block, axis, [(i ^ 1, i) for i in range(lax.axis_size(axis))])  2.63 us
    pallas_call x1, Pallas kernels, fetched(): pl.pallas_call(functools.partial(fetch_kernel, axis), in_specs=[HBM] * 4,...  1.34 us
  transfers between devices with their start and end apart: 9, of which 6 were waited for; matrix products, arithmetic and copies ran while one was open for 0% of the time, Pallas kernels for 8%

profile of v6, /device:TPU:0, one launch (start us, length us, event | category | flops | bytes accessed | tf_op | source)
XLA Modules:
  0.0 33.2 jit_solution(2474218200582092844)
XLA Ops:
  0.6 1.3 %shard_map.59 = (bf16[128,512]{1,0:T(8,128)(2,1)S(1)}, f32[8,128]{1,0:T(8,128)S(1)}, bf16[128,4096]{1,0:T(8,128)(2,1)S(1)}) custom-call(bf16[128,256]{1,0:T(8,128)(2,1)} %k_hbm.1, bf16[128,256]{1,0:T(8,128)(2,1)} %v_hbm.1, s32[16]{0:T(128)} %win_hbm.1, bf16[128,4096]{1,0:T(8,128)(2,1)} %q_hbm.1), custom_call_target="tpu_custom_call" | custom-call | tf_op jit(solution)/shard_map/pallas_call | solution.py:247
  2.0 0.5 %collective-permute-start = (bf16[128,512]{1,0:T(8,128)(2,1)S(1)}, bf16[128,512]{1,0:T(8,128)(2,1)S(1)}, u32[]{:S(2)}, u32[]{:S(2)}) collective-permute-start(bf16[128,512]{1,0:T(8,128)(2,1)S(1)} %get-tuple-element.15.own), channel_id=1, source_target_pairs={{1,0},{0,1},{3,2},{2,3},{5,4},{4,5},{7,6},{6,7},{9,8},{8,9},{11,10... | collective-permute-start | bytes 393224 | tf_op jit(solution)/shard_map/ppermute | solution.py:31
  2.5 2.6 %collective-permute-start.1 = (bf16[128,512]{1,0:T(8,128)(2,1)S(1)}, bf16[128,512]{1,0:T(8,128)(2,1)S(1)}, u32[]{:S(2)}, u32[]{:S(2)}) collective-permute-start(bf16[128,512]{1,0:T(8,128)(2,1)S(1)} %get-tuple-element.15.own), channel_id=1, source_target_pairs={{0,4},{1,5},{2,6},{3,7},{4,8},{5,9},{6,10},{7,11},{8,12},{9,13},{1... | collective-permute-start | bytes 393224 | tf_op jit(solution)/shard_map/ppermute | solution.py:27
  5.1 0.0 collective-permute-done.other
  5.1 1.8 %shard_map.60 = (f32[144,4096]{1,0:T(8,128)S(1)}, f32[8,128]{1,0:T(8,128)S(1)}) custom-call(f32[8,128]{1,0:T(8,128)S(1)} %get-tuple-element.13.mark_in, bf16[128,4096]{1,0:T(8,128)(2,1)S(1)} %get-tuple-element.14.q_ref, bf16[128,512]{1,0:T(8,128)(2,1)S(1)} %get-tuple-element.15.own, bf16[128,512]{1,0:T(8,128)(2,1)S(1)} %collective-permute-done.other), custom_call_target="tpu_custom_call" | custom-call | flops 536870912 | bytes 1048576 | tf_op jit(solution)/shard_map/pallas_call | solution.py:206
  7.0 4.3 %collective-permute-done.1.block_ref = bf16[128,512]{1,0:T(8,128)(2,1)S(1)} collective-permute-done((bf16[128,512]{1,0:T(8,128)(2,1)S(1)}, bf16[128,512]{1,0:T(8,128)(2,1)S(1)}, u32[]{:S(2)}, u32[]{:S(2)}) %collective-permute-start.1) | collective-permute-done | bytes 131104 | tf_op jit(solution)/shard_map/ppermute | solution.py:27
  11.3 0.0 collective-permute-start.2
  11.3 1.5 %collective-permute-start.3 = (bf16[128,512]{1,0:T(8,128)(2,1)S(1)}, bf16[128,512]{1,0:T(8,128)(2,1)S(1)}, u32[]{:S(2)}, u32[]{:S(2)}) collective-permute-start(bf16[128,512]{1,0:T(8,128)(2,1)S(1)} %get-tuple-element.15.own), channel_id=1, source_target_pairs={{0,2},{1,3},{2,4},{3,5},{4,6},{5,7},{6,8},{7,9},{8,10},{9,11},{10,... | collective-permute-start | bytes 393224 | tf_op jit(solution)/shard_map/ppermute | solution.py:27
  12.8 0.0 collective-permute-done.2.refs_1_
  12.8 0.4 %shard_map.62 = (f32[144,4096]{1,0:T(8,128)S(1)}, f32[8,128]{1,0:T(8,128)S(1)}) custom-call(f32[8,128]{1,0:T(8,128)S(1)} %get-tuple-element.16.earlier_ref.mark_in, bf16[128,4096]{1,0:T(8,128)(2,1)S(1)} %get-tuple-element.14.q_ref, bf16[128,512]{1,0:T(8,128)(2,1)S(1)} %shard_map.61.refs_0_, ...), custom_call_target="tpu_custom_call", output_to_operand_aliasing={{0}: (4, {})} | custom-call | flops 536870912 | bytes 1048576 | tf_op jit(solution)/shard_map/pallas_call | solution.py:206
  13.2 6.6 %collective-permute-done.3.block_ref = bf16[128,512]{1,0:T(8,128)(2,1)S(1)} collective-permute-done((bf16[128,512]{1,0:T(8,128)(2,1)S(1)}, bf16[128,512]{1,0:T(8,128)(2,1)S(1)}, u32[]{:S(2)}, u32[]{:S(2)}) %collective-permute-start.3) | collective-permute-done | bytes 131104 | tf_op jit(solution)/shard_map/ppermute | solution.py:27
  19.9 0.0 collective-permute-start.4
  19.9 0.0 collective-permute-start.7
  19.9 0.1 collective-permute-start.5
  19.9 1.3 %collective-permute-done.4.refs_1_ = bf16[128,512]{1,0:T(8,128)(2,1)S(1)} collective-permute-done((bf16[128,512]{1,0:T(8,128)(2,1)S(1)}, bf16[128,512]{1,0:T(8,128)(2,1)S(1)}, u32[]{:S(2)}, u32[]{:S(2)}) %collective-permute-start.4) | collective-permute-done | bytes 131104 | tf_op jit(solution)/shard_map/ppermute | solution.py:31
  21.2 0.4 %shard_map.64 = (f32[144,4096]{1,0:T(8,128)S(1)}, f32[8,128]{1,0:T(8,128)S(1)}) custom-call(f32[8,128]{1,0:T(8,128)S(1)} %get-tuple-element.18.earlier_ref.mark_in, bf16[128,4096]{1,0:T(8,128)(2,1)S(1)} %get-tuple-element.14.q_ref, bf16[128,512]{1,0:T(8,128)(2,1)S(1)} %shard_map.63.refs_0_, ...), custom_call_target="tpu_custom_call", output_to_operand_aliasing={{0}: (4, {})} | custom-call | flops 536870912 | bytes 1048576 | tf_op jit(solution)/shard_map/pallas_call | solution.py:206
  21.7 6.3 %collective-permute-done.7.block_ref = bf16[128,512]{1,0:T(8,128)(2,1)S(1)} collective-permute-done((bf16[128,512]{1,0:T(8,128)(2,1)S(1)}, bf16[128,512]{1,0:T(8,128)(2,1)S(1)}, u32[]{:S(2)}, u32[]{:S(2)}) %collective-permute-start.7) | collective-permute-done | bytes 131104 | tf_op jit(solution)/shard_map/ppermute | solution.py:27
  28.0 0.0 collective-permute-start.8
  28.0 2.4 %collective-permute-done.5.block_ref = bf16[128,512]{1,0:T(8,128)(2,1)S(1)} collective-permute-done((bf16[128,512]{1,0:T(8,128)(2,1)S(1)}, bf16[128,512]{1,0:T(8,128)(2,1)S(1)}, u32[]{:S(2)}, u32[]{:S(2)}) %collective-permute-start.5) | collective-permute-done | bytes 131104 | tf_op jit(solution)/shard_map/ppermute | solution.py:27
  30.4 0.0 collective-permute-start.6
  30.4 0.0 collective-permute-done.8.refs_3_
  30.4 1.3 %collective-permute-done.6.refs_1_ = bf16[128,512]{1,0:T(8,128)(2,1)S(1)} collective-permute-done((bf16[128,512]{1,0:T(8,128)(2,1)S(1)}, bf16[128,512]{1,0:T(8,128)(2,1)S(1)}, u32[]{:S(2)}, u32[]{:S(2)}) %collective-permute-start.6) | collective-permute-done | bytes 131104 | tf_op jit(solution)/shard_map/ppermute | solution.py:31
  31.7 1.5 %shard_map.67 = (bf16[128,4096]{1,0:T(8,128)(2,1)}, f32[32,128]{1,0:T(8,128)}) custom-call(f32[8,128]{1,0:T(8,128)S(1)} %get-tuple-element.20.earlier_ref.mark_in, bf16[128,4096]{1,0:T(8,128)(2,1)S(1)} %get-tuple-element.14.q_ref, bf16[128,512]{1,0:T(8,128)(2,1)S(1)} %shard_map.65.refs_0_, bf16[128,512]{1,0:T(8,128)(2,1)S(1)} %collective-permute-done.6.refs_1_, ...), custom_call_target="tpu_custom_call" | custom-call | flops 1073741824 | bytes 1048576 | tf_op jit(solution)/shard_map/pallas_call | solution.py:206
  (4 shorter events, 0.0 us)
Async XLA Ops:
  2.0 3.2 %collective-permute-start = (bf16[128,512]{1,0:T(8,128)(2,1)S(1)}, bf16[128,512]{1,0:T(8,128)(2,1)S(1)}, u32[]{:S(2)}, u32[]{:S(2)}) collective-permute-start(bf16[128,512]{1,0:T(8,128)(2,1)S(1)} %get-tuple-element.15.own), channel_id=1, source_target_pairs={{1,0},{0,1},{3,2},{2,3},{5,4},{4,5},{7,6},{6,7},{9,8},{8,9},{11,10... | collective-permute-start | bytes 393224 | tf_op jit(solution)/shard_map/ppermute | solution.py:31
  2.5 8.8 %collective-permute-start.1 = (bf16[128,512]{1,0:T(8,128)(2,1)S(1)}, bf16[128,512]{1,0:T(8,128)(2,1)S(1)}, u32[]{:S(2)}, u32[]{:S(2)}) collective-permute-start(bf16[128,512]{1,0:T(8,128)(2,1)S(1)} %get-tuple-element.15.own), channel_id=1, source_target_pairs={{0,4},{1,5},{2,6},{3,7},{4,8},{5,9},{6,10},{7,11},{8,12},{9,13},{1... | collective-permute-start | bytes 393224 | tf_op jit(solution)/shard_map/ppermute | solution.py:27
  11.3 1.5 %collective-permute-start.2 = (bf16[128,512]{1,0:T(8,128)(2,1)S(1)}, bf16[128,512]{1,0:T(8,128)(2,1)S(1)}, u32[]{:S(2)}, u32[]{:S(2)}) collective-permute-start(bf16[128,512]{1,0:T(8,128)(2,1)S(1)} %shard_map.61.refs_0_), channel_id=1, source_target_pairs={{1,0},{0,1},{3,2},{2,3},{5,4},{4,5},{7,6},{6,7},{9,8},{8,9},{11,10... | collective-permute-start | bytes 393224 | tf_op jit(solution)/shard_map/ppermute | solution.py:31
  11.3 8.6 %collective-permute-start.3 = (bf16[128,512]{1,0:T(8,128)(2,1)S(1)}, bf16[128,512]{1,0:T(8,128)(2,1)S(1)}, u32[]{:S(2)}, u32[]{:S(2)}) collective-permute-start(bf16[128,512]{1,0:T(8,128)(2,1)S(1)} %get-tuple-element.15.own), channel_id=1, source_target_pairs={{0,2},{1,3},{2,4},{3,5},{4,6},{5,7},{6,8},{7,9},{8,10},{9,11},{10,... | collective-permute-start | bytes 393224 | tf_op jit(solution)/shard_map/ppermute | solution.py:27
  19.9 1.3 %collective-permute-start.4 = (bf16[128,512]{1,0:T(8,128)(2,1)S(1)}, bf16[128,512]{1,0:T(8,128)(2,1)S(1)}, u32[]{:S(2)}, u32[]{:S(2)}) collective-permute-start(bf16[128,512]{1,0:T(8,128)(2,1)S(1)} %shard_map.63.refs_0_), channel_id=1, source_target_pairs={{1,0},{0,1},{3,2},{2,3},{5,4},{4,5},{7,6},{6,7},{9,8},{8,9},{11,10... | collective-permute-start | bytes 393224 | tf_op jit(solution)/shard_map/ppermute | solution.py:31
  19.9 8.1 %collective-permute-start.7 = (bf16[128,512]{1,0:T(8,128)(2,1)S(1)}, bf16[128,512]{1,0:T(8,128)(2,1)S(1)}, u32[]{:S(2)}, u32[]{:S(2)}) collective-permute-start(bf16[128,512]{1,0:T(8,128)(2,1)S(1)} %shard_map.63.refs_0_), channel_id=1, source_target_pairs={{0,4},{1,5},{2,6},{3,7},{4,8},{5,9},{6,10},{7,11},{8,12},{9,13},{1... | collective-permute-start | bytes 393224 | tf_op jit(solution)/shard_map/ppermute | solution.py:27
  19.9 10.5 %collective-permute-start.5 = (bf16[128,512]{1,0:T(8,128)(2,1)S(1)}, bf16[128,512]{1,0:T(8,128)(2,1)S(1)}, u32[]{:S(2)}, u32[]{:S(2)}) collective-permute-start(bf16[128,512]{1,0:T(8,128)(2,1)S(1)} %shard_map.61.refs_0_), channel_id=1, source_target_pairs={{0,4},{1,5},{2,6},{3,7},{4,8},{5,9},{6,10},{7,11},{8,12},{9,13},{1... | collective-permute-start | bytes 393224 | tf_op jit(solution)/shard_map/ppermute | solution.py:27
  28.0 2.4 %collective-permute-start.8 = (bf16[128,512]{1,0:T(8,128)(2,1)S(1)}, bf16[128,512]{1,0:T(8,128)(2,1)S(1)}, u32[]{:S(2)}, u32[]{:S(2)}) collective-permute-start(bf16[128,512]{1,0:T(8,128)(2,1)S(1)} %shard_map.66.refs_2_), channel_id=1, source_target_pairs={{1,0},{0,1},{3,2},{2,3},{5,4},{4,5},{7,6},{6,7},{9,8},{8,9},{11,10... | collective-permute-start | bytes 393224 | tf_op jit(solution)/shard_map/ppermute | solution.py:31
  30.4 1.3 %collective-permute-start.6 = (bf16[128,512]{1,0:T(8,128)(2,1)S(1)}, bf16[128,512]{1,0:T(8,128)(2,1)S(1)}, u32[]{:S(2)}, u32[]{:S(2)}) collective-permute-start(bf16[128,512]{1,0:T(8,128)(2,1)S(1)} %shard_map.65.refs_0_), channel_id=1, source_target_pairs={{1,0},{0,1},{3,2},{2,3},{5,4},{4,5},{7,6},{6,7},{9,8},{8,9},{11,10... | collective-permute-start | bytes 393224 | tf_op jit(solution)/shard_map/ppermute | solution.py:31

commit v7 on v3

--- a/solution.py
+++ b/solution.py
@@ -35,7 +35,7 @@
     return lax.dot_general(left, right, (dims, ((), ())), preferred_element_type=jnp.float32)
 
 
-def run_chunks(q_ref, blocks, flags, row_flags, state_in, state_out, s_buf, p_buf, out_ref, log_ref):
+def run_chunks(q_ref, blocks, flags, row_flags, state_in, state_out, s_buf, p_buf, outs):
     rows, width = q_ref.shape
     groups = blocks[0].shape[1] // (2 * HD)
     slots, keys, wide = s_buf.shape
@@ -87,11 +87,11 @@
         summed = dot(value_ext[c // per_group], p_buf[c % slots], ((1,), (0,)))[:TOP_ROW]
         if factor is not None:
             summed = summed + state_in[0:TOP_ROW, lanes] * factor
-        if out_ref is None:
+        if outs is None:
             state_out[0:TOP_ROW, lanes] = summed
             state_out[TOP_ROW : TOP_ROW + 1, lanes] = top
         else:
-            finish(summed, top, c, heads, out_ref, log_ref)
+            finish(summed, top, c, heads, *outs)
 
     held = {}
     for t in range(chunks + 2):
@@ -103,16 +103,22 @@
             sum_up(t - 2, *held.pop(t - 2))
 
 
-def finish(summed, top, c, heads, out_ref, log_ref):
+def write_back(c, wide, out_hbm, out_buf, sems):
+    lanes = pl.ds(c * wide, wide)
+    return pltpu.make_async_copy(out_buf.at[:, lanes], out_hbm.at[:, lanes], sems.at[c])
+
+
+def finish(summed, top, c, heads, out_hbm, log_ref, out_buf, sems):
     total = summed[HD : HD + 1]
     result = summed[:HD] * (1.0 / total)
     logs = top * SCALE + jnp.log(total)
     first = c * heads
     for h in range(heads):
         lanes = slice(h * HD, (h + 1) * HD)
-        out_ref[:, (first + h) * HD : (first + h + 1) * HD] = result[:, lanes].T.astype(
-            out_ref.dtype
+        out_buf[:, (first + h) * HD : (first + h + 1) * HD] = result[:, lanes].T.astype(
+            out_buf.dtype
         )
+    write_back(c, heads * HD, out_hbm, out_buf, sems).start()
     log_ref[first : first + heads, :] = jnp.concatenate(
         [logs[:, h * HD : (h + 1) * HD] for h in range(heads)], 0
     )
@@ -140,7 +146,7 @@
     flags = jnp.concatenate([other_flags, own_flags], 0).astype(jnp.bfloat16)
     row_flags = jnp.where((lane == 0) | (lane > row), HIDDEN, 0.0).astype(jnp.bfloat16)
     run_chunks(
-        q_ref, [other, own], flags, row_flags, None, state_out, s_buf, p_buf, None, None
+        q_ref, [other, own], flags, row_flags, None, state_out, s_buf, p_buf, None
     )
 
 
@@ -149,9 +155,10 @@
     count = 2 * len(distances)
     blocks, state_in = refs[:count], refs[count]
     if last:
-        state_out, (out_ref, log_ref, s_buf, p_buf) = None, refs[count + 1 :]
+        state_out, (out_hbm, log_ref, s_buf, p_buf, out_buf, sems) = None, refs[count + 1 :]
+        outs = (out_hbm, log_ref, out_buf, sems)
     else:
-        (state_out, mark, s_buf, p_buf), out_ref, log_ref = refs[count + 1 :], None, None
+        (state_out, mark, s_buf, p_buf), outs = refs[count + 1 :], None
         mark[...] = mark_in[...]
     rows = blocks[0].shape[0]
     lowest = lowest_of(mark_in)
@@ -166,19 +173,25 @@
         ).astype(jnp.bfloat16)
         row_flags = jnp.where(lane == 0, HIDDEN, 0.0).astype(jnp.bfloat16)
         run_chunks(
-            q_ref, blocks, flags, row_flags, state_in, state_out, s_buf, p_buf, out_ref, log_ref
+            q_ref, blocks, flags, row_flags, state_in, state_out, s_buf, p_buf, outs
         )
+
+    wide = s_buf.shape[2]
+    chunks = q_ref.shape[1] // wide
 
     @pl.when(jnp.logical_not(needed))
     def _():
         if last:
-            wide = s_buf.shape[2]
-            for c in range(q_ref.shape[1] // wide):
+            for c in range(chunks):
                 lanes = slice(c * wide, (c + 1) * wide)
                 top = state_in[TOP_ROW : TOP_ROW + 1, lanes]
-                finish(state_in[0:TOP_ROW, lanes], top, c, wide // HD, out_ref, log_ref)
+                finish(state_in[0:TOP_ROW, lanes], top, c, wide // HD, *outs)
         else:
             state_out[...] = state_in[...]
+
+    if last:
+        for c in range(chunks):
+            write_back(c, wide, out_hbm, out_buf, sems).wait()
 
 
 def attend(kernel, mark, queries, blocks, state, last):
@@ -203,15 +216,21 @@
             jax.ShapeDtypeStruct((STATE_ROWS, width), jnp.float32),
             jax.ShapeDtypeStruct(MARK, jnp.float32),
         ]
+    scratch = [
+        pltpu.VMEM((2, keys, wide), jnp.float32),
+        pltpu.VMEM((2, keys, wide), jnp.bfloat16),
+    ]
+    if last:
+        scratch += [
+            pltpu.VMEM((rows, width), jnp.bfloat16),
+            pltpu.SemaphoreType.DMA((width // wide,)),
+        ]
     return pl.pallas_call(
         kernel,
         in_specs=[VMEM] * len(operands),
-        out_specs=[VMEM] * len(out_shape),
+        out_specs=[HBM, VMEM] if last else [VMEM] * 2,
         out_shape=out_shape,
-        scratch_shapes=[
-            pltpu.VMEM((2, keys, wide), jnp.float32),
-            pltpu.VMEM((2, keys, wide), jnp.bfloat16),
-        ],
+        scratch_shapes=scratch,
         input_output_aliases=aliases,
         cost_estimate=pl.CostEstimate(
             flops=4 * keys * rows * width,
@@ -285,7 +304,7 @@
         functools.partial(near_kernel, axis), mark, queries, [own, other], None, False
     )
     for first in range(2, reach + 1, 4):
-        distances = [d for d in (first + 2, first) if d <= reach]
+        distances = [d for d in (first, first + 2) if d <= reach]
         last = first + 4 > reach
         blocks = []
         for d in distances:

time: 26.4 us -> 28.9 us (1.095)
  the two profiles are of different devices: /device:TPU:15 before, /device:TPU:0 now
where the time goes in v7:
time: 28.9 us; the launch traced here: 28.8 us
  waiting for transfers between devices  16.6 us (57%)
  starting transfers between devices  5.98 us (21%)
  Pallas kernels  5.49 us (19%)
  between operations  0.66 us (2%)
    ppermute x4, waiting for transfers between devices, shifted(): lax.ppermute(block, axis, [(i, (i + distance) % size) for i in range(size)])  15.2 us
    ppermute x4, starting transfers between devices, shifted(): lax.ppermute(block, axis, [(i, (i + distance) % size) for i in range(size)])  5.45 us
    pallas_call x3, Pallas kernels, attend(): pl.pallas_call(kernel, in_specs=[VMEM] * len(operands), out_specs=[HBM, V...  4.15 us
    ppermute x5, waiting for transfers between devices, swapped(): lax.ppermute(block, axis, [(i ^ 1, i) for i in range(lax.axis_size(axis))])  1.4 us
    pallas_call x1, Pallas kernels, fetched(): pl.pallas_call(functools.partial(fetch_kernel, axis), in_specs=[HBM] * 4,...  1.34 us
  transfers between devices with their start and end apart: 9, of which 5 were waited for; matrix products, arithmetic and copies ran while one was open for 0% of the time, Pallas kernels for 8%

profile of v7, /device:TPU:0, one launch (start us, length us, event | category | flops | bytes accessed | tf_op | source)
XLA Modules:
  0.0 28.8 jit_solution(1486560037303208169)
XLA Ops:
  0.6 1.3 %shard_map.59 = (bf16[128,512]{1,0:T(8,128)(2,1)S(1)}, f32[8,128]{1,0:T(8,128)S(1)}, bf16[128,4096]{1,0:T(8,128)(2,1)S(1)}) custom-call(bf16[128,256]{1,0:T(8,128)(2,1)} %k_hbm.1, bf16[128,256]{1,0:T(8,128)(2,1)} %v_hbm.1, s32[16]{0:T(128)} %win_hbm.1, bf16[128,4096]{1,0:T(8,128)(2,1)} %q_hbm.1), custom_call_target="tpu_custom_call" | custom-call | tf_op jit(solution)/shard_map/pallas_call | solution.py:266
  2.0 0.5 %collective-permute-start = (bf16[128,512]{1,0:T(8,128)(2,1)S(1)}, bf16[128,512]{1,0:T(8,128)(2,1)S(1)}, u32[]{:S(2)}, u32[]{:S(2)}) collective-permute-start(bf16[128,512]{1,0:T(8,128)(2,1)S(1)} %get-tuple-element.13.own), channel_id=1, source_target_pairs={{1,0},{0,1},{3,2},{2,3},{5,4},{4,5},{7,6},{6,7},{9,8},{8,9},{11,10... | collective-permute-start | bytes 393224 | tf_op jit(solution)/shard_map/ppermute | solution.py:31
  2.5 2.6 %collective-permute-start.3 = (bf16[128,512]{1,0:T(8,128)(2,1)S(1)}, bf16[128,512]{1,0:T(8,128)(2,1)S(1)}, u32[]{:S(2)}, u32[]{:S(2)}) collective-permute-start(bf16[128,512]{1,0:T(8,128)(2,1)S(1)} %get-tuple-element.13.own), channel_id=1, source_target_pairs={{0,4},{1,5},{2,6},{3,7},{4,8},{5,9},{6,10},{7,11},{8,12},{9,13},{1... | collective-permute-start | bytes 393224 | tf_op jit(solution)/shard_map/ppermute | solution.py:27
  5.1 1.5 %collective-permute-start.1 = (bf16[128,512]{1,0:T(8,128)(2,1)S(1)}, bf16[128,512]{1,0:T(8,128)(2,1)S(1)}, u32[]{:S(2)}, u32[]{:S(2)}) collective-permute-start(bf16[128,512]{1,0:T(8,128)(2,1)S(1)} %get-tuple-element.13.own), channel_id=1, source_target_pairs={{0,2},{1,3},{2,4},{3,5},{4,6},{5,7},{6,8},{7,9},{8,10},{9,11},{10,... | collective-permute-start | bytes 393224 | tf_op jit(solution)/shard_map/ppermute | solution.py:27
  6.7 0.0 collective-permute-done.other
  6.7 1.8 %shard_map.60 = (f32[144,4096]{1,0:T(8,128)S(1)}, f32[8,128]{1,0:T(8,128)S(1)}) custom-call(f32[8,128]{1,0:T(8,128)S(1)} %get-tuple-element.11.mark_in, bf16[128,4096]{1,0:T(8,128)(2,1)S(1)} %get-tuple-element.12.q_ref, bf16[128,512]{1,0:T(8,128)(2,1)S(1)} %get-tuple-element.13.own, bf16[128,512]{1,0:T(8,128)(2,1)S(1)} %collective-permute-done.other), custom_call_target="tpu_custom_call" | custom-call | flops 536870912 | bytes 1048576 | tf_op jit(solution)/shard_map/pallas_call | solution.py:228
  8.5 2.8 %collective-permute-done.3.block_ref = bf16[128,512]{1,0:T(8,128)(2,1)S(1)} collective-permute-done((bf16[128,512]{1,0:T(8,128)(2,1)S(1)}, bf16[128,512]{1,0:T(8,128)(2,1)S(1)}, u32[]{:S(2)}, u32[]{:S(2)}) %collective-permute-start.3) | collective-permute-done | bytes 131104 | tf_op jit(solution)/shard_map/ppermute | solution.py:27
  11.3 0.0 collective-permute-start.4
  11.3 3.8 %collective-permute-done.1.block_ref = bf16[128,512]{1,0:T(8,128)(2,1)S(1)} collective-permute-done((bf16[128,512]{1,0:T(8,128)(2,1)S(1)}, bf16[128,512]{1,0:T(8,128)(2,1)S(1)}, u32[]{:S(2)}, u32[]{:S(2)}) %collective-permute-start.1) | collective-permute-done | bytes 131104 | tf_op jit(solution)/shard_map/ppermute | solution.py:27
  15.0 0.0 collective-permute-start.2
  15.0 0.0 collective-permute-start.7
  15.0 1.3 %collective-permute-start.5 = (bf16[128,512]{1,0:T(8,128)(2,1)S(1)}, bf16[128,512]{1,0:T(8,128)(2,1)S(1)}, u32[]{:S(2)}, u32[]{:S(2)}) collective-permute-start(bf16[128,512]{1,0:T(8,128)(2,1)S(1)} %shard_map.61.refs_0_), channel_id=1, source_target_pairs={{0,4},{1,5},{2,6},{3,7},{4,8},{5,9},{6,10},{7,11},{8,12},{9,13},{1... | collective-permute-start | bytes 393224 | tf_op jit(solution)/shard_map/ppermute | solution.py:27
  16.3 0.0 collective-permute-done.4.refs_3_
  16.3 0.0 collective-permute-done.2.refs_1_
  16.4 0.4 %shard_map.63 = (f32[144,4096]{1,0:T(8,128)S(1)}, f32[8,128]{1,0:T(8,128)S(1)}) custom-call(f32[8,128]{1,0:T(8,128)S(1)} %get-tuple-element.14.earlier_ref.mark_in, bf16[128,4096]{1,0:T(8,128)(2,1)S(1)} %get-tuple-element.12.q_ref, bf16[128,512]{1,0:T(8,128)(2,1)S(1)} %shard_map.61.refs_0_, ...), custom_call_target="tpu_custom_call", output_to_operand_aliasing={{0}: (6, {})} | custom-call | flops 1073741824 | bytes 1048576 | tf_op jit(solution)/shard_map/pallas_call | solution.py:228
  16.8 6.3 %collective-permute-done.7.block_ref = bf16[128,512]{1,0:T(8,128)(2,1)S(1)} collective-permute-done((bf16[128,512]{1,0:T(8,128)(2,1)S(1)}, bf16[128,512]{1,0:T(8,128)(2,1)S(1)}, u32[]{:S(2)}, u32[]{:S(2)}) %collective-permute-start.7) | collective-permute-done | bytes 131104 | tf_op jit(solution)/shard_map/ppermute | solution.py:27
  23.1 0.0 collective-permute-start.8
  23.1 2.4 %collective-permute-done.5.block_ref = bf16[128,512]{1,0:T(8,128)(2,1)S(1)} collective-permute-done((bf16[128,512]{1,0:T(8,128)(2,1)S(1)}, bf16[128,512]{1,0:T(8,128)(2,1)S(1)}, u32[]{:S(2)}, u32[]{:S(2)}) %collective-permute-start.5) | collective-permute-done | bytes 131104 | tf_op jit(solution)/shard_map/ppermute | solution.py:27
  25.5 0.0 collective-permute-start.6
  25.6 0.0 collective-permute-done.8.refs_3_
  25.6 1.3 %collective-permute-done.6.refs_1_ = bf16[128,512]{1,0:T(8,128)(2,1)S(1)} collective-permute-done((bf16[128,512]{1,0:T(8,128)(2,1)S(1)}, bf16[128,512]{1,0:T(8,128)(2,1)S(1)}, u32[]{:S(2)}, u32[]{:S(2)}) %collective-permute-start.6) | collective-permute-done | bytes 131104 | tf_op jit(solution)/shard_map/ppermute | solution.py:31
  26.9 1.9 %shard_map.66 = (bf16[128,4096]{1,0:T(8,128)(2,1)}, f32[32,128]{1,0:T(8,128)}) custom-call(f32[8,128]{1,0:T(8,128)S(1)} %get-tuple-element.16.earlier_ref.mark_in, bf16[128,4096]{1,0:T(8,128)(2,1)S(1)} %get-tuple-element.12.q_ref, bf16[128,512]{1,0:T(8,128)(2,1)S(1)} %shard_map.64.refs_0_, bf16[128,512]{1,0:T(8,128)(2,1)S(1)} %collective-permute-done.6.refs_1_, ...), custom_call_target="tpu_custom_call" | custom-call | flops 1073741824 | bytes 1048576 | tf_op jit(solution)/shard_map/pallas_call | solution.py:228
  (4 shorter events, 0.0 us)
Async XLA Ops:
  2.0 4.7 %collective-permute-start = (bf16[128,512]{1,0:T(8,128)(2,1)S(1)}, bf16[128,512]{1,0:T(8,128)(2,1)S(1)}, u32[]{:S(2)}, u32[]{:S(2)}) collective-permute-start(bf16[128,512]{1,0:T(8,128)(2,1)S(1)} %get-tuple-element.13.own), channel_id=1, source_target_pairs={{1,0},{0,1},{3,2},{2,3},{5,4},{4,5},{7,6},{6,7},{9,8},{8,9},{11,10... | collective-permute-start | bytes 393224 | tf_op jit(solution)/shard_map/ppermute | solution.py:31
  2.5 8.8 %collective-permute-start.3 = (bf16[128,512]{1,0:T(8,128)(2,1)S(1)}, bf16[128,512]{1,0:T(8,128)(2,1)S(1)}, u32[]{:S(2)}, u32[]{:S(2)}) collective-permute-start(bf16[128,512]{1,0:T(8,128)(2,1)S(1)} %get-tuple-element.13.own), channel_id=1, source_target_pairs={{0,4},{1,5},{2,6},{3,7},{4,8},{5,9},{6,10},{7,11},{8,12},{9,13},{1... | collective-permute-start | bytes 393224 | tf_op jit(solution)/shard_map/ppermute | solution.py:27
  5.1 9.9 %collective-permute-start.1 = (bf16[128,512]{1,0:T(8,128)(2,1)S(1)}, bf16[128,512]{1,0:T(8,128)(2,1)S(1)}, u32[]{:S(2)}, u32[]{:S(2)}) collective-permute-start(bf16[128,512]{1,0:T(8,128)(2,1)S(1)} %get-tuple-element.13.own), channel_id=1, source_target_pairs={{0,2},{1,3},{2,4},{3,5},{4,6},{5,7},{6,8},{7,9},{8,10},{9,11},{10,... | collective-permute-start | bytes 393224 | tf_op jit(solution)/shard_map/ppermute | solution.py:27
  11.3 5.1 %collective-permute-start.4 = (bf16[128,512]{1,0:T(8,128)(2,1)S(1)}, bf16[128,512]{1,0:T(8,128)(2,1)S(1)}, u32[]{:S(2)}, u32[]{:S(2)}) collective-permute-start(bf16[128,512]{1,0:T(8,128)(2,1)S(1)} %shard_map.62.refs_2_), channel_id=1, source_target_pairs={{1,0},{0,1},{3,2},{2,3},{5,4},{4,5},{7,6},{6,7},{9,8},{8,9},{11,10... | collective-permute-start | bytes 393224 | tf_op jit(solution)/shard_map/ppermute | solution.py:31
  15.0 1.3 %collective-permute-start.2 = (bf16[128,512]{1,0:T(8,128)(2,1)S(1)}, bf16[128,512]{1,0:T(8,128)(2,1)S(1)}, u32[]{:S(2)}, u32[]{:S(2)}) collective-permute-start(bf16[128,512]{1,0:T(8,128)(2,1)S(1)} %shard_map.61.refs_0_), channel_id=1, source_target_pairs={{1,0},{0,1},{3,2},{2,3},{5,4},{4,5},{7,6},{6,7},{9,8},{8,9},{11,10... | collective-permute-start | bytes 393224 | tf_op jit(solution)/shard_map/ppermute | solution.py:31
  15.0 8.1 %collective-permute-start.7 = (bf16[128,512]{1,0:T(8,128)(2,1)S(1)}, bf16[128,512]{1,0:T(8,128)(2,1)S(1)}, u32[]{:S(2)}, u32[]{:S(2)}) collective-permute-start(bf16[128,512]{1,0:T(8,128)(2,1)S(1)} %shard_map.62.refs_2_), channel_id=1, source_target_pairs={{0,4},{1,5},{2,6},{3,7},{4,8},{5,9},{6,10},{7,11},{8,12},{9,13},{1... | collective-permute-start | bytes 393224 | tf_op jit(solution)/shard_map/ppermute | solution.py:27
  15.0 10.5 %collective-permute-start.5 = (bf16[128,512]{1,0:T(8,128)(2,1)S(1)}, bf16[128,512]{1,0:T(8,128)(2,1)S(1)}, u32[]{:S(2)}, u32[]{:S(2)}) collective-permute-start(bf16[128,512]{1,0:T(8,128)(2,1)S(1)} %shard_map.61.refs_0_), channel_id=1, source_target_pairs={{0,4},{1,5},{2,6},{3,7},{4,8},{5,9},{6,10},{7,11},{8,12},{9,13},{1... | collective-permute-start | bytes 393224 | tf_op jit(solution)/shard_map/ppermute | solution.py:27
  23.1 2.4 %collective-permute-start.8 = (bf16[128,512]{1,0:T(8,128)(2,1)S(1)}, bf16[128,512]{1,0:T(8,128)(2,1)S(1)}, u32[]{:S(2)}, u32[]{:S(2)}) collective-permute-start(bf16[128,512]{1,0:T(8,128)(2,1)S(1)} %shard_map.65.refs_2_), channel_id=1, source_target_pairs={{1,0},{0,1},{3,2},{2,3},{5,4},{4,5},{7,6},{6,7},{9,8},{8,9},{11,10... | collective-permute-start | bytes 393224 | tf_op jit(solution)/shard_map/ppermute | solution.py:31
  25.5 1.3 %collective-permute-start.6 = (bf16[128,512]{1,0:T(8,128)(2,1)S(1)}, bf16[128,512]{1,0:T(8,128)(2,1)S(1)}, u32[]{:S(2)}, u32[]{:S(2)}) collective-permute-start(bf16[128,512]{1,0:T(8,128)(2,1)S(1)} %shard_map.64.refs_0_), channel_id=1, source_target_pairs={{1,0},{0,1},{3,2},{2,3},{5,4},{4,5},{7,6},{6,7},{9,8},{8,9},{11,10... | collective-permute-start | bytes 393224 | tf_op jit(solution)/shard_map/ppermute | solution.py:31

commit v8 on v3

--- a/solution.py
+++ b/solution.py
@@ -22,9 +22,13 @@
 MARK = (8, HD)
 
 
-def shifted(block, axis, distance):
+def first_reach(core, turn):
+    return 4 - 2 * (core ^ turn)
+
+
+def shifted(block, axis, distances):
     size = lax.axis_size(axis)
-    return lax.ppermute(block, axis, [(i, (i + distance) % size) for i in range(size)])
+    return lax.ppermute(block, axis, [(i, (i + distances[i % 2]) % size) for i in range(size)])
 
 
 def swapped(block, axis):
@@ -144,9 +148,9 @@
     )
 
 
-def far_kernel(axis, distances, last, mark_in, q_ref, *refs):
+def far_kernel(axis, level, last, mark_in, q_ref, *refs):
     me = lax.axis_index(axis)
-    count = 2 * len(distances)
+    count = 4
     blocks, state_in = refs[:count], refs[count]
     if last:
         state_out, (out_ref, log_ref, s_buf, p_buf) = None, refs[count + 1 :]
@@ -155,7 +159,11 @@
         mark[...] = mark_in[...]
     rows = blocks[0].shape[0]
     lowest = lowest_of(mark_in)
-    starts = [(who - d) * rows for d in distances for who in (me, me ^ 1)]
+    starts = [
+        (who - level - first_reach(who & 1, turn)) * rows
+        for turn in (0, 1)
+        for who in (me, me ^ 1)
+    ]
     needed = functools.reduce(jnp.logical_or, [s + rows > lowest for s in starts])
 
     @pl.when(needed)
@@ -280,27 +288,27 @@
     reach = lax.axis_size(axis) // 2
     own, mark, queries = fetched(axis, queries, keys, values, windows)
     other = swapped(own, axis)
-    held = {4: shifted(own, axis, 4), 2: shifted(own, axis, 2)}
+    arrived = [shifted(own, axis, [first_reach(core, turn) for core in (0, 1)]) for turn in (0, 1)]
     state, mark = attend(
         functools.partial(near_kernel, axis), mark, queries, [own, other], None, False
     )
-    for first in range(2, reach + 1, 4):
-        distances = [d for d in (first + 2, first) if d <= reach]
-        last = first + 4 > reach
-        blocks = []
-        for d in distances:
-            held[d] = tied(held[d], mark)
-            if d + 4 <= reach:
-                held[d + 4] = shifted(held[d], axis, 4)
-            blocks += [held[d], swapped(held[d], axis)]
+    for level in range(0, reach, 4):
+        last = level + 4 >= reach
+        blocks, later = [], []
+        for block in arrived:
+            block = tied(block, mark)
+            if not last:
+                later.append(shifted(block, axis, (4, 4)))
+            blocks += [block, swapped(block, axis)]
         result = attend(
-            functools.partial(far_kernel, axis, distances, last),
+            functools.partial(far_kernel, axis, level, last),
             mark,
             queries,
             blocks,
             state,
             last,
         )
+        arrived = later
         state, mark = result
     return result[0], result[1].T
 

time: 26.4 us -> 27.6 us (1.045)
  the two profiles are of different devices: /device:TPU:15 before, /device:TPU:0 now
where the time goes in v8:
time: 27.6 us; the launch traced here: 27.4 us
  waiting for transfers between devices  13.7 us (50%)
  starting transfers between devices  7.95 us (29%)
  Pallas kernels  5.09 us (18%)
  between operations  0.67 us (2%)
    ppermute x4, waiting for transfers between devices, shifted(): lax.ppermute(block, axis, [(i, (i + distances[i % 2]) % size) for i in ra...  12.4 us
    ppermute x4, starting transfers between devices, shifted(): lax.ppermute(block, axis, [(i, (i + distances[i % 2]) % size) for i in ra...  5.31 us
    pallas_call x3, Pallas kernels, attend(): pl.pallas_call(kernel, in_specs=[VMEM] * len(operands), out_specs=[VMEM]...  3.75 us
    ppermute x5, starting transfers between devices, swapped(): lax.ppermute(block, axis, [(i ^ 1, i) for i in range(lax.axis_size(axis))])  2.64 us
    ppermute x5, waiting for transfers between devices, swapped(): lax.ppermute(block, axis, [(i ^ 1, i) for i in range(lax.axis_size(axis))])  1.35 us
    pallas_call x1, Pallas kernels, fetched(): pl.pallas_call(functools.partial(fetch_kernel, axis), in_specs=[HBM] * 4,...  1.34 us
  transfers between devices with their start and end apart: 9, of which 4 were waited for; matrix products, arithmetic and copies ran while one was open for 0% of the time, Pallas kernels for 8%

profile of v8, /device:TPU:0, one launch (start us, length us, event | category | flops | bytes accessed | tf_op | source)
XLA Modules:
  0.0 27.4 jit_solution(12561275498803114975)
XLA Ops:
  0.6 1.3 %shard_map.59 = (bf16[128,512]{1,0:T(8,128)(2,1)S(1)}, f32[8,128]{1,0:T(8,128)S(1)}, bf16[128,4096]{1,0:T(8,128)(2,1)S(1)}) custom-call(bf16[128,256]{1,0:T(8,128)(2,1)} %k_hbm.1, bf16[128,256]{1,0:T(8,128)(2,1)} %v_hbm.1, s32[16]{0:T(128)} %win_hbm.1, bf16[128,4096]{1,0:T(8,128)(2,1)} %q_hbm.1), custom_call_target="tpu_custom_call" | custom-call | tf_op jit(solution)/shard_map/pallas_call | solution.py:255
  2.0 0.5 %collective-permute-start = (bf16[128,512]{1,0:T(8,128)(2,1)S(1)}, bf16[128,512]{1,0:T(8,128)(2,1)S(1)}, u32[]{:S(2)}, u32[]{:S(2)}) collective-permute-start(bf16[128,512]{1,0:T(8,128)(2,1)S(1)} %get-tuple-element.13.own), channel_id=1, source_target_pairs={{1,0},{0,1},{3,2},{2,3},{5,4},{4,5},{7,6},{6,7},{9,8},{8,9},{11,10... | collective-permute-start | bytes 393224 | tf_op jit(solution)/shard_map/ppermute | solution.py:35
  2.5 2.6 %collective-permute-start.3 = (bf16[128,512]{1,0:T(8,128)(2,1)S(1)}, bf16[128,512]{1,0:T(8,128)(2,1)S(1)}, u32[]{:S(2)}, u32[]{:S(2)}) collective-permute-start(bf16[128,512]{1,0:T(8,128)(2,1)S(1)} %get-tuple-element.13.own), channel_id=1, source_target_pairs={{0,2},{1,5},{2,4},{3,7},{4,6},{5,9},{6,8},{7,11},{8,10},{9,13},{10... | collective-permute-start | bytes 393224 | tf_op jit(solution)/shard_map/ppermute | solution.py:31
  5.1 1.6 %collective-permute-start.1 = (bf16[128,512]{1,0:T(8,128)(2,1)S(1)}, bf16[128,512]{1,0:T(8,128)(2,1)S(1)}, u32[]{:S(2)}, u32[]{:S(2)}) collective-permute-start(bf16[128,512]{1,0:T(8,128)(2,1)S(1)} %get-tuple-element.13.own), channel_id=1, source_target_pairs={{0,4},{1,3},{2,6},{3,5},{4,8},{5,7},{6,10},{7,9},{8,12},{9,11},{10... | collective-permute-start | bytes 393224 | tf_op jit(solution)/shard_map/ppermute | solution.py:31
  6.7 0.0 collective-permute-done.other
  6.7 1.8 %shard_map.60 = (f32[144,4096]{1,0:T(8,128)S(1)}, f32[8,128]{1,0:T(8,128)S(1)}) custom-call(f32[8,128]{1,0:T(8,128)S(1)} %get-tuple-element.11.mark_in, bf16[128,4096]{1,0:T(8,128)(2,1)S(1)} %get-tuple-element.12.q_ref, bf16[128,512]{1,0:T(8,128)(2,1)S(1)} %get-tuple-element.13.own, bf16[128,512]{1,0:T(8,128)(2,1)S(1)} %collective-permute-done.other), custom_call_target="tpu_custom_call" | custom-call | flops 536870912 | bytes 1048576 | tf_op jit(solution)/shard_map/pallas_call | solution.py:214
  8.5 4.0 %collective-permute-done.3.block_ref = bf16[128,512]{1,0:T(8,128)(2,1)S(1)} collective-permute-done((bf16[128,512]{1,0:T(8,128)(2,1)S(1)}, bf16[128,512]{1,0:T(8,128)(2,1)S(1)}, u32[]{:S(2)}, u32[]{:S(2)}) %collective-permute-start.3) | collective-permute-done | bytes 131104 | tf_op jit(solution)/shard_map/ppermute | solution.py:31
  12.5 0.0 collective-permute-start.4
  12.5 0.0 collective-permute-done.1.block_ref
  12.5 2.1 %collective-permute-start.2 = (bf16[128,512]{1,0:T(8,128)(2,1)S(1)}, bf16[128,512]{1,0:T(8,128)(2,1)S(1)}, u32[]{:S(2)}, u32[]{:S(2)}) collective-permute-start(bf16[128,512]{1,0:T(8,128)(2,1)S(1)} %shard_map.61.refs_0_), channel_id=1, source_target_pairs={{1,0},{0,1},{3,2},{2,3},{5,4},{4,5},{7,6},{6,7},{9,8},{8,9},{11,10... | collective-permute-start | bytes 393224 | tf_op jit(solution)/shard_map/ppermute | solution.py:35
  14.6 0.0 collective-permute-start.7
  14.6 1.1 %collective-permute-start.5 = (bf16[128,512]{1,0:T(8,128)(2,1)S(1)}, bf16[128,512]{1,0:T(8,128)(2,1)S(1)}, u32[]{:S(2)}, u32[]{:S(2)}) collective-permute-start(bf16[128,512]{1,0:T(8,128)(2,1)S(1)} %shard_map.61.refs_0_), channel_id=1, source_target_pairs={{0,4},{1,5},{2,6},{3,7},{4,8},{5,9},{6,10},{7,11},{8,12},{9,13},{1... | collective-permute-start | bytes 393224 | tf_op jit(solution)/shard_map/ppermute | solution.py:31
  15.8 0.0 collective-permute-done.4.refs_3_
  15.8 0.0 collective-permute-done.2.refs_1_
  15.8 0.4 %shard_map.63 = (f32[144,4096]{1,0:T(8,128)S(1)}, f32[8,128]{1,0:T(8,128)S(1)}) custom-call(f32[8,128]{1,0:T(8,128)S(1)} %get-tuple-element.14.earlier_ref.mark_in, bf16[128,4096]{1,0:T(8,128)(2,1)S(1)} %get-tuple-element.12.q_ref, bf16[128,512]{1,0:T(8,128)(2,1)S(1)} %shard_map.61.refs_0_, ...), custom_call_target="tpu_custom_call", output_to_operand_aliasing={{0}: (6, {})} | custom-call | flops 1073741824 | bytes 1048576 | tf_op jit(solution)/shard_map/pallas_call | solution.py:214
  16.2 6.6 %collective-permute-done.7.block_ref = bf16[128,512]{1,0:T(8,128)(2,1)S(1)} collective-permute-done((bf16[128,512]{1,0:T(8,128)(2,1)S(1)}, bf16[128,512]{1,0:T(8,128)(2,1)S(1)}, u32[]{:S(2)}, u32[]{:S(2)}) %collective-permute-start.7) | collective-permute-done | bytes 131104 | tf_op jit(solution)/shard_map/ppermute | solution.py:31
  22.8 0.0 collective-permute-start.8
  22.8 1.8 %collective-permute-done.5.block_ref = bf16[128,512]{1,0:T(8,128)(2,1)S(1)} collective-permute-done((bf16[128,512]{1,0:T(8,128)(2,1)S(1)}, bf16[128,512]{1,0:T(8,128)(2,1)S(1)}, u32[]{:S(2)}, u32[]{:S(2)}) %collective-permute-start.5) | collective-permute-done | bytes 131104 | tf_op jit(solution)/shard_map/ppermute | solution.py:31
  24.6 0.0 collective-permute-start.6
  24.6 0.0 collective-permute-done.8.refs_3_
  24.6 1.3 %collective-permute-done.6.refs_1_ = bf16[128,512]{1,0:T(8,128)(2,1)S(1)} collective-permute-done((bf16[128,512]{1,0:T(8,128)(2,1)S(1)}, bf16[128,512]{1,0:T(8,128)(2,1)S(1)}, u32[]{:S(2)}, u32[]{:S(2)}) %collective-permute-start.6) | collective-permute-done | bytes 131104 | tf_op jit(solution)/shard_map/ppermute | solution.py:35
  26.0 1.5 %shard_map.66 = (bf16[128,4096]{1,0:T(8,128)(2,1)}, f32[32,128]{1,0:T(8,128)}) custom-call(f32[8,128]{1,0:T(8,128)S(1)} %get-tuple-element.16.earlier_ref.mark_in, bf16[128,4096]{1,0:T(8,128)(2,1)S(1)} %get-tuple-element.12.q_ref, bf16[128,512]{1,0:T(8,128)(2,1)S(1)} %shard_map.64.refs_0_, bf16[128,512]{1,0:T(8,128)(2,1)S(1)} %collective-permute-done.6.refs_1_, ...), custom_call_target="tpu_custom_call" | custom-call | flops 1073741824 | bytes 1048576 | tf_op jit(solution)/shard_map/pallas_call | solution.py:214
  (4 shorter events, 0.0 us)
Async XLA Ops:
  2.0 4.7 %collective-permute-start = (bf16[128,512]{1,0:T(8,128)(2,1)S(1)}, bf16[128,512]{1,0:T(8,128)(2,1)S(1)}, u32[]{:S(2)}, u32[]{:S(2)}) collective-permute-start(bf16[128,512]{1,0:T(8,128)(2,1)S(1)} %get-tuple-element.13.own), channel_id=1, source_target_pairs={{1,0},{0,1},{3,2},{2,3},{5,4},{4,5},{7,6},{6,7},{9,8},{8,9},{11,10... | collective-permute-start | bytes 393224 | tf_op jit(solution)/shard_map/ppermute | solution.py:35
  2.5 10.0 %collective-permute-start.3 = (bf16[128,512]{1,0:T(8,128)(2,1)S(1)}, bf16[128,512]{1,0:T(8,128)(2,1)S(1)}, u32[]{:S(2)}, u32[]{:S(2)}) collective-permute-start(bf16[128,512]{1,0:T(8,128)(2,1)S(1)} %get-tuple-element.13.own), channel_id=1, source_target_pairs={{0,2},{1,5},{2,4},{3,7},{4,6},{5,9},{6,8},{7,11},{8,10},{9,13},{10... | collective-permute-start | bytes 393224 | tf_op jit(solution)/shard_map/ppermute | solution.py:31
  5.1 7.4 %collective-permute-start.1 = (bf16[128,512]{1,0:T(8,128)(2,1)S(1)}, bf16[128,512]{1,0:T(8,128)(2,1)S(1)}, u32[]{:S(2)}, u32[]{:S(2)}) collective-permute-start(bf16[128,512]{1,0:T(8,128)(2,1)S(1)} %get-tuple-element.13.own), channel_id=1, source_target_pairs={{0,4},{1,3},{2,6},{3,5},{4,8},{5,7},{6,10},{7,9},{8,12},{9,11},{10... | collective-permute-start | bytes 393224 | tf_op jit(solution)/shard_map/ppermute | solution.py:31
  12.5 3.3 %collective-permute-start.4 = (bf16[128,512]{1,0:T(8,128)(2,1)S(1)}, bf16[128,512]{1,0:T(8,128)(2,1)S(1)}, u32[]{:S(2)}, u32[]{:S(2)}) collective-permute-start(bf16[128,512]{1,0:T(8,128)(2,1)S(1)} %shard_map.62.refs_2_), channel_id=1, source_target_pairs={{1,0},{0,1},{3,2},{2,3},{5,4},{4,5},{7,6},{6,7},{9,8},{8,9},{11,10... | collective-permute-start | bytes 393224 | tf_op jit(solution)/shard_map/ppermute | solution.py:35
  12.5 3.3 %collective-permute-start.2 = (bf16[128,512]{1,0:T(8,128)(2,1)S(1)}, bf16[128,512]{1,0:T(8,128)(2,1)S(1)}, u32[]{:S(2)}, u32[]{:S(2)}) collective-permute-start(bf16[128,512]{1,0:T(8,128)(2,1)S(1)} %shard_map.61.refs_0_), channel_id=1, source_target_pairs={{1,0},{0,1},{3,2},{2,3},{5,4},{4,5},{7,6},{6,7},{9,8},{8,9},{11,10... | collective-permute-start | bytes 393224 | tf_op jit(solution)/shard_map/ppermute | solution.py:35
  14.6 8.2 %collective-permute-start.7 = (bf16[128,512]{1,0:T(8,128)(2,1)S(1)}, bf16[128,512]{1,0:T(8,128)(2,1)S(1)}, u32[]{:S(2)}, u32[]{:S(2)}) collective-permute-start(bf16[128,512]{1,0:T(8,128)(2,1)S(1)} %shard_map.62.refs_2_), channel_id=1, source_target_pairs={{0,4},{1,5},{2,6},{3,7},{4,8},{5,9},{6,10},{7,11},{8,12},{9,13},{1... | collective-permute-start | bytes 393224 | tf_op jit(solution)/shard_map/ppermute | solution.py:31
  14.6 10.0 %collective-permute-start.5 = (bf16[128,512]{1,0:T(8,128)(2,1)S(1)}, bf16[128,512]{1,0:T(8,128)(2,1)S(1)}, u32[]{:S(2)}, u32[]{:S(2)}) collective-permute-start(bf16[128,512]{1,0:T(8,128)(2,1)S(1)} %shard_map.61.refs_0_), channel_id=1, source_target_pairs={{0,4},{1,5},{2,6},{3,7},{4,8},{5,9},{6,10},{7,11},{8,12},{9,13},{1... | collective-permute-start | bytes 393224 | tf_op jit(solution)/shard_map/ppermute | solution.py:31
  22.8 1.9 %collective-permute-start.8 = (bf16[128,512]{1,0:T(8,128)(2,1)S(1)}, bf16[128,512]{1,0:T(8,128)(2,1)S(1)}, u32[]{:S(2)}, u32[]{:S(2)}) collective-permute-start(bf16[128,512]{1,0:T(8,128)(2,1)S(1)} %shard_map.65.refs_2_), channel_id=1, source_target_pairs={{1,0},{0,1},{3,2},{2,3},{5,4},{4,5},{7,6},{6,7},{9,8},{8,9},{11,10... | collective-permute-start | bytes 393224 | tf_op jit(solution)/shard_map/ppermute | solution.py:35
  24.6 1.3 %collective-permute-start.6 = (bf16[128,512]{1,0:T(8,128)(2,1)S(1)}, bf16[128,512]{1,0:T(8,128)(2,1)S(1)}, u32[]{:S(2)}, u32[]{:S(2)}) collective-permute-start(bf16[128,512]{1,0:T(8,128)(2,1)S(1)} %shard_map.64.refs_0_), channel_id=1, source_target_pairs={{1,0},{0,1},{3,2},{2,3},{5,4},{4,5},{7,6},{6,7},{9,8},{8,9},{11,10... | collective-permute-start | bytes 393224 | tf_op jit(solution)/shard_map/ppermute | solution.py:35
